TPU v7x, 512 devices: a whole 4x8x8 slice. The times are simulated.
512 devices in a mesh: dp: 8 (over y_lo, core), tm: 64 (over x, y_hi, z).
Axes of the slice: x: 4, y: 8 (y_hi: 2, y_lo: 4; y = y_hi * 4 + y_lo), z: 8, core: 2. Of those that a mesh axis runs over, the one named last changes fastest.
Arguments:
- queries: bfloat16 [8, 64, 128, 576], P('dp', 'tm'), may hold values from -48 to 48
- keys: bfloat16 [8, 64, 128, 576], P('dp', 'tm'), may hold values from -48 to 48
- values: bfloat16 [8, 64, 128, 576], P('dp', 'tm'), may hold values from -6 to 6
- out_weight: bfloat16 [576, 1152], P('tm', 'dp'), may hold values from -0.25 to 0.25
- upstream: bfloat16 [8, 64, 128, 1152], P('dp', 'tm'), may hold values from -16 to 16
- timestep: int32 [8], P('dp'), may hold values from 0 to 999
Outputs:
- output: bfloat16 [8, 64, 128, 1152], P('dp', 'tm')
- query_grad: bfloat16 [8, 64, 128, 576], P('dp', 'tm')
- key_grad: bfloat16 [8, 64, 128, 576], P('dp', 'tm')
- value_grad: bfloat16 [8, 64, 128, 576], P('dp', 'tm')
- weight_grad: float32 [576, 1152], P('tm', 'dp')
All inputs are finite; a program needn't handle non-finite values.
Results may differ from a plain program's by a relative error of at most 0.0065.
Values may be sent and summed in bfloat16 or wider, within the bound.
No kernel may reach another device: no remote copies, remote signals or barrier semaphores. Data moves between devices by JAX's collectives and lax.ppermute only.
A program may use at most 64 MiB of HBM per device.

v0:
```python
import jax
import jax.numpy as jnp
from jax import lax
from jax.sharding import PartitionSpec as P

D = 1152
HEADS = 8


def slab_scores(query_slab, key_slab):
    clips, frames, patches, feats = query_slab.shape
    qh = query_slab.reshape(clips, frames, patches, HEADS, feats // HEADS)
    kh = key_slab.reshape(clips, frames, patches, HEADS, feats // HEADS)
    factor = 1.0 / jnp.sqrt(jnp.float32(feats // HEADS))
    scores = jnp.einsum("cfphe,cgphe->cphfg", qh, kh, preferred_element_type=jnp.float32) * factor
    shifted = scores - jnp.max(scores, axis=-1, keepdims=True)
    expd = jnp.exp(shifted)
    return expd / jnp.sum(expd, axis=-1, keepdims=True)


def gate_table(timestep):
    freq = jnp.exp(-jnp.log(10000.0) * jnp.arange(D).astype(jnp.float32) / D)
    return 1.5 + jnp.sin(timestep.astype(jnp.float32)[:, None] * freq[None, :])


def shards(queries, keys, values, out_weight, upstream, timestep):
    clips, frames_dev, patches, feats = queries.shape
    head_size = feats // HEADS
    factor = 1.0 / jnp.sqrt(jnp.float32(head_size))
    query_slab, key_slab, value_slab = (
        lax.all_to_all(queries, "tm", split_axis=2, concat_axis=1, tiled=True),
        lax.all_to_all(keys, "tm", split_axis=2, concat_axis=1, tiled=True),
        lax.all_to_all(values, "tm", split_axis=2, concat_axis=1, tiled=True),
    )
    frames = query_slab.shape[1]
    slab_patches = query_slab.shape[2]
    split_shape = (clips, frames, slab_patches, HEADS, head_size)
    vh = value_slab.reshape(split_shape)
    probs = slab_scores(query_slab, key_slab)
    probs_low = probs.astype(jnp.bfloat16)
    attended_slab = jnp.einsum(
        "cphfg,cgphe->cfphe", probs_low, vh, preferred_element_type=jnp.float32
    )
    attended_slab = attended_slab.astype(jnp.bfloat16).reshape(clips, frames, slab_patches, feats)
    attended = lax.all_to_all(attended_slab, "tm", split_axis=1, concat_axis=2, tiled=True)
    cols = lax.all_gather(out_weight, "dp", axis=1, tiled=True)
    weight = lax.all_gather(cols, "tm", axis=0, tiled=True)
    gate = gate_table(timestep)
    flat_att = attended.reshape(clips, -1, feats)
    proj = jnp.einsum("cth,hd->ctd", flat_att, weight, preferred_element_type=jnp.float32)
    output = (gate[:, None, :] * proj).astype(jnp.bfloat16).reshape(upstream.shape)
    scaled = (gate[:, None, :] * upstream.reshape(clips, -1, D)).astype(jnp.bfloat16)
    attended_grad = jnp.einsum("ctd,hd->cth", scaled, weight, preferred_element_type=jnp.float32)
    attended_grad = attended_grad.astype(jnp.bfloat16).reshape(queries.shape)
    att_rows = flat_att.reshape(-1, feats)
    scaled_rows = scaled.reshape(-1, D)
    row_share = lax.psum_scatter(
        lax.dot_general(
            att_rows, scaled_rows, (((0,), (0,)), ((), ())), preferred_element_type=jnp.float32
        ),
        "tm",
        scatter_dimension=0,
        tiled=True,
    )
    weight_grad = lax.psum_scatter(row_share, "dp", scatter_dimension=1, tiled=True)
    grad_slab = lax.all_to_all(attended_grad, "tm", split_axis=2, concat_axis=1, tiled=True)
    gh = grad_slab.reshape(split_shape)
    prob_grad = jnp.einsum("cfphe,cgphe->cphfg", gh, vh, preferred_element_type=jnp.float32)
    value_grad = jnp.einsum("cphfg,cfphe->cgphe", probs_low, gh, preferred_element_type=jnp.float32)
    inner = jnp.sum(probs * prob_grad, axis=-1, keepdims=True)
    score_grad = (probs * (prob_grad - inner)).astype(jnp.bfloat16)
    qh = query_slab.reshape(split_shape)
    kh = key_slab.reshape(split_shape)
    query_grad = (
        jnp.einsum("cphfg,cgphe->cfphe", score_grad, kh, preferred_element_type=jnp.float32)
        * factor
    )
    key_grad = (
        jnp.einsum("cphfg,cfphe->cgphe", score_grad, qh, preferred_element_type=jnp.float32)
        * factor
    )
    slab_shape = (clips, frames, slab_patches, feats)
    query_grad = query_grad.astype(jnp.bfloat16).reshape(slab_shape)
    key_grad = key_grad.astype(jnp.bfloat16).reshape(slab_shape)
    value_grad = value_grad.astype(jnp.bfloat16).reshape(slab_shape)
    query_back, key_back, value_back = (
        lax.all_to_all(query_grad, "tm", split_axis=1, concat_axis=2, tiled=True),
        lax.all_to_all(key_grad, "tm", split_axis=1, concat_axis=2, tiled=True),
        lax.all_to_all(value_grad, "tm", split_axis=1, concat_axis=2, tiled=True),
    )
    return (output, query_back, key_back, value_back, weight_grad)


def solution(mesh):
    return jax.shard_map(
        shards,
        mesh=mesh,
        in_specs=(
            P("dp", "tm", None, None),
            P("dp", "tm", None, None),
            P("dp", "tm", None, None),
            P("tm", "dp"),
            P("dp", "tm", None, None),
            P("dp"),
        ),
        out_specs=(
            P("dp", "tm", None, None),
            P("dp", "tm", None, None),
            P("dp", "tm", None, None),
            P("dp", "tm", None, None),
            P("tm", "dp"),
        ),
        check_vma=False,
    )
```

profile of v0, /device:TPU:4, one launch (start us, length us, event | category | flops | bytes accessed | tf_op | source)
XLA Modules:
  0.0 1044.8 jit_solution(11351478099410307156)
XLA Ops:
  7.2 14.4 %all-gather = bf16[8,144,9]{1,2,0:T(8,128)(2,1)S(1)} all-gather(bf16[1,144,9]{1,2,0:T(8,128)(2,1)} %bitcast.89), channel_id=1, replica_groups=mesh['dp'=8,'tm'=64] {'dp'}, dimensions={0}, use_global_device_ids=true | all-gather | bytes 23328 | tf_op jit(solution)/shard_map/all_gather | solution.py:46
  21.7 0.7 reshape.212
  22.4 1.1 copy.41
  23.6 0.5 broadcast.68
  24.1 1.7 reduce.16
  25.8 0.7 reshape.230
  26.5 19.0 %all-to-all-start = ((bf16[64,2,576]{2,1,0:T(2,128)(2,1)}), bf16[64,2,576]{2,1,0:T(2,128)(2,1)S(1)}, u32[]{:S(2)}, u32[]{:S(2)}) async-start(bf16[64,2,576]{2,1,0:T(2,128)(2,1)} %reshape.230), calls=%async_computation | async-start | bytes 327680 | tf_op jit(solution)/shard_map/all_to_all | solution.py:31
  45.8 1.7 reduce.15
  47.4 0.7 reshape.228
  48.1 10.2 all-to-all-done
  58.3 7.7 all-to-all-start.1
  66.2 1.7 reduce.14
  67.9 0.7 reshape.226
  68.8 10.0 all-to-all-done.1
  78.8 6.8 all-to-all-start.2
  85.7 0.9 bitcast_reduce_fusion.1
  87.0 0.9 bitcast_reduce_fusion.2
  88.2 10.5 %all-to-all-done.2 = bf16[64,2,576]{2,1,0:T(2,128)(2,1)S(1)} async-done(((bf16[64,2,576]{2,1,0:T(2,128)(2,1)}), bf16[64,2,576]{2,1,0:T(2,128)(2,1)S(1)}, u32[]{:S(2)}, u32[]{:S(2)}) %all-to-all-start.2) | async-done | bytes 147488 | tf_op jit(solution)/shard_map/all_to_all | solution.py:33
  98.9 0.9 bitcast_reduce_fusion.3
  100.9 1.2 reshape.215
  102.1 7.3 all-to-all-start.3
  110.1 11.9 %all-to-all-done.3 = bf16[1,64,2,576]{3,2,0,1:T(2,128)(2,1)S(1)} async-done(((bf16[1,64,2,576]{3,2,0,1:T(2,128)(2,1)}), bf16[1,64,2,576]{3,2,0,1:T(2,128)(2,1)S(1)}, u32[]{:S(2)}, u32[]{:S(2)}) %all-to-all-start.3) | async-done | bytes 147488 | tf_op jit(solution)/shard_map/all_to_all | solution.py:45
  122.2 2.1 fusion.16
  124.3 40.5 %all-gather.4.cloned.1.call-done = bf16[64,9,1152]{2,1,0:T(8,128)(2,1)} async-done(((bf16[1,9,1152]{2,1,0:T(8,128)(2,1)}), bf16[64,9,1152]{2,1,0:T(8,128)(2,1)}) %all-gather.4.cloned.1.call-update) | async-done | bytes 1327120 | tf_op jit(solution)/shard_map/all_gather | solution.py:47
  164.8 2.6 reshape.214
  167.4 0.5 fusion.11
  168.2 1.7 reduce.17
  169.9 22.1 %all_to_all.81 = bf16[64,2,576]{2,1,0:T(2,128)(2,1)S(1)} all-to-all(bf16[64,2,576]{2,1,0:T(2,128)(2,1)S(1)} %reshape.232), channel_id=1, replica_groups=mesh['dp'=8,'tm'=64] {'tm'}, dimensions={0} | all-to-all | bytes 294912 | tf_op jit(solution)/shard_map/all_to_all | solution.py:66
  192.2 0.9 bitcast_reduce_fusion
  193.7 0.4 copy-done.1
  194.6 1.2 reshape.217
  195.8 7.1 all-to-all-start.6
  203.4 1.2 reshape.216
  204.5 11.1 %all-to-all-done.6 = bf16[1,64,2,576]{3,2,0,1:T(2,128)(2,1)S(1)} async-done(((bf16[1,64,2,576]{3,2,0,1:T(2,128)(2,1)}), bf16[1,64,2,576]{3,2,0,1:T(2,128)(2,1)S(1)}, u32[]{:S(2)}, u32[]{:S(2)}) %all-to-all-start.6) | async-done | bytes 147488 | tf_op jit(solution)/shard_map/all_to_all | solution.py:88
  215.6 7.3 all-to-all-start.5
  222.9 1.3 dynamic-slice
  225.2 1.2 reshape.218
  226.4 9.2 all-to-all-done.5
  235.6 7.0 all-to-all-start.7
  242.7 724.6 %all-reduce.3.cloned.1.call-done = f32[576,1152]{1,0:T(8,128)} async-done(((f32[576,1152]{1,0:T(8,128)}), f32[576,1152]{1,0:T(8,128)}) %all-reduce.3.cloned.1.call-update) | async-done | bytes 2654224
  967.3 0.9 constant_dynamic-slice_fusion
  968.2 1.1 copy.73
  969.3 1.1 fusion.2
  970.6 0.8 copy.65
  971.5 0.8 copy.64
  972.4 0.8 copy.66
  973.2 63.5 %reduce-scatter.4.cloned.1.call-done = f32[144,9]{1,0:T(8,128)} async-done(((f32[1152,9]{1,0:T(8,128)}), f32[144,9]{1,0:T(8,128)}) %reduce-scatter.4.cloned.1.call-update) | async-done | bytes 5200
  1036.7 1.6 copy.74
  (45 shorter events, 5.7 us)
Async XLA Ops:
  7.2 38.3 %copy-start.3 = (bf16[1,1,128,576]{2,3,1,0:T(8,128)(2,1)S(1)}, bf16[1,1,128,576]{2,3,1,0:T(8,128)(2,1)}, u32[]{:S(2)}) copy-start(bf16[1,1,128,576]{2,3,1,0:T(8,128)(2,1)} %param.7) | copy-start | bytes 442372
  7.2 157.6 %all-gather.4.cloned.1.call-start = ((), (), s32[]{:S(2)}) async-start(), calls=%async_computation.9 | async-start | bytes 2396160 | tf_op jit(solution)/shard_map/all_gather | solution.py:47
  24.1 41.9 %copy-start.4 = (bf16[1,1,128,576]{2,3,1,0:T(8,128)(2,1)S(1)}, bf16[1,1,128,576]{2,3,1,0:T(8,128)(2,1)}, u32[]{:S(2)}) copy-start(bf16[1,1,128,576]{2,3,1,0:T(8,128)(2,1)} %param.8) | copy-start | bytes 442372
  26.5 31.8 %all-to-all-start = ((bf16[64,2,576]{2,1,0:T(2,128)(2,1)}), bf16[64,2,576]{2,1,0:T(2,128)(2,1)S(1)}, u32[]{:S(2)}, u32[]{:S(2)}) async-start(bf16[64,2,576]{2,1,0:T(2,128)(2,1)} %reshape.230), calls=%async_computation | async-start | bytes 327680 | tf_op jit(solution)/shard_map/all_to_all | solution.py:31
  58.3 20.5 %all-to-all-start.1 = ((bf16[64,2,576]{2,1,0:T(2,128)(2,1)}), bf16[64,2,576]{2,1,0:T(2,128)(2,1)S(1)}, u32[]{:S(2)}, u32[]{:S(2)}) async-start(bf16[64,2,576]{2,1,0:T(2,128)(2,1)} %reshape.228), calls=%async_computation.1 | async-start | bytes 327680 | tf_op jit(solution)/shard_map/all_to_all | solution.py:32
  78.8 19.9 %all-to-all-start.2 = ((bf16[64,2,576]{2,1,0:T(2,128)(2,1)}), bf16[64,2,576]{2,1,0:T(2,128)(2,1)S(1)}, u32[]{:S(2)}, u32[]{:S(2)}) async-start(bf16[64,2,576]{2,1,0:T(2,128)(2,1)} %reshape.226), calls=%async_computation.2 | async-start | bytes 327680 | tf_op jit(solution)/shard_map/all_to_all | solution.py:33
  100.7 21.5 %copy-start = (bf16[1,1,128,1152]{3,2,1,0:T(8,128)(2,1)S(1)}, bf16[1,1,128,1152]{3,2,1,0:T(8,128)(2,1)}, u32[]{:S(2)}) copy-start(bf16[1,1,128,1152]{3,2,1,0:T(8,128)(2,1)} %param.10) | copy-start | bytes 884740
  102.1 20.0 %all-to-all-start.3 = ((bf16[1,64,2,576]{3,2,0,1:T(2,128)(2,1)}), bf16[1,64,2,576]{3,2,0,1:T(2,128)(2,1)S(1)}, u32[]{:S(2)}, u32[]{:S(2)}) async-start(bf16[1,64,2,576]{3,2,0,1:T(2,128)(2,1)} %reshape.215), calls=%async_computation.3 | async-start | bytes 327680 | tf_op jit(solution)/shard_map/all_to_all | solution.py:45
  109.4 858.0 %all-reduce.3.cloned.1.call-start = ((), (), s32[]{:S(2)}) async-start(), calls=%async_computation.11 | async-start | bytes 5308416
  193.4 0.7 copy-start.1
  194.6 30.2 %copy-start.2 = (bf16[64,2,8,72]{3,2,1,0:T(8,128)(2,1)S(1)}, bf16[64,2,8,72]{3,2,1,0:T(8,128)(2,1)}, u32[]{:S(2)}) copy-start(bf16[64,2,8,72]{3,2,1,0:T(8,128)(2,1)} %copy-done.1) | copy-start | bytes 442372
  195.8 19.8 %all-to-all-start.6 = ((bf16[1,64,2,576]{3,2,0,1:T(2,128)(2,1)}), bf16[1,64,2,576]{3,2,0,1:T(2,128)(2,1)S(1)}, u32[]{:S(2)}, u32[]{:S(2)}) async-start(bf16[1,64,2,576]{3,2,0,1:T(2,128)(2,1)} %reshape.217), calls=%async_computation.6 | async-start | bytes 327680 | tf_op jit(solution)/shard_map/all_to_all | solution.py:88
  215.6 20.0 %all-to-all-start.5 = ((bf16[1,64,2,576]{3,2,0,1:T(2,128)(2,1)}), bf16[1,64,2,576]{3,2,0,1:T(2,128)(2,1)S(1)}, u32[]{:S(2)}, u32[]{:S(2)}) async-start(bf16[1,64,2,576]{3,2,0,1:T(2,128)(2,1)} %reshape.216), calls=%async_computation.5 | async-start | bytes 327680 | tf_op jit(solution)/shard_map/all_to_all | solution.py:87
  235.6 736.7 %all-to-all-start.7 = ((bf16[1,64,2,576]{3,2,0,1:T(2,128)(2,1)}), bf16[1,64,2,576]{3,2,0,1:T(2,128)(2,1)S(1)}, u32[]{:S(2)}, u32[]{:S(2)}) async-start(bf16[1,64,2,576]{3,2,0,1:T(2,128)(2,1)} %reshape.218), calls=%async_computation.7 | async-start | bytes 327680 | tf_op jit(solution)/shard_map/all_to_all | solution.py:89
  242.6 794.0 %reduce-scatter.4.cloned.1.call-start = ((), (), s32[]{:S(2)}) async-start(), calls=%async_computation.10 | async-start | bytes 663552
Sparse Core Ops, SparseCore 0:
  22.5 142.1 all-gather.3
  167.7 799.5 all-reduce.2
  970.4 66.2 reduce-scatter.3
where the time goes:
time: 1050 us; the launch traced here: 1040 us
  waiting for transfers between devices  892 us (85%)
  starting transfers between devices  62.3 us (6%)
  blocking collectives  36.5 us (3%)
  local copies, waits for them, and re-layouts  26.9 us (3%)
  between operations  15.4 us (1%)
    unnamed x5, waiting for transfers between devices  788 us
    all_gather x1, waiting for transfers between devices, shards(): weight = lax.all_gather(cols, 'tm', axis=0, tiled=True)  40.5 us
    all_to_all x1, blocking collectives, shards(): lax.all_to_all(attended_grad, 'tm', split_axis=2, concat_axis=1, tiled=True)  22.1 us
  transfers between devices with their start and end apart: 10, of which 9 were waited for; matrix products, arithmetic and copies ran while one was open for 3% of the time, Pallas kernels for 0%

commit v1 on v0

v1 whole, which is shorter than its diff:
```python
import jax
import jax.numpy as jnp
from jax import lax
from jax.sharding import PartitionSpec as P

D = 1152
HEADS = 8
CORES = 2
F32 = jnp.float32
BF16 = jnp.bfloat16


def slab_scores(query_slab, key_slab):
    frames, patches, feats = query_slab.shape
    qh = query_slab.reshape(frames, patches, HEADS, feats // HEADS)
    kh = key_slab.reshape(frames, patches, HEADS, feats // HEADS)
    factor = 1.0 / jnp.sqrt(F32(feats // HEADS))
    scores = jnp.einsum("fphe,gphe->phfg", qh, kh, preferred_element_type=F32) * factor
    shifted = scores - jnp.max(scores, axis=-1, keepdims=True)
    expd = jnp.exp(shifted)
    return expd / jnp.sum(expd, axis=-1, keepdims=True)


def gate_table(timestep):
    freq = jnp.exp(-jnp.log(10000.0) * jnp.arange(D).astype(F32) / D)
    return 1.5 + jnp.sin(timestep.astype(F32)[:, None] * freq[None, :])


def shards(dp_size, tm_size, queries, keys, values, out_weight, upstream, timestep):
    patches, feats = queries.shape[2:]
    head_size = feats // HEADS
    per = patches // tm_size
    factor = 1.0 / jnp.sqrt(F32(head_size))
    lines = dp_size // CORES
    dp = lax.axis_index("dp")
    line, core = dp // CORES, dp % CORES

    def shift_line(x, s):
        return lax.ppermute(x, "dp", [(d, (d + CORES * s) % dp_size) for d in range(dp_size)])

    def swap_core(x):
        return lax.ppermute(x, "dp", [(d, d ^ 1) for d in range(dp_size)])

    rows, cols = out_weight.shape
    half = lines * cols
    got = [out_weight] + [shift_line(out_weight, s) for s in range(1, lines)]
    around = jnp.stack([got[-i % lines] for i in range(2 * lines - 1)], axis=1)
    own_rows = lax.dynamic_slice_in_dim(around, (lines - line) % lines, lines, axis=1)
    own_rows = jnp.broadcast_to(
        own_rows.reshape(1, per, rows * half // per), (tm_size, per, rows * half // per)
    )
    sent = jnp.concatenate(
        [x.reshape(tm_size, per, x.shape[-1]) for x in (queries, keys, values, upstream)] + [own_rows],
        axis=2,
    )
    slab = lax.all_to_all(sent, "tm", split_axis=0, concat_axis=0, tiled=True)
    query_slab = slab[:, :, :feats]
    key_slab = slab[:, :, feats : 2 * feats]
    value_slab = slab[:, :, 2 * feats : 3 * feats]
    up_slab = slab[:, :, 3 * feats : 3 * feats + D]
    own_half = slab[:, :, 3 * feats + D :].reshape(tm_size * rows, half)
    other_half = swap_core(own_half)
    even = jnp.where(core == 0, own_half, other_half).reshape(feats, lines, 1, cols)
    odd = jnp.where(core == 0, other_half, own_half).reshape(feats, lines, 1, cols)
    weight = jnp.concatenate([even, odd], axis=2).reshape(feats, D)

    split_shape = (tm_size, per, HEADS, head_size)
    vh = value_slab.reshape(split_shape)
    probs = slab_scores(query_slab, key_slab)
    probs_low = probs.astype(BF16)
    attended = jnp.einsum("phfg,gphe->fphe", probs_low, vh, preferred_element_type=F32)
    attended = attended.astype(BF16).reshape(tm_size * per, feats)
    gate = gate_table(timestep)
    scaled = (gate * up_slab.reshape(tm_size * per, D)).astype(BF16)
    by_core = scaled.reshape(-1, lines, CORES, cols)
    mine = jnp.where(core == 0, by_core[:, :, 0], by_core[:, :, 1]).reshape(-1, half)
    theirs = jnp.where(core == 0, by_core[:, :, 1], by_core[:, :, 0]).reshape(-1, half)
    swapped = swap_core(jnp.concatenate([attended, theirs], axis=1))
    att_rows = jnp.concatenate([attended, swapped[:, :feats]], axis=0)
    scaled_rows = jnp.concatenate([mine, swapped[:, feats:]], axis=0)
    share = lax.dot_general(
        att_rows, scaled_rows, (((0,), (0,)), ((), ())), preferred_element_type=F32
    )
    share = share.astype(BF16).reshape(tm_size, per, rows * half // per)

    attended_grad = lax.dot_general(
        scaled, weight, (((1,), (1,)), ((), ())), preferred_element_type=F32
    ).astype(BF16)
    gh = attended_grad.reshape(split_shape)
    prob_grad = jnp.einsum("fphe,gphe->phfg", gh, vh, preferred_element_type=F32)
    value_grad = jnp.einsum("phfg,fphe->gphe", probs_low, gh, preferred_element_type=F32)
    inner = jnp.sum(probs * prob_grad, axis=-1, keepdims=True)
    score_grad = (probs * (prob_grad - inner)).astype(BF16)
    qh = query_slab.reshape(split_shape)
    kh = key_slab.reshape(split_shape)
    query_grad = jnp.einsum("phfg,gphe->fphe", score_grad, kh, preferred_element_type=F32) * factor
    key_grad = jnp.einsum("phfg,fphe->gphe", score_grad, qh, preferred_element_type=F32) * factor
    back = jnp.concatenate(
        [
            x.astype(BF16).reshape(tm_size, per, feats)
            for x in (attended, query_grad, key_grad, value_grad)
        ]
        + [share],
        axis=2,
    )
    frame = lax.all_to_all(back, "tm", split_axis=0, concat_axis=0, tiled=True)
    att_frame, query_back, key_back, value_back = (
        frame[:, :, i * feats : (i + 1) * feats].reshape(patches, feats) for i in range(4)
    )
    proj = lax.dot_general(att_frame, weight, (((1,), (0,)), ((), ())), preferred_element_type=F32)
    output = (gate * proj).astype(BF16).reshape(upstream.shape)
    total = jnp.sum(frame[:, :, 4 * feats :].astype(F32), axis=0).reshape(rows, lines, cols)
    weight_grad = lax.dynamic_index_in_dim(total, line, 1, keepdims=False)
    for s in range(1, lines):
        piece = lax.dynamic_index_in_dim(total, (line + s) % lines, 1, keepdims=False)
        weight_grad = weight_grad + shift_line(piece, s)
    shape = queries.shape
    return (
        output,
        query_back.reshape(shape),
        key_back.reshape(shape),
        value_back.reshape(shape),
        weight_grad,
    )


def solution(mesh):
    sizes = mesh.shape["dp"], mesh.shape["tm"]

    def body(*args):
        return shards(*sizes, *args)

    act = P("dp", "tm", None, None)
    return jax.shard_map(
        body,
        mesh=mesh,
        in_specs=(act, act, act, P("tm", "dp"), act, P("dp")),
        out_specs=(act, act, act, act, P("tm", "dp")),
        check_vma=False,
    )
```

time: 1050 us -> 183 us (0.17)
  the two profiles are of different devices: /device:TPU:4 before, /device:TPU:1 now
where the time goes in v1:
time: 183 us; the launch traced here: 182 us
  starting transfers between devices  64.4 us (35%)
  waiting for transfers between devices  63.6 us (35%)
  local copies, waits for them, and re-layouts  39.4 us (22%)
  other arithmetic  7.36 us (4%)
  matrix products  5.19 us (3%)
  between operations  2.05 us (1%)
    all_to_all x1, waiting for transfers between devices, shards(): frame = lax.all_to_all(back, 'tm', split_axis=0, concat_axis=0, tiled=True)  32 us
    all_to_all x1, waiting for transfers between devices, shards(): slab = lax.all_to_all(sent, 'tm', split_axis=0, concat_axis=0, tiled=True)  31.5 us
    ppermute x6, starting transfers between devices, shift_line(): lax.ppermute(x, 'dp', [(d, (d + CORES * s) % dp_size) for d in range(dp_s...  28.4 us
    all_to_all x1, starting transfers between devices, shards(): slab = lax.all_to_all(sent, 'tm', split_axis=0, concat_axis=0, tiled=True)  17.2 us
    all_to_all x1, starting transfers between devices, shards(): frame = lax.all_to_all(back, 'tm', split_axis=0, concat_axis=0, tiled=True)  10.2 us
    ppermute x2, starting transfers between devices, swap_core(): return lax.ppermute(x, 'dp', [(d, d ^ 1) for d in range(dp_size)])  8.65 us
    concatenate x1, local copies, waits for them, and re-layouts, shards(): jnp.concatenate([x.reshape(tm_size, per, x.shape[-1]) for x in (queries,...  7.81 us
    unnamed x41, local copies, waits for them, and re-layouts  6.98 us
  transfers between devices with their start and end apart: 10, of which 2 were waited for; matrix products, arithmetic and copies ran while one was open for 8% of the time, Pallas kernels for 0%

profile of v1, /device:TPU:1, one launch (start us, length us, event | category | flops | bytes accessed | tf_op | source)
XLA Modules:
  0.0 182.0 jit_solution(16974545590363249057)
XLA Ops:
  0.7 6.2 %collective-permute-start = (bf16[9,144]{1,0:T(8,128)(2,1)}, bf16[9,144]{1,0:T(8,128)(2,1)S(1)}, u32[]{:S(2)}, u32[]{:S(2)}) collective-permute-start(bf16[9,144]{1,0:T(8,128)(2,1)} %param.9), channel_id=1, source_target_pairs={{0,384},{64,448},{128,0},{192,64},{256,128},{320,192},{384,256},{4... | collective-permute-start | bytes 7784 | tf_op jit(solution)/shard_map/ppermute | solution.py:39
  6.8 1.9 %collective-permute-start.2 = (bf16[9,144]{1,0:T(8,128)(2,1)}, bf16[9,144]{1,0:T(8,128)(2,1)S(1)}, u32[]{:S(2)}, u32[]{:S(2)}) collective-permute-start(bf16[9,144]{1,0:T(8,128)(2,1)} %param.9), channel_id=1, source_target_pairs={{0,128},{64,192},{128,256},{192,320},{256,384},{320,448},{384,0},{... | collective-permute-start | bytes 7784 | tf_op jit(solution)/shard_map/ppermute | solution.py:39
  8.8 2.3 %collective-permute-start.1 = (bf16[9,144]{1,0:T(8,128)(2,1)}, bf16[9,144]{1,0:T(8,128)(2,1)S(1)}, u32[]{:S(2)}, u32[]{:S(2)}) collective-permute-start(bf16[9,144]{1,0:T(8,128)(2,1)} %param.9), channel_id=1, source_target_pairs={{0,256},{64,320},{128,384},{192,448},{256,0},{320,64},{384,128},{4... | collective-permute-start | bytes 7784 | tf_op jit(solution)/shard_map/ppermute | solution.py:39
  11.1 0.7 constant_dynamic-update-slice_fusion.6
  11.8 1.1 copy.56
  13.0 1.1 copy.57
  14.1 1.1 copy.58
  16.0 7.8 %concatenate.18 = bf16[64,2,5472]{2,1,0:T(2,128)(2,1)} concatenate(bf16[64,2,576]{2,1,0:T(2,128)(2,1)S(1)} %reshape.119, bf16[64,2,576]{2,1,0:T(2,128)(2,1)S(1)} %reshape.120, bf16[64,2,576]{2,1,0:T(2,128)(2,1)S(1)} %reshape.121, bf16[64,2,1152]{2,1,0:T(2,128)(2,1)S(1)} %reshape.122, bf16[64,2,2592]{2,1,0:T(2,128)(2,1)S(1)} %broadcast_in_dim.5), dimensions={2} | concatenate | bytes 2801664 | tf_op jit(solution)/shard_map/concatenate | solution.py:52
  23.9 17.2 %all-to-all-start = ((bf16[64,2,5472]{2,1,0:T(2,128)(2,1)}), bf16[64,2,5472]{2,1,0:T(2,128)(2,1)S(1)}, u32[]{:S(2)}, u32[]{:S(2)}) async-start(bf16[64,2,5472]{2,1,0:T(2,128)(2,1)} %concatenate.18), calls=%async_computation | async-start | bytes 2818048 | tf_op jit(solution)/shard_map/all_to_all | solution.py:56
  41.9 31.5 %all-to-all-done = bf16[64,2,5472]{2,1,0:T(2,128)(2,1)S(1)} async-done(((bf16[64,2,5472]{2,1,0:T(2,128)(2,1)}), bf16[64,2,5472]{2,1,0:T(2,128)(2,1)S(1)}, u32[]{:S(2)}, u32[]{:S(2)}) %all-to-all-start) | async-done | bytes 1400864 | tf_op jit(solution)/shard_map/all_to_all | solution.py:56
  73.4 0.4 fusion.57
  74.7 1.1 fusion.60
  75.8 0.5 fusion.9
  76.8 1.2 reshape.140
  78.0 1.3 slice.62
  79.2 1.2 reshape.126
  80.5 1.4 slice_convert_fusion
  81.9 3.1 %reshape.139 = f32[128,4,2,144]{3,2,1,0:T(2,128)S(1)} reshape(f32[64,2,1152]{2,1,0:T(2,128)} %slice_convert_fusion) | data formatting | bytes 1179648 | tf_op jit(solution)/shard_map/convert_element_type | solution.py:74
  85.3 1.2 broadcast_select_fusion
  86.5 0.4 copy.82
  87.1 0.8 pad_maximum_fusion.1
  88.0 6.5 %collective-permute-start.4 = (bf16[128,1152]{1,0:T(8,128)(2,1)}, bf16[128,1152]{1,0:T(8,128)(2,1)}, u32[]{:S(2)}, u32[]{:S(2)}) collective-permute-start(bf16[128,1152]{1,0:T(8,128)(2,1)} %pad_maximum_fusion.1), channel_id=1, source_target_pairs={{0,64},{64,0},{128,192},{192,128},{256,320},{320,256},{384,448},{4... | collective-permute-start | bytes 884744 | tf_op jit(solution)/shard_map/ppermute | solution.py:42
  94.5 2.1 %collective-permute-start.3 = (bf16[576,576]{1,0:T(8,128)(2,1)S(1)}, bf16[576,576]{1,0:T(8,128)(2,1)}, u32[]{:S(2)}, u32[]{:S(2)}) collective-permute-start(bf16[576,576]{1,0:T(8,128)(2,1)S(1)} %reshape.126), channel_id=1, source_target_pairs={{0,64},{64,0},{128,192},{192,128},{256,320},{320,256},{384,448},{4... | collective-permute-start | bytes 1990664 | tf_op jit(solution)/shard_map/ppermute | solution.py:42
  96.6 0.6 multiply_convert_fusion.1
  97.3 0.4 copy.84
  97.9 1.1 fusion.59
  99.1 0.4 convolution_convert_fusion
  99.5 2.1 %reshape.135 = bf16[64,2,2592]{2,1,0:T(2,128)(2,1)} reshape(bf16[576,576]{1,0:T(8,128)(2,1)S(1)} %convolution_convert_fusion) | data formatting | bytes 1327104 | tf_op jit(solution)/shard_map/reshape | solution.py:84
  101.6 1.3 broadcast_select_fusion.3
  104.0 0.7 convolution_convert_fusion.3
  105.1 0.4 fusion.10
  105.6 0.6 copy-done.8
  107.3 0.5 reshape.143
  108.0 0.5 reshape.141
  108.7 0.5 reshape.142
  109.2 6.1 %concatenate.23 = bf16[64,2,4896]{2,1,0:T(2,128)(2,1)} concatenate(bf16[64,2,576]{2,1,0:T(2,128)(2,1)S(1)} %copy-done.5, bf16[64,2,576]{2,1,0:T(2,128)(2,1)S(1)} %reshape.141, bf16[64,2,576]{2,1,0:T(2,128)(2,1)S(1)} %reshape.142, bf16[64,2,576]{2,1,0:T(2,128)(2,1)S(1)} %reshape.143, bf16[64,2,2592]{2,1,0:T(2,128)(2,1)S(1)} %copy-done), dimensions={2} | concatenate | bytes 2506752 | tf_op jit(solution)/shard_map/concatenate | solution.py:98
  115.4 10.2 %all-to-all-start.1 = ((bf16[64,2,4896]{2,1,0:T(2,128)(2,1)}), bf16[64,2,4896]{2,1,0:T(2,128)(2,1)S(1)}, u32[]{:S(2)}, u32[]{:S(2)}) async-start(bf16[64,2,4896]{2,1,0:T(2,128)(2,1)} %concatenate.23), calls=%async_computation.1 | async-start | bytes 2555904 | tf_op jit(solution)/shard_map/all_to_all | solution.py:106
  125.7 32.0 %all-to-all-done.1 = bf16[64,2,4896]{2,1,0:T(2,128)(2,1)S(1)} async-done(((bf16[64,2,4896]{2,1,0:T(2,128)(2,1)}), bf16[64,2,4896]{2,1,0:T(2,128)(2,1)S(1)}, u32[]{:S(2)}, u32[]{:S(2)}) %all-to-all-start.1) | async-done | bytes 1253408 | tf_op jit(solution)/shard_map/all_to_all | solution.py:106
  157.7 0.6 convert_reduce_fusion
  158.5 11.7 %collective-permute-start.5 = (f32[9,144]{1,0:T(8,128)S(1)}, f32[9,144]{1,0:T(8,128)S(1)}, u32[]{:S(2)}, u32[]{:S(2)}) collective-permute-start(f32[9,144]{1,0:T(8,128)S(1)} %bitcast.74), channel_id=1, source_target_pairs={{0,128},{64,192},{128,256},{192,320},{256,384},{320,448},{384,0},{... | collective-permute-start | bytes 15560 | tf_op jit(solution)/shard_map/ppermute | solution.py:39
  170.2 1.9 %collective-permute-start.6 = (f32[9,144]{1,0:T(8,128)S(1)}, f32[9,144]{1,0:T(8,128)S(1)}, u32[]{:S(2)}, u32[]{:S(2)}) collective-permute-start(f32[9,144]{1,0:T(8,128)S(1)} %bitcast.73), channel_id=1, source_target_pairs={{0,256},{64,320},{128,384},{192,448},{256,0},{320,64},{384,128},{4... | collective-permute-start | bytes 15560 | tf_op jit(solution)/shard_map/ppermute | solution.py:39
  172.2 4.3 %collective-permute-start.7 = (f32[9,144]{1,0:T(8,128)S(1)}, f32[9,144]{1,0:T(8,128)S(1)}, u32[]{:S(2)}, u32[]{:S(2)}) collective-permute-start(f32[9,144]{1,0:T(8,128)S(1)} %bitcast.72), channel_id=1, source_target_pairs={{0,384},{64,448},{128,0},{192,64},{256,128},{320,192},{384,256},{4... | collective-permute-start | bytes 15560 | tf_op jit(solution)/shard_map/ppermute | solution.py:39
  176.4 0.7 fusion.58
  177.3 1.3 fusion.2
  178.7 0.8 copy.92
  179.6 0.8 copy.91
  180.6 0.8 copy.90
  181.4 0.6 fusion.29
  (80 shorter events, 6.8 us)
Async XLA Ops:
  0.6 14.9 %copy-start.12 = (bf16[9,144]{1,0:T(8,128)(2,1)S(1)}, bf16[9,144]{1,0:T(8,128)(2,1)}, u32[]{:S(2)}) copy-start(bf16[9,144]{1,0:T(8,128)(2,1)} %param.9) | copy-start | bytes 7780
  0.6 14.7 %copy-start.9 = (bf16[1,1,128,1152]{3,2,1,0:T(8,128)(2,1)S(1)}, bf16[1,1,128,1152]{3,2,1,0:T(8,128)(2,1)}, u32[]{:S(2)}) copy-start(bf16[1,1,128,1152]{3,2,1,0:T(8,128)(2,1)} %param.10) | copy-start | bytes 884740
  0.7 14.8 %collective-permute-start = (bf16[9,144]{1,0:T(8,128)(2,1)}, bf16[9,144]{1,0:T(8,128)(2,1)S(1)}, u32[]{:S(2)}, u32[]{:S(2)}) collective-permute-start(bf16[9,144]{1,0:T(8,128)(2,1)} %param.9), channel_id=1, source_target_pairs={{0,384},{64,448},{128,0},{192,64},{256,128},{320,192},{384,256},{4... | collective-permute-start | bytes 7784 | tf_op jit(solution)/shard_map/ppermute | solution.py:39
  6.8 8.6 %collective-permute-start.2 = (bf16[9,144]{1,0:T(8,128)(2,1)}, bf16[9,144]{1,0:T(8,128)(2,1)S(1)}, u32[]{:S(2)}, u32[]{:S(2)}) collective-permute-start(bf16[9,144]{1,0:T(8,128)(2,1)} %param.9), channel_id=1, source_target_pairs={{0,128},{64,192},{128,256},{192,320},{256,384},{320,448},{384,0},{... | collective-permute-start | bytes 7784 | tf_op jit(solution)/shard_map/ppermute | solution.py:39
  8.8 6.7 %collective-permute-start.1 = (bf16[9,144]{1,0:T(8,128)(2,1)}, bf16[9,144]{1,0:T(8,128)(2,1)S(1)}, u32[]{:S(2)}, u32[]{:S(2)}) collective-permute-start(bf16[9,144]{1,0:T(8,128)(2,1)} %param.9), channel_id=1, source_target_pairs={{0,256},{64,320},{128,384},{192,448},{256,0},{320,64},{384,128},{4... | collective-permute-start | bytes 7784 | tf_op jit(solution)/shard_map/ppermute | solution.py:39
  23.9 49.5 %all-to-all-start = ((bf16[64,2,5472]{2,1,0:T(2,128)(2,1)}), bf16[64,2,5472]{2,1,0:T(2,128)(2,1)S(1)}, u32[]{:S(2)}, u32[]{:S(2)}) async-start(bf16[64,2,5472]{2,1,0:T(2,128)(2,1)} %concatenate.18), calls=%async_computation | async-start | bytes 2818048 | tf_op jit(solution)/shard_map/all_to_all | solution.py:56
  74.1 1.7 copy-start.1
  74.4 1.9 %copy-start.3 = (bf16[64,2,8,72]{3,2,1,0:T(8,128)(2,1)}, bf16[64,2,8,72]{3,2,1,0:T(8,128)(2,1)S(1)}, u32[]{:S(2)}) copy-start(bf16[64,2,8,72]{3,2,1,0:T(8,128)(2,1)S(1)} %reshape.146) | copy-start | bytes 442372
  74.7 1.7 copy-start.10
  76.8 10.4 %copy-start.6 = (bf16[128,576]{1,0:T(8,128)(2,1)}, bf16[128,576]{1,0:T(8,128)(2,1)S(1)}, u32[]{:S(2)}) copy-start(bf16[128,576]{1,0:T(8,128)(2,1)S(1)} %reshape.134) | copy-start | bytes 442372
  88.0 11.1 %copy-start.7 = (bf16[128,576]{1,0:T(8,128)(2,1)S(1)}, bf16[128,576]{1,0:T(8,128)(2,1)}, u32[]{:S(2)}) copy-start(bf16[128,576]{1,0:T(8,128)(2,1)} %copy-done.6) | copy-start | bytes 442372
  88.0 10.0 %collective-permute-start.4 = (bf16[128,1152]{1,0:T(8,128)(2,1)}, bf16[128,1152]{1,0:T(8,128)(2,1)}, u32[]{:S(2)}, u32[]{:S(2)}) collective-permute-start(bf16[128,1152]{1,0:T(8,128)(2,1)} %pad_maximum_fusion.1), channel_id=1, source_target_pairs={{0,64},{64,0},{128,192},{192,128},{256,320},{320,256},{384,448},{4... | collective-permute-start | bytes 884744 | tf_op jit(solution)/shard_map/ppermute | solution.py:42
  94.5 7.2 %collective-permute-start.3 = (bf16[576,576]{1,0:T(8,128)(2,1)S(1)}, bf16[576,576]{1,0:T(8,128)(2,1)}, u32[]{:S(2)}, u32[]{:S(2)}) collective-permute-start(bf16[576,576]{1,0:T(8,128)(2,1)S(1)} %reshape.126), channel_id=1, source_target_pairs={{0,64},{64,0},{128,192},{192,128},{256,320},{320,256},{384,448},{4... | collective-permute-start | bytes 1990664 | tf_op jit(solution)/shard_map/ppermute | solution.py:42
  104.0 1.1 copy-start.2
  104.0 1.1 copy-start.4
  105.1 1.0 copy-start.8
  105.1 1.1 copy-start.11
  107.1 2.1 %copy-start = (bf16[64,2,2592]{2,1,0:T(2,128)(2,1)S(1)}, bf16[64,2,2592]{2,1,0:T(2,128)(2,1)}, u32[]{:S(2)}) copy-start(bf16[64,2,2592]{2,1,0:T(2,128)(2,1)} %reshape.135) | copy-start | bytes 1990660
  107.1 2.1 %copy-start.5 = (bf16[64,2,576]{2,1,0:T(2,128)(2,1)S(1)}, bf16[64,2,576]{2,1,0:T(2,128)(2,1)}, u32[]{:S(2)}) copy-start(bf16[64,2,576]{2,1,0:T(2,128)(2,1)} %reshape.140) | copy-start | bytes 442372
  115.4 42.3 %all-to-all-start.1 = ((bf16[64,2,4896]{2,1,0:T(2,128)(2,1)}), bf16[64,2,4896]{2,1,0:T(2,128)(2,1)S(1)}, u32[]{:S(2)}, u32[]{:S(2)}) async-start(bf16[64,2,4896]{2,1,0:T(2,128)(2,1)} %concatenate.23), calls=%async_computation.1 | async-start | bytes 2555904 | tf_op jit(solution)/shard_map/all_to_all | solution.py:106
  158.5 22.9 %collective-permute-start.5 = (f32[9,144]{1,0:T(8,128)S(1)}, f32[9,144]{1,0:T(8,128)S(1)}, u32[]{:S(2)}, u32[]{:S(2)}) collective-permute-start(f32[9,144]{1,0:T(8,128)S(1)} %bitcast.74), channel_id=1, source_target_pairs={{0,128},{64,192},{128,256},{192,320},{256,384},{320,448},{384,0},{... | collective-permute-start | bytes 15560 | tf_op jit(solution)/shard_map/ppermute | solution.py:39
  170.2 11.1 %collective-permute-start.6 = (f32[9,144]{1,0:T(8,128)S(1)}, f32[9,144]{1,0:T(8,128)S(1)}, u32[]{:S(2)}, u32[]{:S(2)}) collective-permute-start(f32[9,144]{1,0:T(8,128)S(1)} %bitcast.73), channel_id=1, source_target_pairs={{0,256},{64,320},{128,384},{192,448},{256,0},{320,64},{384,128},{4... | collective-permute-start | bytes 15560 | tf_op jit(solution)/shard_map/ppermute | solution.py:39
  172.2 9.2 %collective-permute-start.7 = (f32[9,144]{1,0:T(8,128)S(1)}, f32[9,144]{1,0:T(8,128)S(1)}, u32[]{:S(2)}, u32[]{:S(2)}) collective-permute-start(f32[9,144]{1,0:T(8,128)S(1)} %bitcast.72), channel_id=1, source_target_pairs={{0,384},{64,448},{128,0},{192,64},{256,128},{320,192},{384,256},{4... | collective-permute-start | bytes 15560 | tf_op jit(solution)/shard_map/ppermute | solution.py:39

commit v2 on v1

v2 whole, which is shorter than its diff:
```python
import functools

import jax
import jax.numpy as jnp
import numpy as np
from jax import lax
from jax.experimental import pallas as pl
from jax.experimental.pallas import tpu as pltpu
from jax.sharding import PartitionSpec as P

D = 1152
HEADS = 8
HEAD = 72
HD = HEADS * HEAD
CORES = 2
LINES = 4
SOURCES = 64
PAIR = 2
TOKENS = SOURCES * PAIR
ROWS = HD // SOURCES
COLS = D // (CORES * LINES)
HALF = D // CORES
SPLIT = (ROWS + 1) // 2
F32 = jnp.float32
BF16 = jnp.bfloat16

W_LANES = 768
AT_U = W_LANES
AT_Q = AT_U + D
AT_K = AT_Q + HD
AT_V = AT_K + HD
IN_LANES = AT_V + HD
AT_G = 4 * HD
OUT_LANES = AT_G + SPLIT * COLS


def iota(shape, dim):
    return lax.broadcasted_iota(jnp.int32, shape, dim)


def order_matrix():
    feature, place = iota((HD, HD), 0), iota((HD, HD), 1)
    return (feature == ROWS * (place & (SOURCES - 1)) + (place >> 6)).astype(BF16)


def head_mask(head):
    return (((iota((1, HD), 1) & (SOURCES - 1)) >> 3) == head).astype(BF16)


def dot(a, b, dims, kind=F32):
    return lax.dot_general(a, b, (dims, ((), ())), preferred_element_type=F32).astype(kind)


NN = ((1,), (0,))
NT = ((1,), (1,))
TN = ((0,), (0,))


def spread(x):
    return x.reshape(SOURCES, PAIR, x.shape[-1])


def pack_kernel(
    core_ref, line_ref, w0, w1, w2, w3, q_ref, k_ref, v_ref, u_ref, x_ref, lines, feats, up, sems
):
    copies = []
    for n, ref in enumerate((q_ref, k_ref, v_ref)):
        for h in range(2):
            part = pl.ds(h * (HD // 2), HD // 2)
            copies.append(
                pltpu.make_async_copy(ref.at[part], feats.at[n, part], sems.at[2 * n + h])
            )
    for h in range(4):
        part = pl.ds(h * (TOKENS // 4), TOKENS // 4)
        copies.append(pltpu.make_async_copy(u_ref.at[part], up.at[part], sems.at[6 + h]))
    for copy in copies:
        copy.start()
    for s, ref in enumerate((w0, w1, w2, w3)):
        w = ref[...].astype(F32)
        rows = [w[i : i + 1] for i in range(ROWS)]
        for j in range(PAIR):
            part = rows[SPLIT * j : SPLIT * (j + 1)]
            pad = jnp.zeros((1, W_LANES - len(part) * COLS), F32)
            lines[s, j : j + 1, :] = jnp.concatenate(part + [pad], axis=1)
    count = TOKENS // LINES
    odd = (iota((count, W_LANES), 0) & 1) == 1
    line, parts = line_ref[0], []
    for b in range(LINES):
        pair = lines[lax.rem(line - b + LINES, LINES)]
        parts.append(jnp.where(odd, pair[1:2], pair[0:1]))
    x_ref[:, :, :W_LANES] = spread(jnp.concatenate(parts, axis=0).astype(BF16))

    order = order_matrix()
    for n, at in enumerate((AT_Q, AT_K, AT_V)):
        copies[2 * n].wait()
        copies[2 * n + 1].wait()
        x_ref[:, :, at : at + HD] = spread(dot(feats[n], order, TN, BF16))
    for copy in copies[6:]:
        copy.wait()
    first = core_ref[0] == 0
    mine, theirs = [], []
    for line in range(LINES):
        a = up[:, (2 * line) * COLS : (2 * line + 1) * COLS]
        b = up[:, (2 * line + 1) * COLS : (2 * line + 2) * COLS]
        mine.append(jnp.where(first, a, b))
        theirs.append(jnp.where(first, b, a))
    x_ref[:, :, AT_U : AT_U + D] = spread(jnp.concatenate(mine + theirs, axis=1))


def weight_kernel(x_ref, own_ref, r1_ref, r2_ref, r3_ref, w_ref, raw):
    for s, ref in enumerate((own_ref, r1_ref, r2_ref, r3_ref)):
        raw[s] = ref[...].reshape(TOKENS, W_LANES)
    x = x_ref[0]
    pick = iota((SOURCES, TOKENS), 1) - PAIR * iota((SOURCES, TOKENS), 0)
    for b in range(LINES):
        block = raw[lax.rem(x - b + LINES, LINES)]
        for j in range(PAIR):
            part = dot((pick == j).astype(BF16), block, NN, BF16)
            for i in range(SPLIT * j, min(SPLIT * (j + 1), ROWS)):
                lane = (i - SPLIT * j) * COLS
                w_ref[i * SOURCES : (i + 1) * SOURCES, b * COLS : (b + 1) * COLS] = part[
                    :, lane : lane + COLS
                ]


def rows_of(x_ref, at, lanes):
    return x_ref[:, :, at : at + lanes].reshape(TOKENS, lanes)


def scale_upstream(x_ref, gate_ref):
    return (gate_ref[...] * rows_of(x_ref, AT_U, D).astype(F32)).astype(BF16)


def forward_kernel(gate_ref, x_ref, probs_ref, swap_ref, mine_ref):
    q, k, v = (rows_of(x_ref, at, HD) for at in (AT_Q, AT_K, AT_V))
    factor = 1.0 / jnp.sqrt(F32(HEAD))
    same = ((iota((TOKENS, TOKENS), 0) ^ iota((TOKENS, TOKENS), 1)) & 1) == 0
    low, v_rows = [], []
    for h in range(HEADS):
        mask = head_mask(h)
        scores = dot(q * mask, k, NT) * factor
        scores = jnp.where(same, scores, -jnp.inf)
        expd = jnp.exp(scores - jnp.max(scores, axis=-1, keepdims=True))
        probs = expd / jnp.sum(expd, axis=-1, keepdims=True)
        probs_ref[h] = probs
        low.append(probs.astype(BF16))
        v_rows.append(v * mask)
    attended = dot(jnp.concatenate(low, axis=1), jnp.concatenate(v_rows, axis=0), NN, BF16)
    scaled = scale_upstream(x_ref, gate_ref)
    swap_ref[:, :HD] = attended
    swap_ref[:, HD:] = scaled[:, HALF:]
    mine_ref[...] = scaled[:, :HALF]


def share_kernel(line_ref, swap_ref, got_ref, mine_ref, o0_ref, o1_ref, o2_ref, o3_ref, packed):
    share = dot(swap_ref[:, :HD], mine_ref[...], TN) + dot(got_ref[:, :HD], got_ref[:, HD:], TN)
    share = share.astype(BF16)
    for b in range(LINES):
        for i in range(ROWS):
            packed[b, :, i * COLS : (i + 1) * COLS] = share[
                i * SOURCES : (i + 1) * SOURCES, b * COLS : (b + 1) * COLS
            ]
    line = line_ref[0]
    for s, ref in enumerate((o0_ref, o1_ref, o2_ref, o3_ref)):
        ref[...] = packed[lax.rem(line + s, LINES)]


def backward_kernel(gate_ref, x_ref, probs_ref, wm_ref, wt_ref, dq_ref, dk_ref, dv_ref):
    q, k, v = (rows_of(x_ref, at, HD) for at in (AT_Q, AT_K, AT_V))
    factor = 1.0 / jnp.sqrt(F32(HEAD))
    scaled = scale_upstream(x_ref, gate_ref)
    grad = dot(scaled[:, :HALF], wm_ref[...], NT) + dot(scaled[:, HALF:], wt_ref[...], NT)
    grad = grad.astype(BF16)
    low, score_grads, g_rows, q_rows, k_rows = [], [], [], [], []
    for h in range(HEADS):
        mask = head_mask(h)
        g_head = grad * mask
        probs = probs_ref[h]
        prob_grad = dot(g_head, v, NT)
        inner = jnp.sum(probs * prob_grad, axis=-1, keepdims=True)
        score_grads.append((probs * (prob_grad - inner)).astype(BF16))
        low.append(probs.astype(BF16))
        g_rows.append(g_head)
        q_rows.append(q * mask)
        k_rows.append(k * mask)
    wide = jnp.concatenate(score_grads, axis=1)
    tall = jnp.concatenate(score_grads, axis=0)
    dq_ref[...] = (dot(wide, jnp.concatenate(k_rows, axis=0), NN) * factor).astype(BF16)
    dk_ref[...] = (dot(tall, jnp.concatenate(q_rows, axis=0), TN) * factor).astype(BF16)
    dv_ref[...] = dot(jnp.concatenate(low, axis=0), jnp.concatenate(g_rows, axis=0), TN, BF16)


def sum_kernel(p0_ref, p1_ref, p2_ref, p3_ref, o_ref):
    total = sum(ref[...].astype(F32) for ref in (p0_ref, p1_ref, p2_ref, p3_ref)).astype(BF16)
    lanes = SPLIT * COLS
    pad = jnp.zeros((SOURCES, PAIR * lanes - ROWS * COLS), BF16)
    low = jnp.concatenate([total[:, lanes:], pad], axis=1)
    put = iota((TOKENS, SOURCES), 0) - PAIR * iota((TOKENS, SOURCES), 1)
    mixed = dot((put == 0).astype(BF16), total[:, :lanes], NN) + dot((put == 1).astype(BF16), low, NN)
    o_ref[...] = mixed.astype(BF16)


def back_kernel(swap_ref, dq_ref, dk_ref, dv_ref, sum_ref, x_ref):
    x_ref[:, :, :HD] = spread(swap_ref[:, :HD])
    for n, ref in enumerate((dq_ref, dk_ref, dv_ref)):
        x_ref[:, :, (n + 1) * HD : (n + 2) * HD] = spread(ref[...])
    x_ref[:, :, AT_G:OUT_LANES] = spread(sum_ref[...])


def final_kernel(
    core_ref, gate_ref, z_ref, wm_ref, wt_ref, out_ref, dq_ref, dk_ref, dv_ref, wg_ref
):
    att = rows_of(z_ref, 0, HD)
    gate = gate_ref[...]
    mine = (gate[:, :HALF] * dot(att, wm_ref[...], NN)).astype(BF16)
    theirs = (gate[:, HALF:] * dot(att, wt_ref[...], NN)).astype(BF16)
    first = core_ref[0] == 0
    parts = []
    for line in range(LINES):
        a = mine[:, line * COLS : (line + 1) * COLS]
        b = theirs[:, line * COLS : (line + 1) * COLS]
        parts += [jnp.where(first, a, b), jnp.where(first, b, a)]
    out_ref[...] = jnp.concatenate(parts, axis=1)
    order = order_matrix()
    for n, ref in enumerate((dq_ref, dk_ref, dv_ref)):
        ref[...] = dot(order, rows_of(z_ref, (n + 1) * HD, HD), NT, BF16)
    pick = ((iota((8, TOKENS), 1) & 1) == iota((8, TOKENS), 0)).astype(BF16)
    sums = dot(pick, rows_of(z_ref, AT_G, SPLIT * COLS), NN)
    for i in range(ROWS):
        j, lane = i // SPLIT, (i % SPLIT) * COLS
        wg_ref[i : i + 1, :] = sums[j : j + 1, lane : lane + COLS]


def call(kernel, outs, args, scalars=0, far=0, scratch=(), flops=10**8, limit=24):
    smem = [pl.BlockSpec(memory_space=pltpu.SMEM)] * scalars
    vmem = [pl.BlockSpec(memory_space=pltpu.VMEM)] * (len(args) - scalars - far)
    hbm = [pl.BlockSpec(memory_space=pltpu.HBM)] * far
    moved = sum(int(np.prod(x.shape)) * x.dtype.itemsize for x in [*args, *outs])
    single = len(outs) == 1
    out_spec = [pl.BlockSpec(memory_space=pltpu.VMEM)] * len(outs)
    return pl.pallas_call(
        kernel,
        out_shape=outs[0] if single else outs,
        in_specs=smem + vmem + hbm,
        out_specs=out_spec[0] if single else out_spec,
        scratch_shapes=scratch,
        cost_estimate=pl.CostEstimate(flops=flops, bytes_accessed=moved, transcendentals=0),
        compiler_params=pltpu.CompilerParams(vmem_limit_bytes=limit * 1024 * 1024),
    )(*args)


def shape(*dims, kind=BF16):
    return jax.ShapeDtypeStruct(dims, kind)


def column_order():
    cols = np.arange(D).reshape(LINES, CORES, COLS)
    return [np.concatenate([cols[:, c].ravel(), cols[:, 1 - c].ravel()]) for c in range(CORES)]


def shards(dp_size, queries, keys, values, out_weight, upstream, timestep):
    dp = lax.axis_index("dp")
    line, core = (dp // CORES).astype(jnp.int32), (dp % CORES).astype(jnp.int32)
    line_s, core_s = line.reshape(1), core.reshape(1)
    x_s = (lax.axis_index("tm") // (SOURCES // LINES)).astype(jnp.int32).reshape(1)

    def shift_line(x, s):
        return lax.ppermute(x, "dp", [(d, (d + CORES * s) % dp_size) for d in range(dp_size)])

    def shift_x(x, s):
        step = SOURCES // LINES
        return lax.ppermute(x, "tm", [(t, (t + step * s) % SOURCES) for t in range(SOURCES)])

    def swap_core(x):
        return lax.ppermute(x, "dp", [(d, d ^ 1) for d in range(dp_size)])

    orders = [o.astype(np.float32) for o in column_order()]
    index = jnp.where(core == 0, orders[0], orders[1])
    freq = jnp.exp(-jnp.log(10000.0) * index / D)
    gate = (1.5 + jnp.sin(timestep.astype(F32)[0] * freq)).reshape(1, D)

    flat = [x.reshape(TOKENS, HD).T for x in (queries, keys, values)]
    weights = [out_weight] + [shift_line(out_weight, s) for s in range(1, LINES)]
    sent = call(
        pack_kernel,
        [shape(SOURCES, PAIR, IN_LANES)],
        (core_s, line_s, *weights, *flat, upstream.reshape(TOKENS, D)),
        scalars=2,
        far=4,
        limit=60,
        scratch=[
            pltpu.VMEM((LINES, 8, W_LANES), F32),
            pltpu.VMEM((3, HD, TOKENS), BF16),
            pltpu.VMEM((TOKENS, D), BF16),
            pltpu.SemaphoreType.DMA((10,)),
        ],
    )
    slab = lax.all_to_all(sent, "tm", split_axis=0, concat_axis=0, tiled=True)

    probs, swap, mine = call(
        forward_kernel,
        [shape(HEADS, TOKENS, TOKENS, kind=F32), shape(TOKENS, HD + HALF), shape(TOKENS, HALF)],
        (gate, slab),
    )
    got = swap_core(swap)
    own_raw, _ = lax.optimization_barrier((slab[:, :, :W_LANES], swap))
    raws = [own_raw] + [shift_x(own_raw, s) for s in range(1, LINES)]
    pieces = call(
        share_kernel,
        [shape(SOURCES, ROWS * COLS)] * LINES,
        (line_s, swap, got, mine),
        scalars=1,
        scratch=[pltpu.VMEM((LINES, SOURCES, ROWS * COLS), BF16)],
    )
    sums = [pieces[0]] + [shift_line(pieces[s], s) for s in range(1, LINES)]
    x_late, _ = lax.optimization_barrier((x_s, pieces[0]))
    w_mine = call(
        weight_kernel,
        [shape(HD, HALF)],
        (x_late, *raws),
        scalars=1,
        scratch=[pltpu.VMEM((LINES, TOKENS, W_LANES), BF16)],
    )
    w_theirs = swap_core(w_mine)
    grads = call(
        backward_kernel, [shape(TOKENS, HD)] * 3, (gate, slab, probs, w_mine, w_theirs), flops=10**9
    )
    total = call(sum_kernel, [shape(TOKENS, SPLIT * COLS)], sums, flops=10**10)
    back = call(back_kernel, [shape(SOURCES, PAIR, OUT_LANES)], (swap, *grads, total))
    frame = lax.all_to_all(back, "tm", split_axis=0, concat_axis=0, tiled=True)
    output, dq, dk, dv, weight_grad = call(
        final_kernel,
        [shape(TOKENS, D)] + [shape(HD, TOKENS)] * 3 + [shape(ROWS, COLS, kind=F32)],
        (core_s, gate, frame, w_mine, w_theirs),
        scalars=1,
    )
    dims = queries.shape
    return (output.reshape(upstream.shape), *(x.T.reshape(dims) for x in (dq, dk, dv)), weight_grad)


def solution(mesh):
    act = P("dp", "tm", None, None)
    return jax.shard_map(
        functools.partial(shards, mesh.shape["dp"]),
        mesh=mesh,
        in_specs=(act, act, act, P("tm", "dp"), act, P("dp")),
        out_specs=(act, act, act, act, P("tm", "dp")),
        check_vma=False,
    )
```

time: 183 us -> 142 us (0.78)
  local copies, waits for them, and re-layouts: 39.4 us -> 0.76 us
  waiting for transfers between devices: 63.6 us -> 31.3 us
  blocking collectives: 0 us -> 31.7 us
  Pallas kernels: 0 us -> 13.7 us
  other arithmetic: 7.36 us -> 0.06 us
  matrix products: 5.19 us -> 0 us
  starting transfers between devices: 64.4 us -> 62.3 us
    all_to_all x1 -> x0, waiting for transfers between devices: 32 us -> none  [shards(): frame = lax.all_to_all(back, 'tm', split_axis=0, concat_axis=0, tiled=True)]
    all_to_all x0 -> x1, blocking collectives: none -> 31.7 us  [shards(): frame = lax.all_to_all(back, 'tm', split_axis=0, concat_axis=0, tiled=True)]
    concatenate x3 -> x0, local copies, waits for them, and re-layouts: 14.1 us -> none  [the longest x1 7.81 us: shards(): jnp.concatenate([x.reshape(tm_size, per, x.shape[-1]) for x in (queries,...]
    pallas_call x0 -> x8, Pallas kernels: none -> 13.7 us  [call(): pl.pallas_call(kernel, out_shape=outs[0] if single else outs, in_specs=sm...]
    all_to_all x1, waiting for transfers between devices: 31.5 us -> 20.4 us  [shards(): slab = lax.all_to_all(sent, 'tm', split_axis=0, concat_axis=0, tiled=True)]
    ppermute x6, waiting for transfers between devices: 0.02 us -> 10.9 us  [shift_line(): lax.ppermute(x, 'dp', [(d, (d + CORES * s) % dp_size) for d in range(dp_s...]
    ppermute x0 -> x3, starting transfers between devices: none -> 10.3 us  [shift_x(): lax.ppermute(x, 'tm', [(t, (t + step * s) % SOURCES) for t in range(SOURC...]
    all_to_all x1 -> x0, starting transfers between devices: 10.2 us -> none  [shards(): frame = lax.all_to_all(back, 'tm', split_axis=0, concat_axis=0, tiled=True)]
  transfers between devices with their start and end apart: 10 -> 12, of which waited for: 2 -> 3; matrix products, arithmetic and copies ran while one was open for 8% -> 0% of each run, Pallas kernels for 0% -> 2%
where the time goes in v2:
time: 142 us; the launch traced here: 141 us
  starting transfers between devices  62.3 us (44%)
  blocking collectives  31.7 us (22%)
  waiting for transfers between devices  31.3 us (22%)
  Pallas kernels  13.7 us (10%)
  between operations  1.59 us (1%)
    all_to_all x1, blocking collectives, shards(): frame = lax.all_to_all(back, 'tm', split_axis=0, concat_axis=0, tiled=True)  31.7 us
    ppermute x6, starting transfers between devices, shift_line(): lax.ppermute(x, 'dp', [(d, (d + CORES * s) % dp_size) for d in range(dp_s...  23.6 us
    all_to_all x1, waiting for transfers between devices, shards(): slab = lax.all_to_all(sent, 'tm', split_axis=0, concat_axis=0, tiled=True)  20.4 us
    all_to_all x1, starting transfers between devices, shards(): slab = lax.all_to_all(sent, 'tm', split_axis=0, concat_axis=0, tiled=True)  17 us
    pallas_call x8, Pallas kernels, call(): pl.pallas_call(kernel, out_shape=outs[0] if single else outs, in_specs=sm...  13.7 us
    ppermute x2, starting transfers between devices, swap_core(): return lax.ppermute(x, 'dp', [(d, d ^ 1) for d in range(dp_size)])  11.5 us
    ppermute x6, waiting for transfers between devices, shift_line(): lax.ppermute(x, 'dp', [(d, (d + CORES * s) % dp_size) for d in range(dp_s...  10.9 us
    ppermute x3, starting transfers between devices, shift_x(): lax.ppermute(x, 'tm', [(t, (t + step * s) % SOURCES) for t in range(SOURC...  10.3 us
  transfers between devices with their start and end apart: 12, of which 3 were waited for; matrix products, arithmetic and copies ran while one was open for 0% of the time, Pallas kernels for 2%

profile of v2, /device:TPU:1, one launch (start us, length us, event | category | flops | bytes accessed | tf_op | source)
XLA Modules:
  0.0 141.4 jit_solution(17754627321948536764)
XLA Ops:
  0.6 4.0 %collective-permute-start = (bf16[9,144]{1,0:T(8,128)(2,1)}, bf16[9,144]{1,0:T(8,128)(2,1)S(1)}, u32[]{:S(2)}, u32[]{:S(2)}) collective-permute-start(bf16[9,144]{1,0:T(8,128)(2,1)} %w0.1), channel_id=1, source_target_pairs={{0,128},{64,192},{128,256},{192,320},{256,384},{320,448},{384,0},{... | collective-permute-start | bytes 7784 | tf_op jit(solution)/shard_map/ppermute | solution.py:268
  4.7 4.2 %collective-permute-start.1 = (bf16[9,144]{1,0:T(8,128)(2,1)}, bf16[9,144]{1,0:T(8,128)(2,1)S(1)}, u32[]{:S(2)}, u32[]{:S(2)}) collective-permute-start(bf16[9,144]{1,0:T(8,128)(2,1)} %w0.1), channel_id=1, source_target_pairs={{0,256},{64,320},{128,384},{192,448},{256,0},{320,64},{384,128},{4... | collective-permute-start | bytes 7784 | tf_op jit(solution)/shard_map/ppermute | solution.py:268
  8.9 3.0 %collective-permute-start.2 = (bf16[9,144]{1,0:T(8,128)(2,1)}, bf16[9,144]{1,0:T(8,128)(2,1)S(1)}, u32[]{:S(2)}, u32[]{:S(2)}) collective-permute-start(bf16[9,144]{1,0:T(8,128)(2,1)} %w0.1), channel_id=1, source_target_pairs={{0,384},{64,448},{128,0},{192,64},{256,128},{320,192},{384,256},{4... | collective-permute-start | bytes 7784 | tf_op jit(solution)/shard_map/ppermute | solution.py:268
  11.9 0.0 collective-permute-done.w1
  11.9 0.0 copy-start
  11.9 0.0 collective-permute-done.1.w2
  11.9 0.0 copy-start.1
  11.9 1.9 %collective-permute-done.2.w3 = bf16[9,144]{1,0:T(8,128)(2,1)S(1)} collective-permute-done((bf16[9,144]{1,0:T(8,128)(2,1)}, bf16[9,144]{1,0:T(8,128)(2,1)S(1)}, u32[]{:S(2)}, u32[]{:S(2)}) %collective-permute-start.2) | collective-permute-done | bytes 2624 | tf_op jit(solution)/shard_map/ppermute | solution.py:268
  13.8 0.0 copy-start.2
  13.8 0.0 copy-done
  13.8 0.0 copy-done.1
  13.8 0.6 copy-done.2
  14.4 4.3 %shard_map.119 = bf16[64,2,3648]{2,1,0:T(2,128)(2,1)} custom-call(s32[1]{0:T(128)} %bitcast.core_ref, s32[1]{0:T(128)} %bitcast.2.line_ref, bf16[9,144]{1,0:T(8,128)(2,1)} %w0.1, bf16[9,144]{1,0:T(8,128)(2,1)} %copy-done, bf16[9,144]{1,0:T(8,128)(2,1)} %copy-done.1, bf16[9,144]{1,0:T(8,128)(2,1)} %copy-done.2, bf16[576,128]{1,0:T(8,128)(2,1)} %bitcast.25, ...), custom_call_target="tpu_custom_call" | custom-call | flops 100000000 | bytes 1681544 | tf_op jit(solution)/shard_map/pallas_call | solution.py:241
  18.7 0.0 copy-start.3
  18.7 0.0 copy-start.4
  18.7 17.0 %all-to-all-start = ((bf16[64,2,3648]{2,1,0:T(2,128)(2,1)}), bf16[64,2,3648]{2,1,0:T(2,128)(2,1)S(1)}, u32[]{:S(2)}, u32[]{:S(2)}) async-start(bf16[64,2,3648]{2,1,0:T(2,128)(2,1)} %shard_map.119), calls=%async_computation | async-start | bytes 1900544 | tf_op jit(solution)/shard_map/all_to_all | solution.py:298
  36.3 0.0 copy-done.3
  36.4 0.0 copy-done.4
  36.4 0.1 sine_add_fusion
  36.4 20.4 %all-to-all-done.x_ref = bf16[64,2,3648]{2,1,0:T(2,128)(2,1)S(1)} async-done(((bf16[64,2,3648]{2,1,0:T(2,128)(2,1)}), bf16[64,2,3648]{2,1,0:T(2,128)(2,1)S(1)}, u32[]{:S(2)}, u32[]{:S(2)}) %all-to-all-start) | async-done | bytes 933920 | tf_op jit(solution)/shard_map/all_to_all | solution.py:298
  56.8 1.3 shard_map.120
  58.2 8.3 %collective-permute-start.3 = (bf16[128,1152]{1,0:T(8,128)(2,1)S(1)}, bf16[128,1152]{1,0:T(8,128)(2,1)S(1)}, u32[]{:S(2)}, u32[]{:S(2)}) collective-permute-start(bf16[128,1152]{1,0:T(8,128)(2,1)S(1)} %get-tuple-element.22.swap_ref), channel_id=1, source_target_pairs={{0,64},{64,0},{128,192},{192,128},{256,320},{320,256},{384,448},{4... | collective-permute-start | bytes 884744 | tf_op jit(solution)/shard_map/ppermute | solution.py:275
  66.5 0.1 slice.4.own_ref
  66.6 3.1 %collective-permute-start.4 = (bf16[64,2,768]{2,1,0:T(2,128)(2,1)S(1)}, bf16[64,2,768]{2,1,0:T(2,128)(2,1)S(1)}, u32[]{:S(2)}, u32[]{:S(2)}) collective-permute-start(bf16[64,2,768]{2,1,0:T(2,128)(2,1)S(1)} %slice.4.own_ref), channel_id=1, source_target_pairs={{0,16},{1,17},{2,18},{3,19},{4,20},{5,21},{6,22},{7,23},{8,24},{9,... | collective-permute-start | bytes 589832 | tf_op jit(solution)/shard_map/ppermute | solution.py:272
  69.7 3.2 %collective-permute-start.5 = (bf16[64,2,768]{2,1,0:T(2,128)(2,1)S(1)}, bf16[64,2,768]{2,1,0:T(2,128)(2,1)S(1)}, u32[]{:S(2)}, u32[]{:S(2)}) collective-permute-start(bf16[64,2,768]{2,1,0:T(2,128)(2,1)S(1)} %slice.4.own_ref), channel_id=1, source_target_pairs={{0,32},{1,33},{2,34},{3,35},{4,36},{5,37},{6,38},{7,39},{8,40},{9,... | collective-permute-start | bytes 589832 | tf_op jit(solution)/shard_map/ppermute | solution.py:272
  72.9 4.0 %collective-permute-start.6 = (bf16[64,2,768]{2,1,0:T(2,128)(2,1)S(1)}, bf16[64,2,768]{2,1,0:T(2,128)(2,1)S(1)}, u32[]{:S(2)}, u32[]{:S(2)}) collective-permute-start(bf16[64,2,768]{2,1,0:T(2,128)(2,1)S(1)} %slice.4.own_ref), channel_id=1, source_target_pairs={{0,48},{1,49},{2,50},{3,51},{4,52},{5,53},{6,54},{7,55},{8,56},{9,... | collective-permute-start | bytes 589832 | tf_op jit(solution)/shard_map/ppermute | solution.py:272
  76.9 0.0 collective-permute-done.3.got_ref
  76.9 1.6 %shard_map.121 = (bf16[64,1296]{1,0:T(8,128)(2,1)S(1)}, bf16[64,1296]{1,0:T(8,128)(2,1)S(1)}, bf16[64,1296]{1,0:T(8,128)(2,1)S(1)}, bf16[64,1296]{1,0:T(8,128)(2,1)}) custom-call(s32[1]{0:T(128)} %bitcast.2.line_ref, bf16[128,1152]{1,0:T(8,128)(2,1)S(1)} %get-tuple-element.22.swap_ref, bf16[128,1152]{1,0:T(8,128)(2,1)S(1)} %collective-permute-done.3.got_ref, ...), custom_call_target="tpu_custom_call" | custom-call | flops 100000000 | bytes 1400836 | tf_op jit(solution)/shard_map/pallas_call | solution.py:241
  78.5 4.9 %collective-permute-start.10 = (bf16[64,1296]{1,0:T(8,128)(2,1)}, bf16[64,1296]{1,0:T(8,128)(2,1)S(1)}, u32[]{:S(2)}, u32[]{:S(2)}) collective-permute-start(bf16[64,1296]{1,0:T(8,128)(2,1)} %get-tuple-element.33), channel_id=1, source_target_pairs={{0,384},{64,448},{128,0},{192,64},{256,128},{320,192},{384,256},{4... | collective-permute-start | bytes 497672 | tf_op jit(solution)/shard_map/ppermute | solution.py:268
  83.4 4.4 %collective-permute-start.8 = (bf16[64,1296]{1,0:T(8,128)(2,1)S(1)}, bf16[64,1296]{1,0:T(8,128)(2,1)S(1)}, u32[]{:S(2)}, u32[]{:S(2)}) collective-permute-start(bf16[64,1296]{1,0:T(8,128)(2,1)S(1)} %get-tuple-element.31), channel_id=1, source_target_pairs={{0,128},{64,192},{128,256},{192,320},{256,384},{320,448},{384,0},{... | collective-permute-start | bytes 497672 | tf_op jit(solution)/shard_map/ppermute | solution.py:268
  87.8 0.0 collective-permute-done.4.r1_ref
  87.8 3.1 %collective-permute-start.9 = (bf16[64,1296]{1,0:T(8,128)(2,1)S(1)}, bf16[64,1296]{1,0:T(8,128)(2,1)}, u32[]{:S(2)}, u32[]{:S(2)}) collective-permute-start(bf16[64,1296]{1,0:T(8,128)(2,1)S(1)} %get-tuple-element.32), channel_id=1, source_target_pairs={{0,256},{64,320},{128,384},{192,448},{256,0},{320,64},{384,128},{4... | collective-permute-start | bytes 497672 | tf_op jit(solution)/shard_map/ppermute | solution.py:268
  90.9 0.0 collective-permute-done.5.r2_ref
  90.9 0.0 collective-permute-done.6.r3_ref
  90.9 0.6 shard_map.122.wm_ref
  91.5 3.2 %collective-permute-start.7 = (bf16[576,576]{1,0:T(8,128)(2,1)S(1)}, bf16[576,576]{1,0:T(8,128)(2,1)S(1)}, u32[]{:S(2)}, u32[]{:S(2)}) collective-permute-start(bf16[576,576]{1,0:T(8,128)(2,1)S(1)} %shard_map.122.wm_ref), channel_id=1, source_target_pairs={{0,64},{64,0},{128,192},{192,128},{256,320},{320,256},{384,448},{4... | collective-permute-start | bytes 1990664 | tf_op jit(solution)/shard_map/ppermute | solution.py:275
  94.8 0.0 collective-permute-done.10.p3_ref
  94.8 0.0 collective-permute-done.8.p1_ref
  94.8 9.0 %collective-permute-done.9.p2_ref = bf16[64,1296]{1,0:T(8,128)(2,1)} collective-permute-done((bf16[64,1296]{1,0:T(8,128)(2,1)S(1)}, bf16[64,1296]{1,0:T(8,128)(2,1)}, u32[]{:S(2)}, u32[]{:S(2)}) %collective-permute-start.9) | collective-permute-done | bytes 165920 | tf_op jit(solution)/shard_map/ppermute | solution.py:268
  103.8 1.3 shard_map.124.sum_ref
  105.1 0.0 collective-permute-done.7.wt_ref
  105.1 2.5 %shard_map.123 = (bf16[128,576]{1,0:T(8,128)(2,1)S(1)}, bf16[128,576]{1,0:T(8,128)(2,1)S(1)}, bf16[128,576]{1,0:T(8,128)(2,1)S(1)}) custom-call(f32[1,1152]{1,0:T(1,128)S(1)} %reshape.47.gate_ref, bf16[64,2,3648]{2,1,0:T(2,128)(2,1)S(1)} %all-to-all-done.x_ref, f32[8,128,128]{2,1,0:T(8,128)S(1)} %get-tuple-element.23.probs_ref, ...), custom_call_target="tpu_custom_call" | custom-call | flops 1000000000 | bytes 3232256 | tf_op jit(solution)/shard_map/pallas_call | solution.py:241
  107.6 0.2 shard_map.125
  107.8 31.7 %all_to_all.10.z_ref = bf16[64,2,3024]{2,1,0:T(2,128)(2,1)S(1)} all-to-all(bf16[64,2,3024]{2,1,0:T(2,128)(2,1)S(1)} %shard_map.125), channel_id=1, replica_groups=mesh['dp'=8,'tm'=64] {'tm'}, dimensions={0} | all-to-all | bytes 1548288 | tf_op jit(solution)/shard_map/all_to_all | solution.py:330
  139.4 2.0 %shard_map.126 = (bf16[128,1152]{1,0:T(8,128)(2,1)}, bf16[576,128]{1,0:T(8,128)(2,1)}, bf16[576,128]{1,0:T(8,128)(2,1)}, bf16[576,128]{1,0:T(8,128)(2,1)}, f32[9,144]{1,0:T(8,128)}) custom-call(s32[1]{0:T(128)} %bitcast.core_ref, f32[1,1152]{1,0:T(1,128)S(1)} %reshape.47.gate_ref, bf16[64,2,3024]{2,1,0:T(2,128)(2,1)S(1)} %all_to_all.10.z_ref, ...), custom_call_target="tpu_custom_call" | custom-call | flops 100000000 | bytes 2848324 | tf_op jit(solution)/shard_map/pallas_call | solution.py:241
  (1 shorter events, 0.0 us)
Async XLA Ops:
  0.6 11.3 %collective-permute-start = (bf16[9,144]{1,0:T(8,128)(2,1)}, bf16[9,144]{1,0:T(8,128)(2,1)S(1)}, u32[]{:S(2)}, u32[]{:S(2)}) collective-permute-start(bf16[9,144]{1,0:T(8,128)(2,1)} %w0.1), channel_id=1, source_target_pairs={{0,128},{64,192},{128,256},{192,320},{256,384},{320,448},{384,0},{... | collective-permute-start | bytes 7784 | tf_op jit(solution)/shard_map/ppermute | solution.py:268
  4.7 7.3 %collective-permute-start.1 = (bf16[9,144]{1,0:T(8,128)(2,1)}, bf16[9,144]{1,0:T(8,128)(2,1)S(1)}, u32[]{:S(2)}, u32[]{:S(2)}) collective-permute-start(bf16[9,144]{1,0:T(8,128)(2,1)} %w0.1), channel_id=1, source_target_pairs={{0,256},{64,320},{128,384},{192,448},{256,0},{320,64},{384,128},{4... | collective-permute-start | bytes 7784 | tf_op jit(solution)/shard_map/ppermute | solution.py:268
  8.9 4.9 %collective-permute-start.2 = (bf16[9,144]{1,0:T(8,128)(2,1)}, bf16[9,144]{1,0:T(8,128)(2,1)S(1)}, u32[]{:S(2)}, u32[]{:S(2)}) collective-permute-start(bf16[9,144]{1,0:T(8,128)(2,1)} %w0.1), channel_id=1, source_target_pairs={{0,384},{64,448},{128,0},{192,64},{256,128},{320,192},{384,256},{4... | collective-permute-start | bytes 7784 | tf_op jit(solution)/shard_map/ppermute | solution.py:268
  11.9 1.9 %copy-start = (bf16[9,144]{1,0:T(8,128)(2,1)}, bf16[9,144]{1,0:T(8,128)(2,1)S(1)}, u32[]{:S(2)}) copy-start(bf16[9,144]{1,0:T(8,128)(2,1)S(1)} %collective-permute-done.w1) | copy-start | bytes 7780
  11.9 1.9 %copy-start.1 = (bf16[9,144]{1,0:T(8,128)(2,1)}, bf16[9,144]{1,0:T(8,128)(2,1)S(1)}, u32[]{:S(2)}) copy-start(bf16[9,144]{1,0:T(8,128)(2,1)S(1)} %collective-permute-done.1.w2) | copy-start | bytes 7780
  13.8 0.6 copy-start.2
  18.7 17.7 %copy-start.3 = (f32[1152]{0:T(1024)S(1)}, f32[1152]{0:T(1024)}, u32[]{:S(2)}) copy-start(f32[1152]{0:T(1024)} %constant.56.clone) | copy-start | bytes 13828
  18.7 17.7 %copy-start.4 = (f32[1152]{0:T(1024)S(1)}, f32[1152]{0:T(1024)}, u32[]{:S(2)}) copy-start(f32[1152]{0:T(1024)} %constant.57.clone) | copy-start | bytes 13828
  18.7 38.1 %all-to-all-start = ((bf16[64,2,3648]{2,1,0:T(2,128)(2,1)}), bf16[64,2,3648]{2,1,0:T(2,128)(2,1)S(1)}, u32[]{:S(2)}, u32[]{:S(2)}) async-start(bf16[64,2,3648]{2,1,0:T(2,128)(2,1)} %shard_map.119), calls=%async_computation | async-start | bytes 1900544 | tf_op jit(solution)/shard_map/all_to_all | solution.py:298
  58.2 18.7 %collective-permute-start.3 = (bf16[128,1152]{1,0:T(8,128)(2,1)S(1)}, bf16[128,1152]{1,0:T(8,128)(2,1)S(1)}, u32[]{:S(2)}, u32[]{:S(2)}) collective-permute-start(bf16[128,1152]{1,0:T(8,128)(2,1)S(1)} %get-tuple-element.22.swap_ref), channel_id=1, source_target_pairs={{0,64},{64,0},{128,192},{192,128},{256,320},{320,256},{384,448},{4... | collective-permute-start | bytes 884744 | tf_op jit(solution)/shard_map/ppermute | solution.py:275
  66.6 21.2 %collective-permute-start.4 = (bf16[64,2,768]{2,1,0:T(2,128)(2,1)S(1)}, bf16[64,2,768]{2,1,0:T(2,128)(2,1)S(1)}, u32[]{:S(2)}, u32[]{:S(2)}) collective-permute-start(bf16[64,2,768]{2,1,0:T(2,128)(2,1)S(1)} %slice.4.own_ref), channel_id=1, source_target_pairs={{0,16},{1,17},{2,18},{3,19},{4,20},{5,21},{6,22},{7,23},{8,24},{9,... | collective-permute-start | bytes 589832 | tf_op jit(solution)/shard_map/ppermute | solution.py:272
  69.7 21.2 %collective-permute-start.5 = (bf16[64,2,768]{2,1,0:T(2,128)(2,1)S(1)}, bf16[64,2,768]{2,1,0:T(2,128)(2,1)S(1)}, u32[]{:S(2)}, u32[]{:S(2)}) collective-permute-start(bf16[64,2,768]{2,1,0:T(2,128)(2,1)S(1)} %slice.4.own_ref), channel_id=1, source_target_pairs={{0,32},{1,33},{2,34},{3,35},{4,36},{5,37},{6,38},{7,39},{8,40},{9,... | collective-permute-start | bytes 589832 | tf_op jit(solution)/shard_map/ppermute | solution.py:272
  72.9 18.0 %collective-permute-start.6 = (bf16[64,2,768]{2,1,0:T(2,128)(2,1)S(1)}, bf16[64,2,768]{2,1,0:T(2,128)(2,1)S(1)}, u32[]{:S(2)}, u32[]{:S(2)}) collective-permute-start(bf16[64,2,768]{2,1,0:T(2,128)(2,1)S(1)} %slice.4.own_ref), channel_id=1, source_target_pairs={{0,48},{1,49},{2,50},{3,51},{4,52},{5,53},{6,54},{7,55},{8,56},{9,... | collective-permute-start | bytes 589832 | tf_op jit(solution)/shard_map/ppermute | solution.py:272
  78.5 16.3 %collective-permute-start.10 = (bf16[64,1296]{1,0:T(8,128)(2,1)}, bf16[64,1296]{1,0:T(8,128)(2,1)S(1)}, u32[]{:S(2)}, u32[]{:S(2)}) collective-permute-start(bf16[64,1296]{1,0:T(8,128)(2,1)} %get-tuple-element.33), channel_id=1, source_target_pairs={{0,384},{64,448},{128,0},{192,64},{256,128},{320,192},{384,256},{4... | collective-permute-start | bytes 497672 | tf_op jit(solution)/shard_map/ppermute | solution.py:268
  83.4 11.5 %collective-permute-start.8 = (bf16[64,1296]{1,0:T(8,128)(2,1)S(1)}, bf16[64,1296]{1,0:T(8,128)(2,1)S(1)}, u32[]{:S(2)}, u32[]{:S(2)}) collective-permute-start(bf16[64,1296]{1,0:T(8,128)(2,1)S(1)} %get-tuple-element.31), channel_id=1, source_target_pairs={{0,128},{64,192},{128,256},{192,320},{256,384},{320,448},{384,0},{... | collective-permute-start | bytes 497672 | tf_op jit(solution)/shard_map/ppermute | solution.py:268
  87.8 16.0 %collective-permute-start.9 = (bf16[64,1296]{1,0:T(8,128)(2,1)S(1)}, bf16[64,1296]{1,0:T(8,128)(2,1)}, u32[]{:S(2)}, u32[]{:S(2)}) collective-permute-start(bf16[64,1296]{1,0:T(8,128)(2,1)S(1)} %get-tuple-element.32), channel_id=1, source_target_pairs={{0,256},{64,320},{128,384},{192,448},{256,0},{320,64},{384,128},{4... | collective-permute-start | bytes 497672 | tf_op jit(solution)/shard_map/ppermute | solution.py:268
  91.5 13.6 %collective-permute-start.7 = (bf16[576,576]{1,0:T(8,128)(2,1)S(1)}, bf16[576,576]{1,0:T(8,128)(2,1)S(1)}, u32[]{:S(2)}, u32[]{:S(2)}) collective-permute-start(bf16[576,576]{1,0:T(8,128)(2,1)S(1)} %shard_map.122.wm_ref), channel_id=1, source_target_pairs={{0,64},{64,0},{128,192},{192,128},{256,320},{320,256},{384,448},{4... | collective-permute-start | bytes 1990664 | tf_op jit(solution)/shard_map/ppermute | solution.py:275

commit v3 on v2

--- a/solution.py
+++ b/solution.py
@@ -1,5 +1,3 @@
-import functools
-
 import jax
 import jax.numpy as jnp
 import numpy as np
@@ -24,8 +22,12 @@
 F32 = jnp.float32
 BF16 = jnp.bfloat16
 
-W_LANES = 768
-AT_U = W_LANES
+AXES = {"line": LINES, "core": CORES, "x": 4, "y": 2, "z": 8}
+OTHERS = ("x", "y", "z")
+W_PEERS = LINES * SOURCES
+W_LANES = (ROWS + 1) // 2 * COLS
+
+AT_U = 0
 AT_Q = AT_U + D
 AT_K = AT_Q + HD
 AT_V = AT_K + HD
@@ -60,42 +62,43 @@
     return x.reshape(SOURCES, PAIR, x.shape[-1])
 
 
-def pack_kernel(
-    core_ref, line_ref, w0, w1, w2, w3, q_ref, k_ref, v_ref, u_ref, x_ref, lines, feats, up, sems
-):
+def repeat_kernel(w_ref, x_ref):
+    w = w_ref[...].astype(F32)
+    rows = [w[i : i + 1] for i in range(ROWS)]
+    pair = []
+    for j in range(PAIR):
+        part = rows[SPLIT * j : SPLIT * (j + 1)]
+        part = part + [jnp.zeros((1, COLS), F32)] * (SPLIT - len(part))
+        pair.append(jnp.concatenate(part, axis=1))
+    odd = (iota((TOKENS, W_LANES), 0) & 1) == 1
+    both = spread(jnp.where(odd, pair[1], pair[0]).astype(BF16))
+    for b in range(LINES):
+        x_ref[b * SOURCES : (b + 1) * SOURCES] = both
+
+
+def pack_kernel(core_ref, q_ref, k_ref, v_ref, u_ref, x_ref, feats, up, packed, sems):
     copies = []
+    for h in range(4):
+        part = pl.ds(h * (TOKENS // 4), TOKENS // 4)
+        copies.append(pltpu.make_async_copy(u_ref.at[part], up.at[part], sems.at[h]))
     for n, ref in enumerate((q_ref, k_ref, v_ref)):
         for h in range(2):
             part = pl.ds(h * (HD // 2), HD // 2)
             copies.append(
-                pltpu.make_async_copy(ref.at[part], feats.at[n, part], sems.at[2 * n + h])
+                pltpu.make_async_copy(ref.at[part], feats.at[n, part], sems.at[4 + 2 * n + h])
             )
-    for h in range(4):
-        part = pl.ds(h * (TOKENS // 4), TOKENS // 4)
-        copies.append(pltpu.make_async_copy(u_ref.at[part], up.at[part], sems.at[6 + h]))
     for copy in copies:
         copy.start()
-    for s, ref in enumerate((w0, w1, w2, w3)):
-        w = ref[...].astype(F32)
-        rows = [w[i : i + 1] for i in range(ROWS)]
-        for j in range(PAIR):
-            part = rows[SPLIT * j : SPLIT * (j + 1)]
-            pad = jnp.zeros((1, W_LANES - len(part) * COLS), F32)
-            lines[s, j : j + 1, :] = jnp.concatenate(part + [pad], axis=1)
-    count = TOKENS // LINES
-    odd = (iota((count, W_LANES), 0) & 1) == 1
-    line, parts = line_ref[0], []
-    for b in range(LINES):
-        pair = lines[lax.rem(line - b + LINES, LINES)]
-        parts.append(jnp.where(odd, pair[1:2], pair[0:1]))
-    x_ref[:, :, :W_LANES] = spread(jnp.concatenate(parts, axis=0).astype(BF16))
-
+
+    def out(n, at, lanes):
+        part = pl.ds(at, lanes)
+        return pltpu.make_async_copy(
+            packed.at[:, :, part], x_ref.at[:, :, part], sems.at[10 + n]
+        )
+
+    outs = [out(0, AT_U, D), out(1, AT_Q, 2 * HD), out(2, AT_V, HD)]
     order = order_matrix()
-    for n, at in enumerate((AT_Q, AT_K, AT_V)):
-        copies[2 * n].wait()
-        copies[2 * n + 1].wait()
-        x_ref[:, :, at : at + HD] = spread(dot(feats[n], order, TN, BF16))
-    for copy in copies[6:]:
+    for copy in copies[:4]:
         copy.wait()
     first = core_ref[0] == 0
     mine, theirs = [], []
@@ -104,16 +107,22 @@
         b = up[:, (2 * line + 1) * COLS : (2 * line + 2) * COLS]
         mine.append(jnp.where(first, a, b))
         theirs.append(jnp.where(first, b, a))
-    x_ref[:, :, AT_U : AT_U + D] = spread(jnp.concatenate(mine + theirs, axis=1))
-
-
-def weight_kernel(x_ref, own_ref, r1_ref, r2_ref, r3_ref, w_ref, raw):
-    for s, ref in enumerate((own_ref, r1_ref, r2_ref, r3_ref)):
-        raw[s] = ref[...].reshape(TOKENS, W_LANES)
-    x = x_ref[0]
+    packed[:, :, AT_U : AT_U + D] = spread(jnp.concatenate(mine + theirs, axis=1))
+    outs[0].start()
+    for n, at in enumerate((AT_Q, AT_K, AT_V)):
+        copies[4 + 2 * n].wait()
+        copies[5 + 2 * n].wait()
+        packed[:, :, at : at + HD] = spread(dot(feats[n], order, TN, BF16))
+        if n > 0:
+            outs[n].start()
+    for copy in outs:
+        copy.wait()
+
+
+def weight_kernel(raw_ref, w_ref):
     pick = iota((SOURCES, TOKENS), 1) - PAIR * iota((SOURCES, TOKENS), 0)
     for b in range(LINES):
-        block = raw[lax.rem(x - b + LINES, LINES)]
+        block = raw_ref[b * SOURCES : (b + 1) * SOURCES].reshape(TOKENS, W_LANES)
         for j in range(PAIR):
             part = dot((pick == j).astype(BF16), block, NN, BF16)
             for i in range(SPLIT * j, min(SPLIT * (j + 1), ROWS)):
@@ -231,13 +240,13 @@
         wg_ref[i : i + 1, :] = sums[j : j + 1, lane : lane + COLS]
 
 
-def call(kernel, outs, args, scalars=0, far=0, scratch=(), flops=10**8, limit=24):
+def call(kernel, outs, args, scalars=0, far=0, far_out=False, scratch=(), flops=10**8, limit=24):
     smem = [pl.BlockSpec(memory_space=pltpu.SMEM)] * scalars
     vmem = [pl.BlockSpec(memory_space=pltpu.VMEM)] * (len(args) - scalars - far)
     hbm = [pl.BlockSpec(memory_space=pltpu.HBM)] * far
     moved = sum(int(np.prod(x.shape)) * x.dtype.itemsize for x in [*args, *outs])
     single = len(outs) == 1
-    out_spec = [pl.BlockSpec(memory_space=pltpu.VMEM)] * len(outs)
+    out_spec = [pl.BlockSpec(memory_space=pltpu.HBM if far_out else pltpu.VMEM)] * len(outs)
     return pl.pallas_call(
         kernel,
         out_shape=outs[0] if single else outs,
@@ -258,21 +267,15 @@
     return [np.concatenate([cols[:, c].ravel(), cols[:, 1 - c].ravel()]) for c in range(CORES)]
 
 
-def shards(dp_size, queries, keys, values, out_weight, upstream, timestep):
-    dp = lax.axis_index("dp")
-    line, core = (dp // CORES).astype(jnp.int32), (dp % CORES).astype(jnp.int32)
-    line_s, core_s = line.reshape(1), core.reshape(1)
-    x_s = (lax.axis_index("tm") // (SOURCES // LINES)).astype(jnp.int32).reshape(1)
+def shards(queries, keys, values, out_weight, upstream, timestep):
+    core = lax.axis_index("core").astype(jnp.int32)
+    core_s, line_s = core.reshape(1), lax.axis_index("line").astype(jnp.int32).reshape(1)
 
     def shift_line(x, s):
-        return lax.ppermute(x, "dp", [(d, (d + CORES * s) % dp_size) for d in range(dp_size)])
-
-    def shift_x(x, s):
-        step = SOURCES // LINES
-        return lax.ppermute(x, "tm", [(t, (t + step * s) % SOURCES) for t in range(SOURCES)])
+        return lax.ppermute(x, "line", [(d, (d + s) % LINES) for d in range(LINES)])
 
     def swap_core(x):
-        return lax.ppermute(x, "dp", [(d, d ^ 1) for d in range(dp_size)])
+        return lax.ppermute(x, "core", [(0, 1), (1, 0)])
 
     orders = [o.astype(np.float32) for o in column_order()]
     index = jnp.where(core == 0, orders[0], orders[1])
@@ -280,22 +283,25 @@
     gate = (1.5 + jnp.sin(timestep.astype(F32)[0] * freq)).reshape(1, D)
 
     flat = [x.reshape(TOKENS, HD).T for x in (queries, keys, values)]
-    weights = [out_weight] + [shift_line(out_weight, s) for s in range(1, LINES)]
     sent = call(
         pack_kernel,
         [shape(SOURCES, PAIR, IN_LANES)],
-        (core_s, line_s, *weights, *flat, upstream.reshape(TOKENS, D)),
-        scalars=2,
+        (core_s, *flat, upstream.reshape(TOKENS, D)),
+        scalars=1,
         far=4,
+        far_out=True,
         limit=60,
         scratch=[
-            pltpu.VMEM((LINES, 8, W_LANES), F32),
             pltpu.VMEM((3, HD, TOKENS), BF16),
             pltpu.VMEM((TOKENS, D), BF16),
-            pltpu.SemaphoreType.DMA((10,)),
+            pltpu.VMEM((SOURCES, PAIR, IN_LANES), BF16),
+            pltpu.SemaphoreType.DMA((13,)),
         ],
     )
-    slab = lax.all_to_all(sent, "tm", split_axis=0, concat_axis=0, tiled=True)
+    w_sent = call(repeat_kernel, [shape(W_PEERS, PAIR, W_LANES)], (out_weight,))
+    slab = lax.all_to_all(sent, OTHERS, split_axis=0, concat_axis=0, tiled=True)
+    w_sent, _ = lax.optimization_barrier((w_sent, slab))
+    w_raw = lax.all_to_all(w_sent, ("line", *OTHERS), split_axis=0, concat_axis=0, tiled=True)
 
     probs, swap, mine = call(
         forward_kernel,
@@ -303,8 +309,6 @@
         (gate, slab),
     )
     got = swap_core(swap)
-    own_raw, _ = lax.optimization_barrier((slab[:, :, :W_LANES], swap))
-    raws = [own_raw] + [shift_x(own_raw, s) for s in range(1, LINES)]
     pieces = call(
         share_kernel,
         [shape(SOURCES, ROWS * COLS)] * LINES,
@@ -313,21 +317,15 @@
         scratch=[pltpu.VMEM((LINES, SOURCES, ROWS * COLS), BF16)],
     )
     sums = [pieces[0]] + [shift_line(pieces[s], s) for s in range(1, LINES)]
-    x_late, _ = lax.optimization_barrier((x_s, pieces[0]))
-    w_mine = call(
-        weight_kernel,
-        [shape(HD, HALF)],
-        (x_late, *raws),
-        scalars=1,
-        scratch=[pltpu.VMEM((LINES, TOKENS, W_LANES), BF16)],
-    )
+    w_raw, _ = lax.optimization_barrier((w_raw, pieces[0]))
+    w_mine = call(weight_kernel, [shape(HD, HALF)], (w_raw,))
     w_theirs = swap_core(w_mine)
     grads = call(
         backward_kernel, [shape(TOKENS, HD)] * 3, (gate, slab, probs, w_mine, w_theirs), flops=10**9
     )
     total = call(sum_kernel, [shape(TOKENS, SPLIT * COLS)], sums, flops=10**10)
     back = call(back_kernel, [shape(SOURCES, PAIR, OUT_LANES)], (swap, *grads, total))
-    frame = lax.all_to_all(back, "tm", split_axis=0, concat_axis=0, tiled=True)
+    frame = lax.all_to_all(back, OTHERS, split_axis=0, concat_axis=0, tiled=True)
     output, dq, dk, dv, weight_grad = call(
         final_kernel,
         [shape(TOKENS, D)] + [shape(HD, TOKENS)] * 3 + [shape(ROWS, COLS, kind=F32)],
@@ -339,11 +337,13 @@
 
 
 def solution(mesh):
-    act = P("dp", "tm", None, None)
+    cut = jax.sharding.Mesh(mesh.devices.reshape(tuple(AXES.values())), tuple(AXES))
+    dp, tm = ("line", "core"), OTHERS
+    act = P(dp, tm, None, None)
     return jax.shard_map(
-        functools.partial(shards, mesh.shape["dp"]),
-        mesh=mesh,
-        in_specs=(act, act, act, P("tm", "dp"), act, P("dp")),
-        out_specs=(act, act, act, act, P("tm", "dp")),
+        shards,
+        mesh=cut,
+        in_specs=(act, act, act, P(tm, dp), act, P(dp)),
+        out_specs=(act, act, act, act, P(tm, dp)),
         check_vma=False,
     )

time: 142 us -> 139 us (0.979)
  the two profiles are of different devices: /device:TPU:1 before, /device:TPU:8 now
where the time goes in v3:
time: 139 us
  starting transfers between devices  41.6 us (30%)
  blocking collectives  41.3 us (30%)
  waiting for transfers between devices  41.1 us (30%)
  Pallas kernels  13.1 us (9%)
  between operations  1.46 us (1%)
    all_to_all x1, blocking collectives, shards(): lax.all_to_all(back, OTHERS, split_axis=0, concat_axis=0, tiled=True)  41.3 us
    all_to_all x1, waiting for transfers between devices, shards(): slab = lax.all_to_all(sent, OTHERS, split_axis=0, concat_axis=0, tiled=True)  27.1 us
    all_to_all x1, starting transfers between devices, shards(): slab = lax.all_to_all(sent, OTHERS, split_axis=0, concat_axis=0, tiled=True)  18.1 us
    pallas_call x9, Pallas kernels, call(): pl.pallas_call(kernel, out_shape=outs[0] if single else outs, in_specs=sm...  13.1 us
    ppermute x3, starting transfers between devices, shift_line(): return lax.ppermute(x, 'line', [(d, (d + s) % LINES) for d in range(LINES)])  11 us
    all_to_all x1, waiting for transfers between devices, shards(): lax.all_to_all(w_sent, ('line', *OTHERS), split_axis=0, concat_axis=0, ti...  8.94 us
    all_to_all x1, starting transfers between devices, shards(): lax.all_to_all(w_sent, ('line', *OTHERS), split_axis=0, concat_axis=0, ti...  8.42 us
    ppermute x2, starting transfers between devices, swap_core(): return lax.ppermute(x, 'core', [(0, 1), (1, 0)])  4.02 us
  transfers between devices with their start and end apart: 7, of which 5 were waited for; matrix products, arithmetic and copies ran while one was open for 0% of the time, Pallas kernels for 4%

profile of v3, /device:TPU:8, one launch (start us, length us, event | category | flops | bytes accessed | tf_op | source)
XLA Modules:
  0.0 138.6 jit_solution(13064548395679946418)
XLA Ops:
  0.6 3.3 %shard_map.119 = bf16[64,2,2880]{2,1,0:T(2,128)(2,1)} custom-call(s32[1]{0:T(128)} %bitcast.core_ref, bf16[576,128]{1,0:T(8,128)(2,1)} %bitcast.24, bf16[576,128]{1,0:T(8,128)(2,1)} %bitcast.25, bf16[576,128]{1,0:T(8,128)(2,1)} %bitcast.26, bf16[128,1152]{1,0:T(8,128)(2,1)} %bitcast.23), custom_call_target="tpu_custom_call" | custom-call | flops 100000000 | bytes 1474564 | tf_op jit(solution)/shard_map/pallas_call | solution.py:250
  4.0 0.0 copy-start
  4.0 18.1 %all-to-all-start = ((bf16[64,2,2880]{2,1,0:T(2,128)(2,1)}), bf16[64,2,2880]{2,1,0:T(2,128)(2,1)S(1)}, u32[]{:S(2)}, u32[]{:S(2)}) async-start(bf16[64,2,2880]{2,1,0:T(2,128)(2,1)} %shard_map.119), calls=%async_computation | async-start | bytes 1507328 | tf_op jit(solution)/shard_map/all_to_all | solution.py:302
  22.2 0.0 copy-done
  22.2 1.1 shard_map.121
  23.3 27.1 %all-to-all-done.x_ref = bf16[64,2,2880]{2,1,0:T(2,128)(2,1)S(1)} async-done(((bf16[64,2,2880]{2,1,0:T(2,128)(2,1)}), bf16[64,2,2880]{2,1,0:T(2,128)(2,1)S(1)}, u32[]{:S(2)}, u32[]{:S(2)}) %all-to-all-start) | async-done | bytes 737312 | tf_op jit(solution)/shard_map/all_to_all | solution.py:302
  50.4 0.0 copy-start.1
  50.4 0.0 copy-start.2
  50.4 8.4 %all-to-all-start.1 = ((bf16[256,2,720]{2,1,0:T(2,128)(2,1)}), bf16[256,2,720]{2,1,0:T(2,128)(2,1)S(1)}, u32[]{:S(2)}, u32[]{:S(2)}) async-start(bf16[256,2,720]{2,1,0:T(2,128)(2,1)} %shard_map.121), calls=%async_computation.1 | async-start | bytes 1572864 | tf_op jit(solution)/shard_map/all_to_all | solution.py:304
  59.5 0.0 copy-done.1
  59.5 0.0 copy-done.2
  59.5 0.1 sine_add_fusion
  59.6 1.3 shard_map.120
  60.9 1.9 %collective-permute-start = (bf16[128,1152]{1,0:T(8,128)(2,1)S(1)}, bf16[128,1152]{1,0:T(8,128)(2,1)S(1)}, u32[]{:S(2)}, u32[]{:S(2)}) collective-permute-start(bf16[128,1152]{1,0:T(8,128)(2,1)S(1)} %get-tuple-element.22.swap_ref), channel_id=1, source_target_pairs={{0,64},{64,0},{1,65},{65,1},{2,66},{66,2},{3,67},{67,3},{4,68},{68... | collective-permute-start | bytes 884744 | tf_op jit(solution)/shard_map/ppermute | solution.py:278
  62.8 1.5 %collective-permute-done.got_ref = bf16[128,1152]{1,0:T(8,128)(2,1)S(1)} collective-permute-done((bf16[128,1152]{1,0:T(8,128)(2,1)S(1)}, bf16[128,1152]{1,0:T(8,128)(2,1)S(1)}, u32[]{:S(2)}, u32[]{:S(2)}) %collective-permute-start) | collective-permute-done | bytes 294944 | tf_op jit(solution)/shard_map/ppermute | solution.py:278
  64.4 0.9 shard_map.122
  65.3 3.8 %collective-permute-start.2 = (bf16[64,1296]{1,0:T(8,128)(2,1)S(1)}, bf16[64,1296]{1,0:T(8,128)(2,1)S(1)}, u32[]{:S(2)}, u32[]{:S(2)}) collective-permute-start(bf16[64,1296]{1,0:T(8,128)(2,1)S(1)} %get-tuple-element.31), channel_id=1, source_target_pairs={{0,128},{128,256},{256,384},{384,0},{1,129},{129,257},{257,385},{3... | collective-permute-start | bytes 497672 | tf_op jit(solution)/shard_map/ppermute | solution.py:275
  69.1 3.8 %collective-permute-start.3 = (bf16[64,1296]{1,0:T(8,128)(2,1)S(1)}, bf16[64,1296]{1,0:T(8,128)(2,1)S(1)}, u32[]{:S(2)}, u32[]{:S(2)}) collective-permute-start(bf16[64,1296]{1,0:T(8,128)(2,1)S(1)} %get-tuple-element.32), channel_id=1, source_target_pairs={{0,256},{128,384},{256,0},{384,128},{1,257},{129,385},{257,1},{385... | collective-permute-start | bytes 497672 | tf_op jit(solution)/shard_map/ppermute | solution.py:275
  72.9 3.4 %collective-permute-start.4 = (bf16[64,1296]{1,0:T(8,128)(2,1)S(1)}, bf16[64,1296]{1,0:T(8,128)(2,1)}, u32[]{:S(2)}, u32[]{:S(2)}) collective-permute-start(bf16[64,1296]{1,0:T(8,128)(2,1)S(1)} %get-tuple-element.33), channel_id=1, source_target_pairs={{0,384},{128,0},{256,128},{384,256},{1,385},{129,1},{257,129},{385... | collective-permute-start | bytes 497672 | tf_op jit(solution)/shard_map/ppermute | solution.py:275
  76.3 8.9 %all-to-all-done.1.raw_ref = bf16[256,2,720]{2,1,0:T(2,128)(2,1)S(1)} async-done(((bf16[256,2,720]{2,1,0:T(2,128)(2,1)}), bf16[256,2,720]{2,1,0:T(2,128)(2,1)S(1)}, u32[]{:S(2)}, u32[]{:S(2)}) %all-to-all-start.1) | async-done | bytes 737312 | tf_op jit(solution)/shard_map/all_to_all | solution.py:304
  85.2 0.5 shard_map.123.wm_ref
  85.7 2.1 %collective-permute-start.1 = (bf16[576,576]{1,0:T(8,128)(2,1)S(1)}, bf16[576,576]{1,0:T(8,128)(2,1)S(1)}, u32[]{:S(2)}, u32[]{:S(2)}) collective-permute-start(bf16[576,576]{1,0:T(8,128)(2,1)S(1)} %shard_map.123.wm_ref), channel_id=1, source_target_pairs={{0,64},{64,0},{1,65},{65,1},{2,66},{66,2},{3,67},{67,3},{4,68},{68... | collective-permute-start | bytes 1990664 | tf_op jit(solution)/shard_map/ppermute | solution.py:278
  87.8 0.0 collective-permute-done.2.p1_ref
  87.8 1.0 collective-permute-done.3.p2_ref
  88.8 2.5 %collective-permute-done.4.p3_ref = bf16[64,1296]{1,0:T(8,128)(2,1)} collective-permute-done((bf16[64,1296]{1,0:T(8,128)(2,1)S(1)}, bf16[64,1296]{1,0:T(8,128)(2,1)}, u32[]{:S(2)}, u32[]{:S(2)}) %collective-permute-start.4) | collective-permute-done | bytes 165920 | tf_op jit(solution)/shard_map/ppermute | solution.py:275
  91.3 1.3 shard_map.125.sum_ref
  92.6 0.0 collective-permute-done.1.wt_ref
  92.6 2.5 %shard_map.124 = (bf16[128,576]{1,0:T(8,128)(2,1)S(1)}, bf16[128,576]{1,0:T(8,128)(2,1)S(1)}, bf16[128,576]{1,0:T(8,128)(2,1)S(1)}) custom-call(f32[1,1152]{1,0:T(1,128)S(1)} %reshape.44.gate_ref, bf16[64,2,2880]{2,1,0:T(2,128)(2,1)S(1)} %all-to-all-done.x_ref, f32[8,128,128]{2,1,0:T(8,128)S(1)} %get-tuple-element.23.probs_ref, ...), custom_call_target="tpu_custom_call" | custom-call | flops 1000000000 | bytes 3035648 | tf_op jit(solution)/shard_map/pallas_call | solution.py:250
  95.0 0.2 shard_map.126
  95.3 41.3 %all_to_all.15.z_ref = bf16[64,2,3024]{2,1,0:T(2,128)(2,1)S(1)} all-to-all(bf16[64,2,3024]{2,1,0:T(2,128)(2,1)S(1)} %shard_map.126), channel_id=1, replica_groups=mesh['line'=4,'core'=2,'x'=4,'y'=2,'z'=8] {'x','y','z'}, dimensions={0} | all-to-all | bytes 1548288 | tf_op jit(solution)/shard_map/all_to_all | solution.py:328
  136.6 2.0 %shard_map.127 = (bf16[128,1152]{1,0:T(8,128)(2,1)}, bf16[576,128]{1,0:T(8,128)(2,1)}, bf16[576,128]{1,0:T(8,128)(2,1)}, bf16[576,128]{1,0:T(8,128)(2,1)}, f32[9,144]{1,0:T(8,128)}) custom-call(s32[1]{0:T(128)} %bitcast.core_ref, f32[1,1152]{1,0:T(1,128)S(1)} %reshape.44.gate_ref, bf16[64,2,3024]{2,1,0:T(2,128)(2,1)S(1)} %all_to_all.15.z_ref, ...), custom_call_target="tpu_custom_call" | custom-call | flops 100000000 | bytes 2848324 | tf_op jit(solution)/shard_map/pallas_call | solution.py:250
  (1 shorter events, 0.0 us)
Async XLA Ops:
  4.0 18.2 %copy-start = (bf16[9,144]{1,0:T(8,128)(2,1)S(1)}, bf16[9,144]{1,0:T(8,128)(2,1)}, u32[]{:S(2)}) copy-start(bf16[9,144]{1,0:T(8,128)(2,1)} %w_ref.1) | copy-start | bytes 7780
  4.0 46.4 %all-to-all-start = ((bf16[64,2,2880]{2,1,0:T(2,128)(2,1)}), bf16[64,2,2880]{2,1,0:T(2,128)(2,1)S(1)}, u32[]{:S(2)}, u32[]{:S(2)}) async-start(bf16[64,2,2880]{2,1,0:T(2,128)(2,1)} %shard_map.119), calls=%async_computation | async-start | bytes 1507328 | tf_op jit(solution)/shard_map/all_to_all | solution.py:302
  50.4 9.1 %copy-start.1 = (f32[1152]{0:T(1024)S(1)}, f32[1152]{0:T(1024)}, u32[]{:S(2)}) copy-start(f32[1152]{0:T(1024)} %constant.25.clone) | copy-start | bytes 13828
  50.4 9.1 %copy-start.2 = (f32[1152]{0:T(1024)S(1)}, f32[1152]{0:T(1024)}, u32[]{:S(2)}) copy-start(f32[1152]{0:T(1024)} %constant.26.clone) | copy-start | bytes 13828
  50.4 34.8 %all-to-all-start.1 = ((bf16[256,2,720]{2,1,0:T(2,128)(2,1)}), bf16[256,2,720]{2,1,0:T(2,128)(2,1)S(1)}, u32[]{:S(2)}, u32[]{:S(2)}) async-start(bf16[256,2,720]{2,1,0:T(2,128)(2,1)} %shard_map.121), calls=%async_computation.1 | async-start | bytes 1572864 | tf_op jit(solution)/shard_map/all_to_all | solution.py:304
  60.9 3.5 %collective-permute-start = (bf16[128,1152]{1,0:T(8,128)(2,1)S(1)}, bf16[128,1152]{1,0:T(8,128)(2,1)S(1)}, u32[]{:S(2)}, u32[]{:S(2)}) collective-permute-start(bf16[128,1152]{1,0:T(8,128)(2,1)S(1)} %get-tuple-element.22.swap_ref), channel_id=1, source_target_pairs={{0,64},{64,0},{1,65},{65,1},{2,66},{66,2},{3,67},{67,3},{4,68},{68... | collective-permute-start | bytes 884744 | tf_op jit(solution)/shard_map/ppermute | solution.py:278
  65.3 22.5 %collective-permute-start.2 = (bf16[64,1296]{1,0:T(8,128)(2,1)S(1)}, bf16[64,1296]{1,0:T(8,128)(2,1)S(1)}, u32[]{:S(2)}, u32[]{:S(2)}) collective-permute-start(bf16[64,1296]{1,0:T(8,128)(2,1)S(1)} %get-tuple-element.31), channel_id=1, source_target_pairs={{0,128},{128,256},{256,384},{384,0},{1,129},{129,257},{257,385},{3... | collective-permute-start | bytes 497672 | tf_op jit(solution)/shard_map/ppermute | solution.py:275
  69.1 19.8 %collective-permute-start.3 = (bf16[64,1296]{1,0:T(8,128)(2,1)S(1)}, bf16[64,1296]{1,0:T(8,128)(2,1)S(1)}, u32[]{:S(2)}, u32[]{:S(2)}) collective-permute-start(bf16[64,1296]{1,0:T(8,128)(2,1)S(1)} %get-tuple-element.32), channel_id=1, source_target_pairs={{0,256},{128,384},{256,0},{384,128},{1,257},{129,385},{257,1},{385... | collective-permute-start | bytes 497672 | tf_op jit(solution)/shard_map/ppermute | solution.py:275
  72.9 18.4 %collective-permute-start.4 = (bf16[64,1296]{1,0:T(8,128)(2,1)S(1)}, bf16[64,1296]{1,0:T(8,128)(2,1)}, u32[]{:S(2)}, u32[]{:S(2)}) collective-permute-start(bf16[64,1296]{1,0:T(8,128)(2,1)S(1)} %get-tuple-element.33), channel_id=1, source_target_pairs={{0,384},{128,0},{256,128},{384,256},{1,385},{129,1},{257,129},{385... | collective-permute-start | bytes 497672 | tf_op jit(solution)/shard_map/ppermute | solution.py:275
  85.7 6.9 %collective-permute-start.1 = (bf16[576,576]{1,0:T(8,128)(2,1)S(1)}, bf16[576,576]{1,0:T(8,128)(2,1)S(1)}, u32[]{:S(2)}, u32[]{:S(2)}) collective-permute-start(bf16[576,576]{1,0:T(8,128)(2,1)S(1)} %shard_map.123.wm_ref), channel_id=1, source_target_pairs={{0,64},{64,0},{1,65},{65,1},{2,66},{66,2},{3,67},{67,3},{4,68},{68... | collective-permute-start | bytes 1990664 | tf_op jit(solution)/shard_map/ppermute | solution.py:278

commit v4 on v3

--- a/solution.py
+++ b/solution.py
@@ -24,8 +24,7 @@
 
 AXES = {"line": LINES, "core": CORES, "x": 4, "y": 2, "z": 8}
 OTHERS = ("x", "y", "z")
-W_PEERS = LINES * SOURCES
-W_LANES = (ROWS + 1) // 2 * COLS
+W_LANES = ROWS * HALF // PAIR
 
 AT_U = 0
 AT_Q = AT_U + D
@@ -62,18 +61,18 @@
     return x.reshape(SOURCES, PAIR, x.shape[-1])
 
 
-def repeat_kernel(w_ref, x_ref):
-    w = w_ref[...].astype(F32)
-    rows = [w[i : i + 1] for i in range(ROWS)]
-    pair = []
-    for j in range(PAIR):
-        part = rows[SPLIT * j : SPLIT * (j + 1)]
-        part = part + [jnp.zeros((1, COLS), F32)] * (SPLIT - len(part))
-        pair.append(jnp.concatenate(part, axis=1))
+def repeat_kernel(line_ref, w0, w1, w2, w3, x_ref, slots):
+    for s, ref in enumerate((w0, w1, w2, w3)):
+        slots[s, :ROWS, :] = ref[...].astype(F32)
+    line = line_ref[0]
+    blocks = [slots[lax.rem(line - b + LINES, LINES)] for b in range(LINES)]
+    full = jnp.concatenate(blocks, axis=1)
+    rows = [full[i : i + 1] for i in range(ROWS)]
+    mid = ROWS // 2
+    top = jnp.concatenate(rows[:mid] + [rows[mid][:, : HALF // 2]], axis=1)
+    low = jnp.concatenate([rows[mid][:, HALF // 2 :]] + rows[mid + 1 :], axis=1)
     odd = (iota((TOKENS, W_LANES), 0) & 1) == 1
-    both = spread(jnp.where(odd, pair[1], pair[0]).astype(BF16))
-    for b in range(LINES):
-        x_ref[b * SOURCES : (b + 1) * SOURCES] = both
+    x_ref[...] = spread(jnp.where(odd, low, top).astype(BF16))
 
 
 def pack_kernel(core_ref, q_ref, k_ref, v_ref, u_ref, x_ref, feats, up, packed, sems):
@@ -121,15 +120,19 @@
 
 def weight_kernel(raw_ref, w_ref):
     pick = iota((SOURCES, TOKENS), 1) - PAIR * iota((SOURCES, TOKENS), 0)
-    for b in range(LINES):
-        block = raw_ref[b * SOURCES : (b + 1) * SOURCES].reshape(TOKENS, W_LANES)
-        for j in range(PAIR):
-            part = dot((pick == j).astype(BF16), block, NN, BF16)
-            for i in range(SPLIT * j, min(SPLIT * (j + 1), ROWS)):
-                lane = (i - SPLIT * j) * COLS
-                w_ref[i * SOURCES : (i + 1) * SOURCES, b * COLS : (b + 1) * COLS] = part[
-                    :, lane : lane + COLS
-                ]
+    raw = raw_ref[...].reshape(TOKENS, W_LANES)
+    top = dot((pick == 0).astype(BF16), raw, NN, BF16)
+    low = dot((pick == 1).astype(BF16), raw, NN, BF16)
+    mid, part = ROWS // 2, HALF // 2
+    for i in range(ROWS):
+        at = slice(i * SOURCES, (i + 1) * SOURCES)
+        if i < mid:
+            w_ref[at, :] = top[:, i * HALF : (i + 1) * HALF]
+        elif i == mid:
+            w_ref[at, :part] = top[:, i * HALF :]
+            w_ref[at, part:] = low[:, :part]
+        else:
+            w_ref[at, :] = low[:, part + (i - mid - 1) * HALF : part + (i - mid) * HALF]
 
 
 def rows_of(x_ref, at, lanes):
@@ -298,10 +301,18 @@
             pltpu.SemaphoreType.DMA((13,)),
         ],
     )
-    w_sent = call(repeat_kernel, [shape(W_PEERS, PAIR, W_LANES)], (out_weight,))
+    own_w, _ = lax.optimization_barrier((out_weight, sent))
+    weights = [own_w] + [shift_line(own_w, s) for s in range(1, LINES)]
     slab = lax.all_to_all(sent, OTHERS, split_axis=0, concat_axis=0, tiled=True)
+    w_sent = call(
+        repeat_kernel,
+        [shape(SOURCES, PAIR, W_LANES)],
+        (line_s, *weights),
+        scalars=1,
+        scratch=[pltpu.VMEM((LINES, 16, COLS), F32)],
+    )
     w_sent, _ = lax.optimization_barrier((w_sent, slab))
-    w_raw = lax.all_to_all(w_sent, ("line", *OTHERS), split_axis=0, concat_axis=0, tiled=True)
+    w_raw = lax.all_to_all(w_sent, OTHERS, split_axis=0, concat_axis=0, tiled=True)
 
     probs, swap, mine = call(
         forward_kernel,

time: 139 us -> 135 us (0.971)
  waiting for transfers between devices: 41.1 us -> 34.9 us
  starting transfers between devices: 41.6 us -> 46.6 us
  blocking collectives: 41.3 us -> 39.3 us
    all_to_all x1, waiting for transfers between devices: 27.1 us -> 10.7 us  [shards(): slab = lax.all_to_all(sent, OTHERS, split_axis=0, concat_axis=0, tiled=True)]
    ppermute x3 -> x6, waiting for transfers between devices: 3.49 us -> 12.5 us  [shift_line(): return lax.ppermute(x, 'line', [(d, (d + s) % LINES) for d in range(LINES)])]
    ppermute x3 -> x6, starting transfers between devices: 11 us -> 19.1 us  [shift_line(): return lax.ppermute(x, 'line', [(d, (d + s) % LINES) for d in range(LINES)])]
    all_to_all x1, starting transfers between devices: 8.42 us -> 5.51 us  [shards(): lax.all_to_all(w_sent, OTHERS, split_axis=0, concat_axis=0, tiled=True)]
    all_to_all x1, blocking collectives: 41.3 us -> 39.3 us  [shards(): lax.all_to_all(back, OTHERS, split_axis=0, concat_axis=0, tiled=True)]
  transfers between devices with their start and end apart: 7 -> 10, of which waited for: 5 -> 6; matrix products, arithmetic and copies ran while one was open for 0% -> 0% of each run, Pallas kernels for 4% -> 3%
where the time goes in v4:
time: 135 us
  starting transfers between devices  46.6 us (35%)
  blocking collectives  39.3 us (29%)
  waiting for transfers between devices  34.9 us (26%)
  Pallas kernels  12.2 us (9%)
  between operations  1.49 us (1%)
    all_to_all x1, blocking collectives, shards(): lax.all_to_all(back, OTHERS, split_axis=0, concat_axis=0, tiled=True)  39.3 us
    ppermute x6, starting transfers between devices, shift_line(): return lax.ppermute(x, 'line', [(d, (d + s) % LINES) for d in range(LINES)])  19.1 us
    all_to_all x1, starting transfers between devices, shards(): slab = lax.all_to_all(sent, OTHERS, split_axis=0, concat_axis=0, tiled=True)  18.2 us
    ppermute x6, waiting for transfers between devices, shift_line(): return lax.ppermute(x, 'line', [(d, (d + s) % LINES) for d in range(LINES)])  12.5 us
    pallas_call x9, Pallas kernels, call(): pl.pallas_call(kernel, out_shape=outs[0] if single else outs, in_specs=sm...  12.2 us
    all_to_all x1, waiting for transfers between devices, shards(): slab = lax.all_to_all(sent, OTHERS, split_axis=0, concat_axis=0, tiled=True)  10.7 us
    all_to_all x1, waiting for transfers between devices, shards(): lax.all_to_all(w_sent, OTHERS, split_axis=0, concat_axis=0, tiled=True)  10.1 us
    all_to_all x1, starting transfers between devices, shards(): lax.all_to_all(w_sent, OTHERS, split_axis=0, concat_axis=0, tiled=True)  5.51 us
  transfers between devices with their start and end apart: 10, of which 6 were waited for; matrix products, arithmetic and copies ran while one was open for 0% of the time, Pallas kernels for 3%

profile of v4, /device:TPU:8, one launch (start us, length us, event | category | flops | bytes accessed | tf_op | source)
XLA Modules:
  0.0 134.5 jit_solution(6644354918404814955)
XLA Ops:
  0.6 3.4 %shard_map.119 = bf16[64,2,2880]{2,1,0:T(2,128)(2,1)} custom-call(s32[1]{0:T(128)} %bitcast.core_ref, bf16[576,128]{1,0:T(8,128)(2,1)} %bitcast.24, bf16[576,128]{1,0:T(8,128)(2,1)} %bitcast.25, bf16[576,128]{1,0:T(8,128)(2,1)} %bitcast.26, bf16[128,1152]{1,0:T(8,128)(2,1)} %bitcast.23), custom_call_target="tpu_custom_call" | custom-call | flops 100000000 | bytes 1474564 | tf_op jit(solution)/shard_map/pallas_call | solution.py:253
  4.0 0.0 copy-start
  4.0 18.2 %all-to-all-start = ((bf16[64,2,2880]{2,1,0:T(2,128)(2,1)}), bf16[64,2,2880]{2,1,0:T(2,128)(2,1)S(1)}, u32[]{:S(2)}, u32[]{:S(2)}) async-start(bf16[64,2,2880]{2,1,0:T(2,128)(2,1)} %shard_map.119), calls=%async_computation | async-start | bytes 1507328 | tf_op jit(solution)/shard_map/all_to_all | solution.py:306
  22.2 0.0 copy-done
  22.2 3.2 %collective-permute-start.2 = (bf16[9,144]{1,0:T(8,128)(2,1)S(1)}, bf16[9,144]{1,0:T(8,128)(2,1)S(1)}, u32[]{:S(2)}, u32[]{:S(2)}) collective-permute-start(bf16[9,144]{1,0:T(8,128)(2,1)S(1)} %copy-done), channel_id=1, source_target_pairs={{0,384},{128,0},{256,128},{384,256},{1,385},{129,1},{257,129},{385... | collective-permute-start | bytes 7784 | tf_op jit(solution)/shard_map/ppermute | solution.py:278
  25.4 2.7 %collective-permute-start.1 = (bf16[9,144]{1,0:T(8,128)(2,1)S(1)}, bf16[9,144]{1,0:T(8,128)(2,1)S(1)}, u32[]{:S(2)}, u32[]{:S(2)}) collective-permute-start(bf16[9,144]{1,0:T(8,128)(2,1)S(1)} %copy-done), channel_id=1, source_target_pairs={{0,256},{128,384},{256,0},{384,128},{1,257},{129,385},{257,1},{385... | collective-permute-start | bytes 7784 | tf_op jit(solution)/shard_map/ppermute | solution.py:278
  28.2 3.5 %collective-permute-start = (bf16[9,144]{1,0:T(8,128)(2,1)S(1)}, bf16[9,144]{1,0:T(8,128)(2,1)S(1)}, u32[]{:S(2)}, u32[]{:S(2)}) collective-permute-start(bf16[9,144]{1,0:T(8,128)(2,1)S(1)} %copy-done), channel_id=1, source_target_pairs={{0,128},{128,256},{256,384},{384,0},{1,129},{129,257},{257,385},{3... | collective-permute-start | bytes 7784 | tf_op jit(solution)/shard_map/ppermute | solution.py:278
  31.7 6.9 %collective-permute-done.2.w3 = bf16[9,144]{1,0:T(8,128)(2,1)S(1)} collective-permute-done((bf16[9,144]{1,0:T(8,128)(2,1)S(1)}, bf16[9,144]{1,0:T(8,128)(2,1)S(1)}, u32[]{:S(2)}, u32[]{:S(2)}) %collective-permute-start.2) | collective-permute-done | bytes 2624 | tf_op jit(solution)/shard_map/ppermute | solution.py:278
  38.5 0.0 collective-permute-done.1.w2
  38.5 0.0 collective-permute-done.w1
  38.5 1.2 shard_map.121
  39.8 10.7 %all-to-all-done.x_ref = bf16[64,2,2880]{2,1,0:T(2,128)(2,1)S(1)} async-done(((bf16[64,2,2880]{2,1,0:T(2,128)(2,1)}), bf16[64,2,2880]{2,1,0:T(2,128)(2,1)S(1)}, u32[]{:S(2)}, u32[]{:S(2)}) %all-to-all-start) | async-done | bytes 737312 | tf_op jit(solution)/shard_map/all_to_all | solution.py:306
  50.5 0.0 copy-start.1
  50.5 0.0 copy-start.2
  50.5 5.5 %all-to-all-start.1 = ((bf16[64,2,2592]{2,1,0:T(2,128)(2,1)}), bf16[64,2,2592]{2,1,0:T(2,128)(2,1)S(1)}, u32[]{:S(2)}, u32[]{:S(2)}) async-start(bf16[64,2,2592]{2,1,0:T(2,128)(2,1)} %shard_map.121), calls=%async_computation.1 | async-start | bytes 1376256 | tf_op jit(solution)/shard_map/all_to_all | solution.py:315
  56.7 0.0 copy-done.1
  56.7 0.0 copy-done.2
  56.7 0.1 sine_add_fusion
  56.8 1.3 shard_map.120
  58.1 1.9 %collective-permute-start.3 = (bf16[128,1152]{1,0:T(8,128)(2,1)S(1)}, bf16[128,1152]{1,0:T(8,128)(2,1)S(1)}, u32[]{:S(2)}, u32[]{:S(2)}) collective-permute-start(bf16[128,1152]{1,0:T(8,128)(2,1)S(1)} %get-tuple-element.23.swap_ref), channel_id=1, source_target_pairs={{0,64},{64,0},{1,65},{65,1},{2,66},{66,2},{3,67},{67,3},{4,68},{68... | collective-permute-start | bytes 884744 | tf_op jit(solution)/shard_map/ppermute | solution.py:281
  60.0 1.5 %collective-permute-done.3.got_ref = bf16[128,1152]{1,0:T(8,128)(2,1)S(1)} collective-permute-done((bf16[128,1152]{1,0:T(8,128)(2,1)S(1)}, bf16[128,1152]{1,0:T(8,128)(2,1)S(1)}, u32[]{:S(2)}, u32[]{:S(2)}) %collective-permute-start.3) | collective-permute-done | bytes 294944 | tf_op jit(solution)/shard_map/ppermute | solution.py:281
  61.6 0.9 shard_map.122
  62.5 2.7 %collective-permute-start.5 = (bf16[64,1296]{1,0:T(8,128)(2,1)S(1)}, bf16[64,1296]{1,0:T(8,128)(2,1)S(1)}, u32[]{:S(2)}, u32[]{:S(2)}) collective-permute-start(bf16[64,1296]{1,0:T(8,128)(2,1)S(1)} %get-tuple-element.33), channel_id=1, source_target_pairs={{0,128},{128,256},{256,384},{384,0},{1,129},{129,257},{257,385},{3... | collective-permute-start | bytes 497672 | tf_op jit(solution)/shard_map/ppermute | solution.py:278
  65.2 5.0 %collective-permute-start.6 = (bf16[64,1296]{1,0:T(8,128)(2,1)S(1)}, bf16[64,1296]{1,0:T(8,128)(2,1)S(1)}, u32[]{:S(2)}, u32[]{:S(2)}) collective-permute-start(bf16[64,1296]{1,0:T(8,128)(2,1)S(1)} %get-tuple-element.34), channel_id=1, source_target_pairs={{0,256},{128,384},{256,0},{384,128},{1,257},{129,385},{257,1},{385... | collective-permute-start | bytes 497672 | tf_op jit(solution)/shard_map/ppermute | solution.py:278
  70.2 1.9 %collective-permute-start.7 = (bf16[64,1296]{1,0:T(8,128)(2,1)S(1)}, bf16[64,1296]{1,0:T(8,128)(2,1)S(1)}, u32[]{:S(2)}, u32[]{:S(2)}) collective-permute-start(bf16[64,1296]{1,0:T(8,128)(2,1)S(1)} %get-tuple-element.35), channel_id=1, source_target_pairs={{0,384},{128,0},{256,128},{384,256},{1,385},{129,1},{257,129},{385... | collective-permute-start | bytes 497672 | tf_op jit(solution)/shard_map/ppermute | solution.py:278
  72.1 10.1 %all-to-all-done.1.raw_ref = bf16[64,2,2592]{2,1,0:T(2,128)(2,1)S(1)} async-done(((bf16[64,2,2592]{2,1,0:T(2,128)(2,1)}), bf16[64,2,2592]{2,1,0:T(2,128)(2,1)S(1)}, u32[]{:S(2)}, u32[]{:S(2)}) %all-to-all-start.1) | async-done | bytes 663584 | tf_op jit(solution)/shard_map/all_to_all | solution.py:315
  82.3 0.5 shard_map.123.wm_ref
  82.7 1.9 %collective-permute-start.4 = (bf16[576,576]{1,0:T(8,128)(2,1)S(1)}, bf16[576,576]{1,0:T(8,128)(2,1)S(1)}, u32[]{:S(2)}, u32[]{:S(2)}) collective-permute-start(bf16[576,576]{1,0:T(8,128)(2,1)S(1)} %shard_map.123.wm_ref), channel_id=1, source_target_pairs={{0,64},{64,0},{1,65},{65,1},{2,66},{66,2},{3,67},{67,3},{4,68},{68... | collective-permute-start | bytes 1990664 | tf_op jit(solution)/shard_map/ppermute | solution.py:281
  84.7 0.0 collective-permute-done.5.p1_ref
  84.7 2.5 %collective-permute-done.6.p2_ref = bf16[64,1296]{1,0:T(8,128)(2,1)S(1)} collective-permute-done((bf16[64,1296]{1,0:T(8,128)(2,1)S(1)}, bf16[64,1296]{1,0:T(8,128)(2,1)S(1)}, u32[]{:S(2)}, u32[]{:S(2)}) %collective-permute-start.6) | collective-permute-done | bytes 165920 | tf_op jit(solution)/shard_map/ppermute | solution.py:278
  87.2 3.1 %collective-permute-done.7.p3_ref = bf16[64,1296]{1,0:T(8,128)(2,1)S(1)} collective-permute-done((bf16[64,1296]{1,0:T(8,128)(2,1)S(1)}, bf16[64,1296]{1,0:T(8,128)(2,1)S(1)}, u32[]{:S(2)}, u32[]{:S(2)}) %collective-permute-start.7) | collective-permute-done | bytes 165920 | tf_op jit(solution)/shard_map/ppermute | solution.py:278
  90.3 0.3 shard_map.125.sum_ref
  90.6 0.0 collective-permute-done.4.wt_ref
  90.7 2.4 %shard_map.124 = (bf16[128,576]{1,0:T(8,128)(2,1)S(1)}, bf16[128,576]{1,0:T(8,128)(2,1)S(1)}, bf16[128,576]{1,0:T(8,128)(2,1)S(1)}) custom-call(f32[1,1152]{1,0:T(1,128)S(1)} %reshape.44.gate_ref, bf16[64,2,2880]{2,1,0:T(2,128)(2,1)S(1)} %all-to-all-done.x_ref, f32[8,128,128]{2,1,0:T(8,128)S(1)} %get-tuple-element.24.probs_ref, ...), custom_call_target="tpu_custom_call" | custom-call | flops 1000000000 | bytes 3035648 | tf_op jit(solution)/shard_map/pallas_call | solution.py:253
  93.1 0.2 shard_map.126
  93.3 39.3 %all_to_all.15.z_ref = bf16[64,2,3024]{2,1,0:T(2,128)(2,1)S(1)} all-to-all(bf16[64,2,3024]{2,1,0:T(2,128)(2,1)S(1)} %shard_map.126), channel_id=1, replica_groups=mesh['line'=4,'core'=2,'x'=4,'y'=2,'z'=8] {'x','y','z'}, dimensions={0} | all-to-all | bytes 1548288 | tf_op jit(solution)/shard_map/all_to_all | solution.py:339
  132.6 2.0 %shard_map.127 = (bf16[128,1152]{1,0:T(8,128)(2,1)}, bf16[576,128]{1,0:T(8,128)(2,1)}, bf16[576,128]{1,0:T(8,128)(2,1)}, bf16[576,128]{1,0:T(8,128)(2,1)}, f32[9,144]{1,0:T(8,128)}) custom-call(s32[1]{0:T(128)} %bitcast.core_ref, f32[1,1152]{1,0:T(1,128)S(1)} %reshape.44.gate_ref, bf16[64,2,3024]{2,1,0:T(2,128)(2,1)S(1)} %all_to_all.15.z_ref, ...), custom_call_target="tpu_custom_call" | custom-call | flops 100000000 | bytes 2848324 | tf_op jit(solution)/shard_map/pallas_call | solution.py:253
  (1 shorter events, 0.0 us)
Async XLA Ops:
  4.0 18.2 %copy-start = (bf16[9,144]{1,0:T(8,128)(2,1)S(1)}, bf16[9,144]{1,0:T(8,128)(2,1)}, u32[]{:S(2)}) copy-start(bf16[9,144]{1,0:T(8,128)(2,1)} %w0) | copy-start | bytes 7780
  4.0 46.5 %all-to-all-start = ((bf16[64,2,2880]{2,1,0:T(2,128)(2,1)}), bf16[64,2,2880]{2,1,0:T(2,128)(2,1)S(1)}, u32[]{:S(2)}, u32[]{:S(2)}) async-start(bf16[64,2,2880]{2,1,0:T(2,128)(2,1)} %shard_map.119), calls=%async_computation | async-start | bytes 1507328 | tf_op jit(solution)/shard_map/all_to_all | solution.py:306
  22.2 16.3 %collective-permute-start.2 = (bf16[9,144]{1,0:T(8,128)(2,1)S(1)}, bf16[9,144]{1,0:T(8,128)(2,1)S(1)}, u32[]{:S(2)}, u32[]{:S(2)}) collective-permute-start(bf16[9,144]{1,0:T(8,128)(2,1)S(1)} %copy-done), channel_id=1, source_target_pairs={{0,384},{128,0},{256,128},{384,256},{1,385},{129,1},{257,129},{385... | collective-permute-start | bytes 7784 | tf_op jit(solution)/shard_map/ppermute | solution.py:278
  25.4 13.1 %collective-permute-start.1 = (bf16[9,144]{1,0:T(8,128)(2,1)S(1)}, bf16[9,144]{1,0:T(8,128)(2,1)S(1)}, u32[]{:S(2)}, u32[]{:S(2)}) collective-permute-start(bf16[9,144]{1,0:T(8,128)(2,1)S(1)} %copy-done), channel_id=1, source_target_pairs={{0,256},{128,384},{256,0},{384,128},{1,257},{129,385},{257,1},{385... | collective-permute-start | bytes 7784 | tf_op jit(solution)/shard_map/ppermute | solution.py:278
  28.2 10.4 %collective-permute-start = (bf16[9,144]{1,0:T(8,128)(2,1)S(1)}, bf16[9,144]{1,0:T(8,128)(2,1)S(1)}, u32[]{:S(2)}, u32[]{:S(2)}) collective-permute-start(bf16[9,144]{1,0:T(8,128)(2,1)S(1)} %copy-done), channel_id=1, source_target_pairs={{0,128},{128,256},{256,384},{384,0},{1,129},{129,257},{257,385},{3... | collective-permute-start | bytes 7784 | tf_op jit(solution)/shard_map/ppermute | solution.py:278
  50.5 6.2 %copy-start.1 = (f32[1152]{0:T(1024)S(1)}, f32[1152]{0:T(1024)}, u32[]{:S(2)}) copy-start(f32[1152]{0:T(1024)} %constant.26.clone) | copy-start | bytes 13828
  50.5 6.2 %copy-start.2 = (f32[1152]{0:T(1024)S(1)}, f32[1152]{0:T(1024)}, u32[]{:S(2)}) copy-start(f32[1152]{0:T(1024)} %constant.25.clone) | copy-start | bytes 13828
  50.5 31.8 %all-to-all-start.1 = ((bf16[64,2,2592]{2,1,0:T(2,128)(2,1)}), bf16[64,2,2592]{2,1,0:T(2,128)(2,1)S(1)}, u32[]{:S(2)}, u32[]{:S(2)}) async-start(bf16[64,2,2592]{2,1,0:T(2,128)(2,1)} %shard_map.121), calls=%async_computation.1 | async-start | bytes 1376256 | tf_op jit(solution)/shard_map/all_to_all | solution.py:315
  58.1 3.5 %collective-permute-start.3 = (bf16[128,1152]{1,0:T(8,128)(2,1)S(1)}, bf16[128,1152]{1,0:T(8,128)(2,1)S(1)}, u32[]{:S(2)}, u32[]{:S(2)}) collective-permute-start(bf16[128,1152]{1,0:T(8,128)(2,1)S(1)} %get-tuple-element.23.swap_ref), channel_id=1, source_target_pairs={{0,64},{64,0},{1,65},{65,1},{2,66},{66,2},{3,67},{67,3},{4,68},{68... | collective-permute-start | bytes 884744 | tf_op jit(solution)/shard_map/ppermute | solution.py:281
  62.5 22.2 %collective-permute-start.5 = (bf16[64,1296]{1,0:T(8,128)(2,1)S(1)}, bf16[64,1296]{1,0:T(8,128)(2,1)S(1)}, u32[]{:S(2)}, u32[]{:S(2)}) collective-permute-start(bf16[64,1296]{1,0:T(8,128)(2,1)S(1)} %get-tuple-element.33), channel_id=1, source_target_pairs={{0,128},{128,256},{256,384},{384,0},{1,129},{129,257},{257,385},{3... | collective-permute-start | bytes 497672 | tf_op jit(solution)/shard_map/ppermute | solution.py:278
  65.2 21.9 %collective-permute-start.6 = (bf16[64,1296]{1,0:T(8,128)(2,1)S(1)}, bf16[64,1296]{1,0:T(8,128)(2,1)S(1)}, u32[]{:S(2)}, u32[]{:S(2)}) collective-permute-start(bf16[64,1296]{1,0:T(8,128)(2,1)S(1)} %get-tuple-element.34), channel_id=1, source_target_pairs={{0,256},{128,384},{256,0},{384,128},{1,257},{129,385},{257,1},{385... | collective-permute-start | bytes 497672 | tf_op jit(solution)/shard_map/ppermute | solution.py:278
  70.2 20.1 %collective-permute-start.7 = (bf16[64,1296]{1,0:T(8,128)(2,1)S(1)}, bf16[64,1296]{1,0:T(8,128)(2,1)S(1)}, u32[]{:S(2)}, u32[]{:S(2)}) collective-permute-start(bf16[64,1296]{1,0:T(8,128)(2,1)S(1)} %get-tuple-element.35), channel_id=1, source_target_pairs={{0,384},{128,0},{256,128},{384,256},{1,385},{129,1},{257,129},{385... | collective-permute-start | bytes 497672 | tf_op jit(solution)/shard_map/ppermute | solution.py:278
  82.7 7.9 %collective-permute-start.4 = (bf16[576,576]{1,0:T(8,128)(2,1)S(1)}, bf16[576,576]{1,0:T(8,128)(2,1)S(1)}, u32[]{:S(2)}, u32[]{:S(2)}) collective-permute-start(bf16[576,576]{1,0:T(8,128)(2,1)S(1)} %shard_map.123.wm_ref), channel_id=1, source_target_pairs={{0,64},{64,0},{1,65},{65,1},{2,66},{66,2},{3,67},{67,3},{4,68},{68... | collective-permute-start | bytes 1990664 | tf_op jit(solution)/shard_map/ppermute | solution.py:281

commit v5 on v4

--- a/solution.py
+++ b/solution.py
@@ -30,7 +30,8 @@
 AT_Q = AT_U + D
 AT_K = AT_Q + HD
 AT_V = AT_K + HD
-IN_LANES = AT_V + HD
+AT_W = AT_V + HD
+IN_LANES = AT_W + W_LANES
 AT_G = 4 * HD
 OUT_LANES = AT_G + SPLIT * COLS
 
@@ -61,21 +62,24 @@
     return x.reshape(SOURCES, PAIR, x.shape[-1])
 
 
-def repeat_kernel(line_ref, w0, w1, w2, w3, x_ref, slots):
-    for s, ref in enumerate((w0, w1, w2, w3)):
-        slots[s, :ROWS, :] = ref[...].astype(F32)
-    line = line_ref[0]
-    blocks = [slots[lax.rem(line - b + LINES, LINES)] for b in range(LINES)]
-    full = jnp.concatenate(blocks, axis=1)
-    rows = [full[i : i + 1] for i in range(ROWS)]
-    mid = ROWS // 2
-    top = jnp.concatenate(rows[:mid] + [rows[mid][:, : HALF // 2]], axis=1)
-    low = jnp.concatenate([rows[mid][:, HALF // 2 :]] + rows[mid + 1 :], axis=1)
-    odd = (iota((TOKENS, W_LANES), 0) & 1) == 1
-    x_ref[...] = spread(jnp.where(odd, low, top).astype(BF16))
-
-
-def pack_kernel(core_ref, q_ref, k_ref, v_ref, u_ref, x_ref, feats, up, packed, sems):
+def pack_kernel(
+    core_ref,
+    line_ref,
+    w0,
+    w1,
+    w2,
+    w3,
+    q_ref,
+    k_ref,
+    v_ref,
+    u_ref,
+    x_ref,
+    feats,
+    up,
+    packed,
+    slots,
+    sems,
+):
     copies = []
     for h in range(4):
         part = pl.ds(h * (TOKENS // 4), TOKENS // 4)
@@ -95,7 +99,18 @@
             packed.at[:, :, part], x_ref.at[:, :, part], sems.at[10 + n]
         )
 
-    outs = [out(0, AT_U, D), out(1, AT_Q, 2 * HD), out(2, AT_V, HD)]
+    outs = [out(0, AT_U, D), out(1, AT_Q, 2 * HD), out(2, AT_V, HD + W_LANES)]
+    for s, ref in enumerate((w0, w1, w2, w3)):
+        slots[s, :ROWS, :] = ref[...].astype(F32)
+    line = line_ref[0]
+    blocks = [slots[lax.rem(line - b + LINES, LINES)] for b in range(LINES)]
+    full = jnp.concatenate(blocks, axis=1)
+    rows = [full[i : i + 1] for i in range(ROWS)]
+    mid = ROWS // 2
+    top = jnp.concatenate(rows[:mid] + [rows[mid][:, : HALF // 2]], axis=1)
+    low = jnp.concatenate([rows[mid][:, HALF // 2 :]] + rows[mid + 1 :], axis=1)
+    odd = (iota((TOKENS, W_LANES), 0) & 1) == 1
+    packed[:, :, AT_W:IN_LANES] = spread(jnp.where(odd, low, top).astype(BF16))
     order = order_matrix()
     for copy in copies[:4]:
         copy.wait()
@@ -120,7 +135,7 @@
 
 def weight_kernel(raw_ref, w_ref):
     pick = iota((SOURCES, TOKENS), 1) - PAIR * iota((SOURCES, TOKENS), 0)
-    raw = raw_ref[...].reshape(TOKENS, W_LANES)
+    raw = rows_of(raw_ref, AT_W, W_LANES)
     top = dot((pick == 0).astype(BF16), raw, NN, BF16)
     low = dot((pick == 1).astype(BF16), raw, NN, BF16)
     mid, part = ROWS // 2, HALF // 2
@@ -286,11 +301,12 @@
     gate = (1.5 + jnp.sin(timestep.astype(F32)[0] * freq)).reshape(1, D)
 
     flat = [x.reshape(TOKENS, HD).T for x in (queries, keys, values)]
+    weights = [out_weight] + [shift_line(out_weight, s) for s in range(1, LINES)]
     sent = call(
         pack_kernel,
         [shape(SOURCES, PAIR, IN_LANES)],
-        (core_s, *flat, upstream.reshape(TOKENS, D)),
-        scalars=1,
+        (core_s, line_s, *weights, *flat, upstream.reshape(TOKENS, D)),
+        scalars=2,
         far=4,
         far_out=True,
         limit=60,
@@ -298,21 +314,11 @@
             pltpu.VMEM((3, HD, TOKENS), BF16),
             pltpu.VMEM((TOKENS, D), BF16),
             pltpu.VMEM((SOURCES, PAIR, IN_LANES), BF16),
+            pltpu.VMEM((LINES, 16, COLS), F32),
             pltpu.SemaphoreType.DMA((13,)),
         ],
     )
-    own_w, _ = lax.optimization_barrier((out_weight, sent))
-    weights = [own_w] + [shift_line(own_w, s) for s in range(1, LINES)]
     slab = lax.all_to_all(sent, OTHERS, split_axis=0, concat_axis=0, tiled=True)
-    w_sent = call(
-        repeat_kernel,
-        [shape(SOURCES, PAIR, W_LANES)],
-        (line_s, *weights),
-        scalars=1,
-        scratch=[pltpu.VMEM((LINES, 16, COLS), F32)],
-    )
-    w_sent, _ = lax.optimization_barrier((w_sent, slab))
-    w_raw = lax.all_to_all(w_sent, OTHERS, split_axis=0, concat_axis=0, tiled=True)
 
     probs, swap, mine = call(
         forward_kernel,
@@ -328,8 +334,7 @@
         scratch=[pltpu.VMEM((LINES, SOURCES, ROWS * COLS), BF16)],
     )
     sums = [pieces[0]] + [shift_line(pieces[s], s) for s in range(1, LINES)]
-    w_raw, _ = lax.optimization_barrier((w_raw, pieces[0]))
-    w_mine = call(weight_kernel, [shape(HD, HALF)], (w_raw,))
+    w_mine = call(weight_kernel, [shape(HD, HALF)], (slab,))
     w_theirs = swap_core(w_mine)
     grads = call(
         backward_kernel, [shape(TOKENS, HD)] * 3, (gate, slab, probs, w_mine, w_theirs), flops=10**9

time: 135 us -> 143 us (1.059)
  waiting for transfers between devices: 34.9 us -> 47 us
  blocking collectives: 39.3 us -> 35.9 us
    all_to_all x1, waiting for transfers between devices: 10.7 us -> 33.6 us  [shards(): slab = lax.all_to_all(sent, OTHERS, split_axis=0, concat_axis=0, tiled=True)]
    all_to_all x1 -> x0, waiting for transfers between devices: 10.1 us -> none  [shards(): lax.all_to_all(w_sent, OTHERS, split_axis=0, concat_axis=0, tiled=True)]
    ppermute x6, starting transfers between devices: 19.1 us -> 27.6 us  [shift_line(): return lax.ppermute(x, 'line', [(d, (d + s) % LINES) for d in range(LINES)])]
    all_to_all x1 -> x0, starting transfers between devices: 5.51 us -> none  [shards(): lax.all_to_all(w_sent, OTHERS, split_axis=0, concat_axis=0, tiled=True)]
    all_to_all x1, starting transfers between devices: 18.2 us -> 13.7 us  [shards(): slab = lax.all_to_all(sent, OTHERS, split_axis=0, concat_axis=0, tiled=True)]
    all_to_all x1, blocking collectives: 39.3 us -> 35.9 us  [shards(): lax.all_to_all(back, OTHERS, split_axis=0, concat_axis=0, tiled=True)]
    pallas_call x9 -> x8, Pallas kernels: 12.2 us -> 12.2 us  [call(): pl.pallas_call(kernel, out_shape=outs[0] if single else outs, in_specs=sm...]
  transfers between devices with their start and end apart: 10 -> 9, of which waited for: 6 -> 6; matrix products, arithmetic and copies ran while one was open for 0% -> 0% of each run, Pallas kernels for 3% -> 1%
where the time goes in v5:
time: 143 us; the launch traced here: 142 us
  waiting for transfers between devices  47 us (33%)
  starting transfers between devices  45.2 us (32%)
  blocking collectives  35.9 us (25%)
  Pallas kernels  12.2 us (9%)
  between operations  1.5 us (1%)
    all_to_all x1, blocking collectives, shards(): lax.all_to_all(back, OTHERS, split_axis=0, concat_axis=0, tiled=True)  35.9 us
    all_to_all x1, waiting for transfers between devices, shards(): slab = lax.all_to_all(sent, OTHERS, split_axis=0, concat_axis=0, tiled=True)  33.6 us
    ppermute x6, starting transfers between devices, shift_line(): return lax.ppermute(x, 'line', [(d, (d + s) % LINES) for d in range(LINES)])  27.6 us
    all_to_all x1, starting transfers between devices, shards(): slab = lax.all_to_all(sent, OTHERS, split_axis=0, concat_axis=0, tiled=True)  13.7 us
    pallas_call x8, Pallas kernels, call(): pl.pallas_call(kernel, out_shape=outs[0] if single else outs, in_specs=sm...  12.2 us
    ppermute x6, waiting for transfers between devices, shift_line(): return lax.ppermute(x, 'line', [(d, (d + s) % LINES) for d in range(LINES)])  11.8 us
    ppermute x2, starting transfers between devices, swap_core(): return lax.ppermute(x, 'core', [(0, 1), (1, 0)])  3.84 us
  transfers between devices with their start and end apart: 9, of which 6 were waited for; matrix products, arithmetic and copies ran while one was open for 0% of the time, Pallas kernels for 1%

profile of v5, /device:TPU:8, one launch (start us, length us, event | category | flops | bytes accessed | tf_op | source)
XLA Modules:
  0.0 142.4 jit_solution(3853347229517448594)
XLA Ops:
  0.6 4.5 %collective-permute-start.1 = (bf16[9,144]{1,0:T(8,128)(2,1)}, bf16[9,144]{1,0:T(8,128)(2,1)S(1)}, u32[]{:S(2)}, u32[]{:S(2)}) collective-permute-start(bf16[9,144]{1,0:T(8,128)(2,1)} %w0.1), channel_id=1, source_target_pairs={{0,256},{128,384},{256,0},{384,128},{1,257},{129,385},{257,1},{385... | collective-permute-start | bytes 7784 | tf_op jit(solution)/shard_map/ppermute | solution.py:293
  5.1 6.6 %collective-permute-start = (bf16[9,144]{1,0:T(8,128)(2,1)}, bf16[9,144]{1,0:T(8,128)(2,1)S(1)}, u32[]{:S(2)}, u32[]{:S(2)}) collective-permute-start(bf16[9,144]{1,0:T(8,128)(2,1)} %w0.1), channel_id=1, source_target_pairs={{0,128},{128,256},{256,384},{384,0},{1,129},{129,257},{257,385},{3... | collective-permute-start | bytes 7784 | tf_op jit(solution)/shard_map/ppermute | solution.py:293
  11.8 1.9 %collective-permute-start.2 = (bf16[9,144]{1,0:T(8,128)(2,1)}, bf16[9,144]{1,0:T(8,128)(2,1)S(1)}, u32[]{:S(2)}, u32[]{:S(2)}) collective-permute-start(bf16[9,144]{1,0:T(8,128)(2,1)} %w0.1), channel_id=1, source_target_pairs={{0,384},{128,0},{256,128},{384,256},{1,385},{129,1},{257,129},{385... | collective-permute-start | bytes 7784 | tf_op jit(solution)/shard_map/ppermute | solution.py:293
  13.7 0.0 collective-permute-done.1.w2
  13.7 0.0 copy-start
  13.7 0.0 collective-permute-done.w1
  13.7 0.0 copy-start.1
  13.7 3.8 %collective-permute-done.2.w3 = bf16[9,144]{1,0:T(8,128)(2,1)S(1)} collective-permute-done((bf16[9,144]{1,0:T(8,128)(2,1)}, bf16[9,144]{1,0:T(8,128)(2,1)S(1)}, u32[]{:S(2)}, u32[]{:S(2)}) %collective-permute-start.2) | collective-permute-done | bytes 2624 | tf_op jit(solution)/shard_map/ppermute | solution.py:293
  17.5 0.0 copy-start.2
  17.5 0.0 copy-done
  17.5 0.0 copy-done.1
  17.5 0.6 copy-done.2
  18.1 4.4 %shard_map.119 = bf16[64,2,5472]{2,1,0:T(2,128)(2,1)} custom-call(s32[1]{0:T(128)} %bitcast.core_ref, s32[1]{0:T(128)} %bitcast.2.line_ref, bf16[9,144]{1,0:T(8,128)(2,1)} %w0.1, bf16[9,144]{1,0:T(8,128)(2,1)} %copy-done.1, bf16[9,144]{1,0:T(8,128)(2,1)} %copy-done, bf16[9,144]{1,0:T(8,128)(2,1)} %copy-done.2, bf16[576,128]{1,0:T(8,128)(2,1)} %bitcast.24, ...), custom_call_target="tpu_custom_call" | custom-call | flops 100000000 | bytes 2148488 | tf_op jit(solution)/shard_map/pallas_call | solution.py:268
  22.5 0.0 copy-start.3
  22.6 0.0 copy-start.4
  22.6 13.7 %all-to-all-start = ((bf16[64,2,5472]{2,1,0:T(2,128)(2,1)}), bf16[64,2,5472]{2,1,0:T(2,128)(2,1)S(1)}, u32[]{:S(2)}, u32[]{:S(2)}) async-start(bf16[64,2,5472]{2,1,0:T(2,128)(2,1)} %shard_map.119), calls=%async_computation | async-start | bytes 2818048 | tf_op jit(solution)/shard_map/all_to_all | solution.py:321
  36.9 0.0 copy-done.3
  36.9 0.0 copy-done.4
  36.9 0.1 sine_add_fusion
  37.0 33.6 %all-to-all-done.x_ref.raw_ref = bf16[64,2,5472]{2,1,0:T(2,128)(2,1)S(1)} async-done(((bf16[64,2,5472]{2,1,0:T(2,128)(2,1)}), bf16[64,2,5472]{2,1,0:T(2,128)(2,1)S(1)}, u32[]{:S(2)}, u32[]{:S(2)}) %all-to-all-start) | async-done | bytes 1400864 | tf_op jit(solution)/shard_map/all_to_all | solution.py:321
  70.7 1.3 shard_map.120
  72.0 1.9 %collective-permute-start.4 = (bf16[128,1152]{1,0:T(8,128)(2,1)S(1)}, bf16[128,1152]{1,0:T(8,128)(2,1)S(1)}, u32[]{:S(2)}, u32[]{:S(2)}) collective-permute-start(bf16[128,1152]{1,0:T(8,128)(2,1)S(1)} %get-tuple-element.20.swap_ref), channel_id=1, source_target_pairs={{0,64},{64,0},{1,65},{65,1},{2,66},{66,2},{3,67},{67,3},{4,68},{68... | collective-permute-start | bytes 884744 | tf_op jit(solution)/shard_map/ppermute | solution.py:296
  73.9 1.5 %collective-permute-done.4.got_ref = bf16[128,1152]{1,0:T(8,128)(2,1)S(1)} collective-permute-done((bf16[128,1152]{1,0:T(8,128)(2,1)S(1)}, bf16[128,1152]{1,0:T(8,128)(2,1)S(1)}, u32[]{:S(2)}, u32[]{:S(2)}) %collective-permute-start.4) | collective-permute-done | bytes 294944 | tf_op jit(solution)/shard_map/ppermute | solution.py:296
  75.5 0.9 shard_map.123
  76.4 8.6 %collective-permute-start.5 = (bf16[64,1296]{1,0:T(8,128)(2,1)S(1)}, bf16[64,1296]{1,0:T(8,128)(2,1)S(1)}, u32[]{:S(2)}, u32[]{:S(2)}) collective-permute-start(bf16[64,1296]{1,0:T(8,128)(2,1)S(1)} %get-tuple-element.27), channel_id=1, source_target_pairs={{0,128},{128,256},{256,384},{384,0},{1,129},{129,257},{257,385},{3... | collective-permute-start | bytes 497672 | tf_op jit(solution)/shard_map/ppermute | solution.py:293
  85.0 2.1 %collective-permute-start.6 = (bf16[64,1296]{1,0:T(8,128)(2,1)S(1)}, bf16[64,1296]{1,0:T(8,128)(2,1)S(1)}, u32[]{:S(2)}, u32[]{:S(2)}) collective-permute-start(bf16[64,1296]{1,0:T(8,128)(2,1)S(1)} %get-tuple-element.28), channel_id=1, source_target_pairs={{0,256},{128,384},{256,0},{384,128},{1,257},{129,385},{257,1},{385... | collective-permute-start | bytes 497672 | tf_op jit(solution)/shard_map/ppermute | solution.py:293
  87.1 3.9 %collective-permute-start.7 = (bf16[64,1296]{1,0:T(8,128)(2,1)S(1)}, bf16[64,1296]{1,0:T(8,128)(2,1)S(1)}, u32[]{:S(2)}, u32[]{:S(2)}) collective-permute-start(bf16[64,1296]{1,0:T(8,128)(2,1)S(1)} %get-tuple-element.29), channel_id=1, source_target_pairs={{0,384},{128,0},{256,128},{384,256},{1,385},{129,1},{257,129},{385... | collective-permute-start | bytes 497672 | tf_op jit(solution)/shard_map/ppermute | solution.py:293
  91.0 0.6 shard_map.121.wm_ref
  91.6 1.9 %collective-permute-start.3 = (bf16[576,576]{1,0:T(8,128)(2,1)S(1)}, bf16[576,576]{1,0:T(8,128)(2,1)S(1)}, u32[]{:S(2)}, u32[]{:S(2)}) collective-permute-start(bf16[576,576]{1,0:T(8,128)(2,1)S(1)} %shard_map.121.wm_ref), channel_id=1, source_target_pairs={{0,64},{64,0},{1,65},{65,1},{2,66},{66,2},{3,67},{67,3},{4,68},{68... | collective-permute-start | bytes 1990664 | tf_op jit(solution)/shard_map/ppermute | solution.py:296
  93.6 4.0 %collective-permute-done.5.p1_ref = bf16[64,1296]{1,0:T(8,128)(2,1)S(1)} collective-permute-done((bf16[64,1296]{1,0:T(8,128)(2,1)S(1)}, bf16[64,1296]{1,0:T(8,128)(2,1)S(1)}, u32[]{:S(2)}, u32[]{:S(2)}) %collective-permute-start.5) | collective-permute-done | bytes 165920 | tf_op jit(solution)/shard_map/ppermute | solution.py:293
  97.6 3.1 %collective-permute-done.6.p2_ref = bf16[64,1296]{1,0:T(8,128)(2,1)S(1)} collective-permute-done((bf16[64,1296]{1,0:T(8,128)(2,1)S(1)}, bf16[64,1296]{1,0:T(8,128)(2,1)S(1)}, u32[]{:S(2)}, u32[]{:S(2)}) %collective-permute-start.6) | collective-permute-done | bytes 165920 | tf_op jit(solution)/shard_map/ppermute | solution.py:293
  100.6 1.0 collective-permute-done.7.p3_ref
  101.6 0.3 shard_map.124.sum_ref
  102.0 0.0 collective-permute-done.3.wt_ref
  102.0 2.4 %shard_map.122 = (bf16[128,576]{1,0:T(8,128)(2,1)S(1)}, bf16[128,576]{1,0:T(8,128)(2,1)S(1)}, bf16[128,576]{1,0:T(8,128)(2,1)S(1)}) custom-call(f32[1,1152]{1,0:T(1,128)S(1)} %reshape.44.gate_ref, bf16[64,2,5472]{2,1,0:T(2,128)(2,1)S(1)} %all-to-all-done.x_ref.raw_ref, f32[8,128,128]{2,1,0:T(8,128)S(1)} %get-tuple-element.21.probs_ref, ...), custom_call_target="tpu_custom_call" | custom-call | flops 1000000000 | bytes 3699200 | tf_op jit(solution)/shard_map/pallas_call | solution.py:268
  104.4 0.2 shard_map.125
  104.6 35.9 %all_to_all.10.z_ref = bf16[64,2,3024]{2,1,0:T(2,128)(2,1)S(1)} all-to-all(bf16[64,2,3024]{2,1,0:T(2,128)(2,1)S(1)} %shard_map.125), channel_id=1, replica_groups=mesh['line'=4,'core'=2,'x'=4,'y'=2,'z'=8] {'x','y','z'}, dimensions={0} | all-to-all | bytes 1548288 | tf_op jit(solution)/shard_map/all_to_all | solution.py:344
  140.5 2.0 %shard_map.126 = (bf16[128,1152]{1,0:T(8,128)(2,1)}, bf16[576,128]{1,0:T(8,128)(2,1)}, bf16[576,128]{1,0:T(8,128)(2,1)}, bf16[576,128]{1,0:T(8,128)(2,1)}, f32[9,144]{1,0:T(8,128)}) custom-call(s32[1]{0:T(128)} %bitcast.core_ref, f32[1,1152]{1,0:T(1,128)S(1)} %reshape.44.gate_ref, bf16[64,2,3024]{2,1,0:T(2,128)(2,1)S(1)} %all_to_all.10.z_ref, ...), custom_call_target="tpu_custom_call" | custom-call | flops 100000000 | bytes 2848324 | tf_op jit(solution)/shard_map/pallas_call | solution.py:268
  (1 shorter events, 0.0 us)
Async XLA Ops:
  0.6 13.1 %collective-permute-start.1 = (bf16[9,144]{1,0:T(8,128)(2,1)}, bf16[9,144]{1,0:T(8,128)(2,1)S(1)}, u32[]{:S(2)}, u32[]{:S(2)}) collective-permute-start(bf16[9,144]{1,0:T(8,128)(2,1)} %w0.1), channel_id=1, source_target_pairs={{0,256},{128,384},{256,0},{384,128},{1,257},{129,385},{257,1},{385... | collective-permute-start | bytes 7784 | tf_op jit(solution)/shard_map/ppermute | solution.py:293
  5.1 8.6 %collective-permute-start = (bf16[9,144]{1,0:T(8,128)(2,1)}, bf16[9,144]{1,0:T(8,128)(2,1)S(1)}, u32[]{:S(2)}, u32[]{:S(2)}) collective-permute-start(bf16[9,144]{1,0:T(8,128)(2,1)} %w0.1), channel_id=1, source_target_pairs={{0,128},{128,256},{256,384},{384,0},{1,129},{129,257},{257,385},{3... | collective-permute-start | bytes 7784 | tf_op jit(solution)/shard_map/ppermute | solution.py:293
  11.8 5.8 %collective-permute-start.2 = (bf16[9,144]{1,0:T(8,128)(2,1)}, bf16[9,144]{1,0:T(8,128)(2,1)S(1)}, u32[]{:S(2)}, u32[]{:S(2)}) collective-permute-start(bf16[9,144]{1,0:T(8,128)(2,1)} %w0.1), channel_id=1, source_target_pairs={{0,384},{128,0},{256,128},{384,256},{1,385},{129,1},{257,129},{385... | collective-permute-start | bytes 7784 | tf_op jit(solution)/shard_map/ppermute | solution.py:293
  13.7 3.8 %copy-start = (bf16[9,144]{1,0:T(8,128)(2,1)}, bf16[9,144]{1,0:T(8,128)(2,1)S(1)}, u32[]{:S(2)}) copy-start(bf16[9,144]{1,0:T(8,128)(2,1)S(1)} %collective-permute-done.1.w2) | copy-start | bytes 7780
  13.7 3.8 %copy-start.1 = (bf16[9,144]{1,0:T(8,128)(2,1)}, bf16[9,144]{1,0:T(8,128)(2,1)S(1)}, u32[]{:S(2)}) copy-start(bf16[9,144]{1,0:T(8,128)(2,1)S(1)} %collective-permute-done.w1) | copy-start | bytes 7780
  17.5 0.6 copy-start.2
  22.5 14.4 %copy-start.3 = (f32[1152]{0:T(1024)S(1)}, f32[1152]{0:T(1024)}, u32[]{:S(2)}) copy-start(f32[1152]{0:T(1024)} %constant.26.clone) | copy-start | bytes 13828
  22.6 14.4 %copy-start.4 = (f32[1152]{0:T(1024)S(1)}, f32[1152]{0:T(1024)}, u32[]{:S(2)}) copy-start(f32[1152]{0:T(1024)} %constant.25.clone) | copy-start | bytes 13828
  22.6 48.1 %all-to-all-start = ((bf16[64,2,5472]{2,1,0:T(2,128)(2,1)}), bf16[64,2,5472]{2,1,0:T(2,128)(2,1)S(1)}, u32[]{:S(2)}, u32[]{:S(2)}) async-start(bf16[64,2,5472]{2,1,0:T(2,128)(2,1)} %shard_map.119), calls=%async_computation | async-start | bytes 2818048 | tf_op jit(solution)/shard_map/all_to_all | solution.py:321
  72.0 3.5 %collective-permute-start.4 = (bf16[128,1152]{1,0:T(8,128)(2,1)S(1)}, bf16[128,1152]{1,0:T(8,128)(2,1)S(1)}, u32[]{:S(2)}, u32[]{:S(2)}) collective-permute-start(bf16[128,1152]{1,0:T(8,128)(2,1)S(1)} %get-tuple-element.20.swap_ref), channel_id=1, source_target_pairs={{0,64},{64,0},{1,65},{65,1},{2,66},{66,2},{3,67},{67,3},{4,68},{68... | collective-permute-start | bytes 884744 | tf_op jit(solution)/shard_map/ppermute | solution.py:296
  76.4 21.2 %collective-permute-start.5 = (bf16[64,1296]{1,0:T(8,128)(2,1)S(1)}, bf16[64,1296]{1,0:T(8,128)(2,1)S(1)}, u32[]{:S(2)}, u32[]{:S(2)}) collective-permute-start(bf16[64,1296]{1,0:T(8,128)(2,1)S(1)} %get-tuple-element.27), channel_id=1, source_target_pairs={{0,128},{128,256},{256,384},{384,0},{1,129},{129,257},{257,385},{3... | collective-permute-start | bytes 497672 | tf_op jit(solution)/shard_map/ppermute | solution.py:293
  85.0 15.7 %collective-permute-start.6 = (bf16[64,1296]{1,0:T(8,128)(2,1)S(1)}, bf16[64,1296]{1,0:T(8,128)(2,1)S(1)}, u32[]{:S(2)}, u32[]{:S(2)}) collective-permute-start(bf16[64,1296]{1,0:T(8,128)(2,1)S(1)} %get-tuple-element.28), channel_id=1, source_target_pairs={{0,256},{128,384},{256,0},{384,128},{1,257},{129,385},{257,1},{385... | collective-permute-start | bytes 497672 | tf_op jit(solution)/shard_map/ppermute | solution.py:293
  87.1 14.5 %collective-permute-start.7 = (bf16[64,1296]{1,0:T(8,128)(2,1)S(1)}, bf16[64,1296]{1,0:T(8,128)(2,1)S(1)}, u32[]{:S(2)}, u32[]{:S(2)}) collective-permute-start(bf16[64,1296]{1,0:T(8,128)(2,1)S(1)} %get-tuple-element.29), channel_id=1, source_target_pairs={{0,384},{128,0},{256,128},{384,256},{1,385},{129,1},{257,129},{385... | collective-permute-start | bytes 497672 | tf_op jit(solution)/shard_map/ppermute | solution.py:293
  91.6 10.3 %collective-permute-start.3 = (bf16[576,576]{1,0:T(8,128)(2,1)S(1)}, bf16[576,576]{1,0:T(8,128)(2,1)S(1)}, u32[]{:S(2)}, u32[]{:S(2)}) collective-permute-start(bf16[576,576]{1,0:T(8,128)(2,1)S(1)} %shard_map.121.wm_ref), channel_id=1, source_target_pairs={{0,64},{64,0},{1,65},{65,1},{2,66},{66,2},{3,67},{67,3},{4,68},{68... | collective-permute-start | bytes 1990664 | tf_op jit(solution)/shard_map/ppermute | solution.py:296

commit v6 on v4

--- a/solution.py
+++ b/solution.py
@@ -304,22 +304,21 @@
     own_w, _ = lax.optimization_barrier((out_weight, sent))
     weights = [own_w] + [shift_line(own_w, s) for s in range(1, LINES)]
     slab = lax.all_to_all(sent, OTHERS, split_axis=0, concat_axis=0, tiled=True)
-    w_sent = call(
-        repeat_kernel,
-        [shape(SOURCES, PAIR, W_LANES)],
-        (line_s, *weights),
-        scalars=1,
-        scratch=[pltpu.VMEM((LINES, 16, COLS), F32)],
-    )
-    w_sent, _ = lax.optimization_barrier((w_sent, slab))
-    w_raw = lax.all_to_all(w_sent, OTHERS, split_axis=0, concat_axis=0, tiled=True)
-
     probs, swap, mine = call(
         forward_kernel,
         [shape(HEADS, TOKENS, TOKENS, kind=F32), shape(TOKENS, HD + HALF), shape(TOKENS, HALF)],
         (gate, slab),
     )
     got = swap_core(swap)
+    *late, _ = lax.optimization_barrier((*weights, swap))
+    w_sent = call(
+        repeat_kernel,
+        [shape(SOURCES, PAIR, W_LANES)],
+        (line_s, *late),
+        scalars=1,
+        scratch=[pltpu.VMEM((LINES, 16, COLS), F32)],
+    )
+    w_raw = lax.all_to_all(w_sent, OTHERS, split_axis=0, concat_axis=0, tiled=True)
     pieces = call(
         share_kernel,
         [shape(SOURCES, ROWS * COLS)] * LINES,

time: 135 us -> 139 us (1.030)
  waiting for transfers between devices: 34.9 us -> 37.5 us
  blocking collectives: 39.3 us -> 40.8 us
  starting transfers between devices: 46.6 us -> 45.1 us
    ppermute x6, waiting for transfers between devices: 12.5 us -> 0.02 us  [shift_line(): return lax.ppermute(x, 'line', [(d, (d + s) % LINES) for d in range(LINES)])]
    all_to_all x1, waiting for transfers between devices: 10.7 us -> 18.1 us  [shards(): slab = lax.all_to_all(sent, OTHERS, split_axis=0, concat_axis=0, tiled=True)]
    all_to_all x1, waiting for transfers between devices: 10.1 us -> 17 us  [shards(): lax.all_to_all(w_sent, OTHERS, split_axis=0, concat_axis=0, tiled=True)]
    all_to_all x1, blocking collectives: 39.3 us -> 40.8 us  [shards(): lax.all_to_all(back, OTHERS, split_axis=0, concat_axis=0, tiled=True)]
  transfers between devices with their start and end apart: 10 -> 10, of which waited for: 6 -> 4; matrix products, arithmetic and copies ran while one was open for 0% -> 0% of each run, Pallas kernels for 3% -> 3%
where the time goes in v6:
time: 139 us; the launch traced here: 138 us
  starting transfers between devices  45.1 us (32%)
  blocking collectives  40.8 us (29%)
  waiting for transfers between devices  37.5 us (27%)
  Pallas kernels  13.2 us (9%)
  between operations  1.53 us (1%)
    all_to_all x1, blocking collectives, shards(): lax.all_to_all(back, OTHERS, split_axis=0, concat_axis=0, tiled=True)  40.8 us
    ppermute x6, starting transfers between devices, shift_line(): return lax.ppermute(x, 'line', [(d, (d + s) % LINES) for d in range(LINES)])  18.3 us
    all_to_all x1, starting transfers between devices, shards(): slab = lax.all_to_all(sent, OTHERS, split_axis=0, concat_axis=0, tiled=True)  18.2 us
    all_to_all x1, waiting for transfers between devices, shards(): slab = lax.all_to_all(sent, OTHERS, split_axis=0, concat_axis=0, tiled=True)  18.1 us
    all_to_all x1, waiting for transfers between devices, shards(): lax.all_to_all(w_sent, OTHERS, split_axis=0, concat_axis=0, tiled=True)  17 us
    pallas_call x9, Pallas kernels, call(): pl.pallas_call(kernel, out_shape=outs[0] if single else outs, in_specs=sm...  13.2 us
    all_to_all x1, starting transfers between devices, shards(): lax.all_to_all(w_sent, OTHERS, split_axis=0, concat_axis=0, tiled=True)  4.77 us
    ppermute x2, starting transfers between devices, swap_core(): return lax.ppermute(x, 'core', [(0, 1), (1, 0)])  3.84 us
  transfers between devices with their start and end apart: 10, of which 4 were waited for; matrix products, arithmetic and copies ran while one was open for 0% of the time, Pallas kernels for 3%

profile of v6, /device:TPU:8, one launch (start us, length us, event | category | flops | bytes accessed | tf_op | source)
XLA Modules:
  0.0 138.2 jit_solution(6233185034020121682)
XLA Ops:
  0.6 3.4 %shard_map.119 = bf16[64,2,2880]{2,1,0:T(2,128)(2,1)} custom-call(s32[1]{0:T(128)} %bitcast.core_ref, bf16[576,128]{1,0:T(8,128)(2,1)} %bitcast.24, bf16[576,128]{1,0:T(8,128)(2,1)} %bitcast.25, bf16[576,128]{1,0:T(8,128)(2,1)} %bitcast.26, bf16[128,1152]{1,0:T(8,128)(2,1)} %bitcast.23), custom_call_target="tpu_custom_call" | custom-call | flops 100000000 | bytes 1474564 | tf_op jit(solution)/shard_map/pallas_call | solution.py:253
  4.0 0.0 copy-start
  4.0 0.0 copy-start.2
  4.0 18.2 %all-to-all-start = ((bf16[64,2,2880]{2,1,0:T(2,128)(2,1)}), bf16[64,2,2880]{2,1,0:T(2,128)(2,1)S(1)}, u32[]{:S(2)}, u32[]{:S(2)}) async-start(bf16[64,2,2880]{2,1,0:T(2,128)(2,1)} %shard_map.119), calls=%async_computation | async-start | bytes 1507328 | tf_op jit(solution)/shard_map/all_to_all | solution.py:306
  22.2 0.0 copy-done
  22.2 0.0 copy-start.1
  22.2 3.2 %collective-permute-start.2 = (bf16[9,144]{1,0:T(8,128)(2,1)S(1)}, bf16[9,144]{1,0:T(8,128)(2,1)S(1)}, u32[]{:S(2)}, u32[]{:S(2)}) collective-permute-start(bf16[9,144]{1,0:T(8,128)(2,1)S(1)} %copy-done), channel_id=1, source_target_pairs={{0,384},{128,0},{256,128},{384,256},{1,385},{129,1},{257,129},{385... | collective-permute-start | bytes 7784 | tf_op jit(solution)/shard_map/ppermute | solution.py:278
  25.5 2.7 %collective-permute-start.1 = (bf16[9,144]{1,0:T(8,128)(2,1)S(1)}, bf16[9,144]{1,0:T(8,128)(2,1)S(1)}, u32[]{:S(2)}, u32[]{:S(2)}) collective-permute-start(bf16[9,144]{1,0:T(8,128)(2,1)S(1)} %copy-done), channel_id=1, source_target_pairs={{0,256},{128,384},{256,0},{384,128},{1,257},{129,385},{257,1},{385... | collective-permute-start | bytes 7784 | tf_op jit(solution)/shard_map/ppermute | solution.py:278
  28.2 3.5 %collective-permute-start = (bf16[9,144]{1,0:T(8,128)(2,1)S(1)}, bf16[9,144]{1,0:T(8,128)(2,1)S(1)}, u32[]{:S(2)}, u32[]{:S(2)}) collective-permute-start(bf16[9,144]{1,0:T(8,128)(2,1)S(1)} %copy-done), channel_id=1, source_target_pairs={{0,128},{128,256},{256,384},{384,0},{1,129},{129,257},{257,385},{3... | collective-permute-start | bytes 7784 | tf_op jit(solution)/shard_map/ppermute | solution.py:278
  32.3 0.0 copy-done.2
  32.3 0.0 copy-done.1
  32.3 0.1 sine_add_fusion
  32.4 18.1 %all-to-all-done.x_ref = bf16[64,2,2880]{2,1,0:T(2,128)(2,1)S(1)} async-done(((bf16[64,2,2880]{2,1,0:T(2,128)(2,1)}), bf16[64,2,2880]{2,1,0:T(2,128)(2,1)S(1)}, u32[]{:S(2)}, u32[]{:S(2)}) %all-to-all-start) | async-done | bytes 737312 | tf_op jit(solution)/shard_map/all_to_all | solution.py:306
  50.5 1.3 shard_map.120
  51.8 0.0 collective-permute-done.2.w3
  51.8 0.0 collective-permute-done.1.w2
  51.9 0.0 collective-permute-done.w1
  51.9 1.2 shard_map.121
  53.1 4.8 %all-to-all-start.1 = ((bf16[64,2,2592]{2,1,0:T(2,128)(2,1)}), bf16[64,2,2592]{2,1,0:T(2,128)(2,1)S(1)}, u32[]{:S(2)}, u32[]{:S(2)}) async-start(bf16[64,2,2592]{2,1,0:T(2,128)(2,1)} %shard_map.121), calls=%async_computation.1 | async-start | bytes 1376256 | tf_op jit(solution)/shard_map/all_to_all | solution.py:321
  57.9 1.9 %collective-permute-start.3 = (bf16[128,1152]{1,0:T(8,128)(2,1)S(1)}, bf16[128,1152]{1,0:T(8,128)(2,1)S(1)}, u32[]{:S(2)}, u32[]{:S(2)}) collective-permute-start(bf16[128,1152]{1,0:T(8,128)(2,1)S(1)} %get-tuple-element.26.swap_ref), channel_id=1, source_target_pairs={{0,64},{64,0},{1,65},{65,1},{2,66},{66,2},{3,67},{67,3},{4,68},{68... | collective-permute-start | bytes 884744 | tf_op jit(solution)/shard_map/ppermute | solution.py:281
  59.8 1.5 %collective-permute-done.3.got_ref = bf16[128,1152]{1,0:T(8,128)(2,1)S(1)} collective-permute-done((bf16[128,1152]{1,0:T(8,128)(2,1)S(1)}, bf16[128,1152]{1,0:T(8,128)(2,1)S(1)}, u32[]{:S(2)}, u32[]{:S(2)}) %collective-permute-start.3) | collective-permute-done | bytes 294944 | tf_op jit(solution)/shard_map/ppermute | solution.py:281
  61.3 0.9 shard_map.122
  62.2 2.6 %collective-permute-start.5 = (bf16[64,1296]{1,0:T(8,128)(2,1)S(1)}, bf16[64,1296]{1,0:T(8,128)(2,1)S(1)}, u32[]{:S(2)}, u32[]{:S(2)}) collective-permute-start(bf16[64,1296]{1,0:T(8,128)(2,1)S(1)} %get-tuple-element.39), channel_id=1, source_target_pairs={{0,128},{128,256},{256,384},{384,0},{1,129},{129,257},{257,385},{3... | collective-permute-start | bytes 497672 | tf_op jit(solution)/shard_map/ppermute | solution.py:278
  64.8 4.4 %collective-permute-start.6 = (bf16[64,1296]{1,0:T(8,128)(2,1)S(1)}, bf16[64,1296]{1,0:T(8,128)(2,1)S(1)}, u32[]{:S(2)}, u32[]{:S(2)}) collective-permute-start(bf16[64,1296]{1,0:T(8,128)(2,1)S(1)} %get-tuple-element.40), channel_id=1, source_target_pairs={{0,256},{128,384},{256,0},{384,128},{1,257},{129,385},{257,1},{385... | collective-permute-start | bytes 497672 | tf_op jit(solution)/shard_map/ppermute | solution.py:278
  69.2 1.9 %collective-permute-start.7 = (bf16[64,1296]{1,0:T(8,128)(2,1)S(1)}, bf16[64,1296]{1,0:T(8,128)(2,1)}, u32[]{:S(2)}, u32[]{:S(2)}) collective-permute-start(bf16[64,1296]{1,0:T(8,128)(2,1)S(1)} %get-tuple-element.41), channel_id=1, source_target_pairs={{0,384},{128,0},{256,128},{384,256},{1,385},{129,1},{257,129},{385... | collective-permute-start | bytes 497672 | tf_op jit(solution)/shard_map/ppermute | solution.py:278
  71.2 17.0 %all-to-all-done.1.raw_ref = bf16[64,2,2592]{2,1,0:T(2,128)(2,1)S(1)} async-done(((bf16[64,2,2592]{2,1,0:T(2,128)(2,1)}), bf16[64,2,2592]{2,1,0:T(2,128)(2,1)S(1)}, u32[]{:S(2)}, u32[]{:S(2)}) %all-to-all-start.1) | async-done | bytes 663584 | tf_op jit(solution)/shard_map/all_to_all | solution.py:321
  88.2 0.5 shard_map.123.wm_ref
  88.7 1.9 %collective-permute-start.4 = (bf16[576,576]{1,0:T(8,128)(2,1)S(1)}, bf16[576,576]{1,0:T(8,128)(2,1)S(1)}, u32[]{:S(2)}, u32[]{:S(2)}) collective-permute-start(bf16[576,576]{1,0:T(8,128)(2,1)S(1)} %shard_map.123.wm_ref), channel_id=1, source_target_pairs={{0,64},{64,0},{1,65},{65,1},{2,66},{66,2},{3,67},{67,3},{4,68},{68... | collective-permute-start | bytes 1990664 | tf_op jit(solution)/shard_map/ppermute | solution.py:281
  90.6 0.0 collective-permute-done.5.p1_ref
  90.6 0.0 collective-permute-done.6.p2_ref
  90.6 0.0 collective-permute-done.7.p3_ref
  90.6 1.3 shard_map.125.sum_ref
  91.9 0.9 collective-permute-done.4.wt_ref
  92.8 2.5 %shard_map.124 = (bf16[128,576]{1,0:T(8,128)(2,1)S(1)}, bf16[128,576]{1,0:T(8,128)(2,1)S(1)}, bf16[128,576]{1,0:T(8,128)(2,1)S(1)}) custom-call(f32[1,1152]{1,0:T(1,128)S(1)} %reshape.44.gate_ref, bf16[64,2,2880]{2,1,0:T(2,128)(2,1)S(1)} %all-to-all-done.x_ref, f32[8,128,128]{2,1,0:T(8,128)S(1)} %get-tuple-element.27.probs_ref, ...), custom_call_target="tpu_custom_call" | custom-call | flops 1000000000 | bytes 3035648 | tf_op jit(solution)/shard_map/pallas_call | solution.py:253
  95.2 0.2 shard_map.126
  95.5 40.8 %all_to_all.15.z_ref = bf16[64,2,3024]{2,1,0:T(2,128)(2,1)S(1)} all-to-all(bf16[64,2,3024]{2,1,0:T(2,128)(2,1)S(1)} %shard_map.126), channel_id=1, replica_groups=mesh['line'=4,'core'=2,'x'=4,'y'=2,'z'=8] {'x','y','z'}, dimensions={0} | all-to-all | bytes 1548288 | tf_op jit(solution)/shard_map/all_to_all | solution.py:338
  136.2 2.0 %shard_map.127 = (bf16[128,1152]{1,0:T(8,128)(2,1)}, bf16[576,128]{1,0:T(8,128)(2,1)}, bf16[576,128]{1,0:T(8,128)(2,1)}, bf16[576,128]{1,0:T(8,128)(2,1)}, f32[9,144]{1,0:T(8,128)}) custom-call(s32[1]{0:T(128)} %bitcast.core_ref, f32[1,1152]{1,0:T(1,128)S(1)} %reshape.44.gate_ref, bf16[64,2,3024]{2,1,0:T(2,128)(2,1)S(1)} %all_to_all.15.z_ref, ...), custom_call_target="tpu_custom_call" | custom-call | flops 100000000 | bytes 2848324 | tf_op jit(solution)/shard_map/pallas_call | solution.py:253
  (1 shorter events, 0.0 us)
Async XLA Ops:
  4.0 18.2 %copy-start = (bf16[9,144]{1,0:T(8,128)(2,1)S(1)}, bf16[9,144]{1,0:T(8,128)(2,1)}, u32[]{:S(2)}) copy-start(bf16[9,144]{1,0:T(8,128)(2,1)} %w0) | copy-start | bytes 7780
  4.0 28.3 %copy-start.2 = (f32[1152]{0:T(1024)S(1)}, f32[1152]{0:T(1024)}, u32[]{:S(2)}) copy-start(f32[1152]{0:T(1024)} %constant.25.clone) | copy-start | bytes 13828
  4.0 46.5 %all-to-all-start = ((bf16[64,2,2880]{2,1,0:T(2,128)(2,1)}), bf16[64,2,2880]{2,1,0:T(2,128)(2,1)S(1)}, u32[]{:S(2)}, u32[]{:S(2)}) async-start(bf16[64,2,2880]{2,1,0:T(2,128)(2,1)} %shard_map.119), calls=%async_computation | async-start | bytes 1507328 | tf_op jit(solution)/shard_map/all_to_all | solution.py:306
  22.2 10.1 %copy-start.1 = (f32[1152]{0:T(1024)S(1)}, f32[1152]{0:T(1024)}, u32[]{:S(2)}) copy-start(f32[1152]{0:T(1024)} %constant.26.clone) | copy-start | bytes 13828
  22.2 29.6 %collective-permute-start.2 = (bf16[9,144]{1,0:T(8,128)(2,1)S(1)}, bf16[9,144]{1,0:T(8,128)(2,1)S(1)}, u32[]{:S(2)}, u32[]{:S(2)}) collective-permute-start(bf16[9,144]{1,0:T(8,128)(2,1)S(1)} %copy-done), channel_id=1, source_target_pairs={{0,384},{128,0},{256,128},{384,256},{1,385},{129,1},{257,129},{385... | collective-permute-start | bytes 7784 | tf_op jit(solution)/shard_map/ppermute | solution.py:278
  25.5 26.4 %collective-permute-start.1 = (bf16[9,144]{1,0:T(8,128)(2,1)S(1)}, bf16[9,144]{1,0:T(8,128)(2,1)S(1)}, u32[]{:S(2)}, u32[]{:S(2)}) collective-permute-start(bf16[9,144]{1,0:T(8,128)(2,1)S(1)} %copy-done), channel_id=1, source_target_pairs={{0,256},{128,384},{256,0},{384,128},{1,257},{129,385},{257,1},{385... | collective-permute-start | bytes 7784 | tf_op jit(solution)/shard_map/ppermute | solution.py:278
  28.2 23.7 %collective-permute-start = (bf16[9,144]{1,0:T(8,128)(2,1)S(1)}, bf16[9,144]{1,0:T(8,128)(2,1)S(1)}, u32[]{:S(2)}, u32[]{:S(2)}) collective-permute-start(bf16[9,144]{1,0:T(8,128)(2,1)S(1)} %copy-done), channel_id=1, source_target_pairs={{0,128},{128,256},{256,384},{384,0},{1,129},{129,257},{257,385},{3... | collective-permute-start | bytes 7784 | tf_op jit(solution)/shard_map/ppermute | solution.py:278
  53.1 35.1 %all-to-all-start.1 = ((bf16[64,2,2592]{2,1,0:T(2,128)(2,1)}), bf16[64,2,2592]{2,1,0:T(2,128)(2,1)S(1)}, u32[]{:S(2)}, u32[]{:S(2)}) async-start(bf16[64,2,2592]{2,1,0:T(2,128)(2,1)} %shard_map.121), calls=%async_computation.1 | async-start | bytes 1376256 | tf_op jit(solution)/shard_map/all_to_all | solution.py:321
  57.9 3.5 %collective-permute-start.3 = (bf16[128,1152]{1,0:T(8,128)(2,1)S(1)}, bf16[128,1152]{1,0:T(8,128)(2,1)S(1)}, u32[]{:S(2)}, u32[]{:S(2)}) collective-permute-start(bf16[128,1152]{1,0:T(8,128)(2,1)S(1)} %get-tuple-element.26.swap_ref), channel_id=1, source_target_pairs={{0,64},{64,0},{1,65},{65,1},{2,66},{66,2},{3,67},{67,3},{4,68},{68... | collective-permute-start | bytes 884744 | tf_op jit(solution)/shard_map/ppermute | solution.py:281
  62.2 28.4 %collective-permute-start.5 = (bf16[64,1296]{1,0:T(8,128)(2,1)S(1)}, bf16[64,1296]{1,0:T(8,128)(2,1)S(1)}, u32[]{:S(2)}, u32[]{:S(2)}) collective-permute-start(bf16[64,1296]{1,0:T(8,128)(2,1)S(1)} %get-tuple-element.39), channel_id=1, source_target_pairs={{0,128},{128,256},{256,384},{384,0},{1,129},{129,257},{257,385},{3... | collective-permute-start | bytes 497672 | tf_op jit(solution)/shard_map/ppermute | solution.py:278
  64.8 25.8 %collective-permute-start.6 = (bf16[64,1296]{1,0:T(8,128)(2,1)S(1)}, bf16[64,1296]{1,0:T(8,128)(2,1)S(1)}, u32[]{:S(2)}, u32[]{:S(2)}) collective-permute-start(bf16[64,1296]{1,0:T(8,128)(2,1)S(1)} %get-tuple-element.40), channel_id=1, source_target_pairs={{0,256},{128,384},{256,0},{384,128},{1,257},{129,385},{257,1},{385... | collective-permute-start | bytes 497672 | tf_op jit(solution)/shard_map/ppermute | solution.py:278
  69.2 21.4 %collective-permute-start.7 = (bf16[64,1296]{1,0:T(8,128)(2,1)S(1)}, bf16[64,1296]{1,0:T(8,128)(2,1)}, u32[]{:S(2)}, u32[]{:S(2)}) collective-permute-start(bf16[64,1296]{1,0:T(8,128)(2,1)S(1)} %get-tuple-element.41), channel_id=1, source_target_pairs={{0,384},{128,0},{256,128},{384,256},{1,385},{129,1},{257,129},{385... | collective-permute-start | bytes 497672 | tf_op jit(solution)/shard_map/ppermute | solution.py:278
  88.7 4.1 %collective-permute-start.4 = (bf16[576,576]{1,0:T(8,128)(2,1)S(1)}, bf16[576,576]{1,0:T(8,128)(2,1)S(1)}, u32[]{:S(2)}, u32[]{:S(2)}) collective-permute-start(bf16[576,576]{1,0:T(8,128)(2,1)S(1)} %shard_map.123.wm_ref), channel_id=1, source_target_pairs={{0,64},{64,0},{1,65},{65,1},{2,66},{66,2},{3,67},{67,3},{4,68},{68... | collective-permute-start | bytes 1990664 | tf_op jit(solution)/shard_map/ppermute | solution.py:281

commit v7 on v3

--- a/solution.py
+++ b/solution.py
@@ -24,10 +24,9 @@
 
 AXES = {"line": LINES, "core": CORES, "x": 4, "y": 2, "z": 8}
 OTHERS = ("x", "y", "z")
-W_PEERS = LINES * SOURCES
-W_LANES = (ROWS + 1) // 2 * COLS
-
-AT_U = 0
+W_LANES = 768
+
+AT_U = W_LANES
 AT_Q = AT_U + D
 AT_K = AT_Q + HD
 AT_V = AT_K + HD
@@ -62,21 +61,9 @@
     return x.reshape(SOURCES, PAIR, x.shape[-1])
 
 
-def repeat_kernel(w_ref, x_ref):
-    w = w_ref[...].astype(F32)
-    rows = [w[i : i + 1] for i in range(ROWS)]
-    pair = []
-    for j in range(PAIR):
-        part = rows[SPLIT * j : SPLIT * (j + 1)]
-        part = part + [jnp.zeros((1, COLS), F32)] * (SPLIT - len(part))
-        pair.append(jnp.concatenate(part, axis=1))
-    odd = (iota((TOKENS, W_LANES), 0) & 1) == 1
-    both = spread(jnp.where(odd, pair[1], pair[0]).astype(BF16))
-    for b in range(LINES):
-        x_ref[b * SOURCES : (b + 1) * SOURCES] = both
-
-
-def pack_kernel(core_ref, q_ref, k_ref, v_ref, u_ref, x_ref, feats, up, packed, sems):
+def pack_kernel(
+    core_ref, w_ref, q_ref, k_ref, v_ref, u_ref, x_ref, feats, up, packed, sems
+):
     copies = []
     for h in range(4):
         part = pl.ds(h * (TOKENS // 4), TOKENS // 4)
@@ -96,7 +83,16 @@
             packed.at[:, :, part], x_ref.at[:, :, part], sems.at[10 + n]
         )
 
-    outs = [out(0, AT_U, D), out(1, AT_Q, 2 * HD), out(2, AT_V, HD)]
+    outs = [out(0, 0, AT_Q), out(1, AT_Q, 2 * HD), out(2, AT_V, HD)]
+    w = w_ref[...].astype(F32)
+    rows = [w[i : i + 1] for i in range(ROWS)]
+    pair = []
+    for j in range(PAIR):
+        part = rows[SPLIT * j : SPLIT * (j + 1)]
+        pad = jnp.zeros((1, W_LANES - len(part) * COLS), F32)
+        pair.append(jnp.concatenate(part + [pad], axis=1))
+    odd = (iota((TOKENS, W_LANES), 0) & 1) == 1
+    packed[:, :, :W_LANES] = spread(jnp.where(odd, pair[1], pair[0]).astype(BF16))
     order = order_matrix()
     for copy in copies[:4]:
         copy.wait()
@@ -119,10 +115,13 @@
         copy.wait()
 
 
-def weight_kernel(raw_ref, w_ref):
+def weight_kernel(first_ref, own_ref, r1_ref, r2_ref, r3_ref, w_ref, raw):
+    for s, ref in enumerate((own_ref, r1_ref, r2_ref, r3_ref)):
+        raw[s] = ref[...].reshape(TOKENS, W_LANES)
+    first = first_ref[0]
     pick = iota((SOURCES, TOKENS), 1) - PAIR * iota((SOURCES, TOKENS), 0)
     for b in range(LINES):
-        block = raw_ref[b * SOURCES : (b + 1) * SOURCES].reshape(TOKENS, W_LANES)
+        block = raw[lax.rem(first - b + LINES, LINES)]
         for j in range(PAIR):
             part = dot((pick == j).astype(BF16), block, NN, BF16)
             for i in range(SPLIT * j, min(SPLIT * (j + 1), ROWS)):
@@ -270,9 +269,21 @@
 def shards(queries, keys, values, out_weight, upstream, timestep):
     core = lax.axis_index("core").astype(jnp.int32)
     core_s, line_s = core.reshape(1), lax.axis_index("line").astype(jnp.int32).reshape(1)
+    first_block = (lax.axis_index("line") + lax.axis_index("x")) % LINES
+    first_s = first_block.astype(jnp.int32).reshape(1)
 
     def shift_line(x, s):
         return lax.ppermute(x, "line", [(d, (d + s) % LINES) for d in range(LINES)])
+
+    def step_line(x):
+        size = AXES["x"]
+        pairs = [
+            (((a + b) % LINES) * size + b, a * size + b) for a in range(LINES) for b in range(size)
+        ]
+        return lax.ppermute(x, ("line", "x"), pairs)
+
+    def shift_x(x, s):
+        return lax.ppermute(x, "x", [(d, (d + s) % LINES) for d in range(LINES)])
 
     def swap_core(x):
         return lax.ppermute(x, "core", [(0, 1), (1, 0)])
@@ -286,7 +297,7 @@
     sent = call(
         pack_kernel,
         [shape(SOURCES, PAIR, IN_LANES)],
-        (core_s, *flat, upstream.reshape(TOKENS, D)),
+        (core_s, out_weight, *flat, upstream.reshape(TOKENS, D)),
         scalars=1,
         far=4,
         far_out=True,
@@ -298,10 +309,7 @@
             pltpu.SemaphoreType.DMA((13,)),
         ],
     )
-    w_sent = call(repeat_kernel, [shape(W_PEERS, PAIR, W_LANES)], (out_weight,))
     slab = lax.all_to_all(sent, OTHERS, split_axis=0, concat_axis=0, tiled=True)
-    w_sent, _ = lax.optimization_barrier((w_sent, slab))
-    w_raw = lax.all_to_all(w_sent, ("line", *OTHERS), split_axis=0, concat_axis=0, tiled=True)
 
     probs, swap, mine = call(
         forward_kernel,
@@ -317,8 +325,15 @@
         scratch=[pltpu.VMEM((LINES, SOURCES, ROWS * COLS), BF16)],
     )
     sums = [pieces[0]] + [shift_line(pieces[s], s) for s in range(1, LINES)]
-    w_raw, _ = lax.optimization_barrier((w_raw, pieces[0]))
-    w_mine = call(weight_kernel, [shape(HD, HALF)], (w_raw,))
+    raw, _ = lax.optimization_barrier((step_line(slab[:, :, :W_LANES]), pieces[0]))
+    raws = [raw] + [shift_x(raw, s) for s in range(1, LINES)]
+    w_mine = call(
+        weight_kernel,
+        [shape(HD, HALF)],
+        (first_s, *raws),
+        scalars=1,
+        scratch=[pltpu.VMEM((LINES, TOKENS, W_LANES), BF16)],
+    )
     w_theirs = swap_core(w_mine)
     grads = call(
         backward_kernel, [shape(TOKENS, HD)] * 3, (gate, slab, probs, w_mine, w_theirs), flops=10**9

time: 139 us -> 142 us (1.022)
  starting transfers between devices: 41.6 us -> 50.3 us
  blocking collectives: 41.3 us -> 35.6 us
    ppermute x0 -> x4, starting transfers between devices: none -> 17.2 us  [the longest x3 16.5 us: shift_x(): return lax.ppermute(x, 'x', [(d, (d + s) % LINES) for d in range(LINES)])]
    all_to_all x1 -> x0, waiting for transfers between devices: 8.94 us -> none  [shards(): lax.all_to_all(w_sent, ('line', *OTHERS), split_axis=0, concat_axis=0, ti...]
    all_to_all x1 -> x0, starting transfers between devices: 8.42 us -> none  [shards(): lax.all_to_all(w_sent, ('line', *OTHERS), split_axis=0, concat_axis=0, ti...]
    all_to_all x1, blocking collectives: 41.3 us -> 35.6 us  [shards(): lax.all_to_all(back, OTHERS, split_axis=0, concat_axis=0, tiled=True)]
    ppermute x3, waiting for transfers between devices: 3.49 us -> 8.24 us  [shift_line(): return lax.ppermute(x, 'line', [(d, (d + s) % LINES) for d in range(LINES)])]
    all_to_all x1, waiting for transfers between devices: 27.1 us -> 31.7 us  [shards(): slab = lax.all_to_all(sent, OTHERS, split_axis=0, concat_axis=0, tiled=True)]
    pallas_call x9 -> x8, Pallas kernels: 13.1 us -> 13 us  [call(): pl.pallas_call(kernel, out_shape=outs[0] if single else outs, in_specs=sm...]
  transfers between devices with their start and end apart: 7 -> 10, of which waited for: 5 -> 4; matrix products, arithmetic and copies ran while one was open for 0% -> 0% of each run, Pallas kernels for 4% -> 2%
where the time goes in v7:
time: 142 us; the launch traced here: 141 us
  starting transfers between devices  50.3 us (35%)
  waiting for transfers between devices  40.6 us (29%)
  blocking collectives  35.6 us (25%)
  Pallas kernels  13 us (9%)
  between operations  1.54 us (1%)
    all_to_all x1, blocking collectives, shards(): lax.all_to_all(back, OTHERS, split_axis=0, concat_axis=0, tiled=True)  35.6 us
    all_to_all x1, waiting for transfers between devices, shards(): slab = lax.all_to_all(sent, OTHERS, split_axis=0, concat_axis=0, tiled=True)  31.7 us
    all_to_all x1, starting transfers between devices, shards(): slab = lax.all_to_all(sent, OTHERS, split_axis=0, concat_axis=0, tiled=True)  18.2 us
    ppermute x3, starting transfers between devices, shift_x(): return lax.ppermute(x, 'x', [(d, (d + s) % LINES) for d in range(LINES)])  16.5 us
    pallas_call x8, Pallas kernels, call(): pl.pallas_call(kernel, out_shape=outs[0] if single else outs, in_specs=sm...  13 us
    ppermute x3, starting transfers between devices, shift_line(): return lax.ppermute(x, 'line', [(d, (d + s) % LINES) for d in range(LINES)])  11.1 us
    ppermute x3, waiting for transfers between devices, shift_line(): return lax.ppermute(x, 'line', [(d, (d + s) % LINES) for d in range(LINES)])  8.24 us
    ppermute x2, starting transfers between devices, swap_core(): return lax.ppermute(x, 'core', [(0, 1), (1, 0)])  3.84 us
  transfers between devices with their start and end apart: 10, of which 4 were waited for; matrix products, arithmetic and copies ran while one was open for 0% of the time, Pallas kernels for 2%

profile of v7, /device:TPU:8, one launch (start us, length us, event | category | flops | bytes accessed | tf_op | source)
XLA Modules:
  0.0 141.3 jit_solution(44332696571173361)
XLA Ops:
  0.6 4.0 %shard_map.119 = bf16[64,2,3648]{2,1,0:T(2,128)(2,1)} custom-call(s32[1]{0:T(128)} %bitcast.core_ref, bf16[9,144]{1,0:T(8,128)(2,1)} %w_ref.1, bf16[576,128]{1,0:T(8,128)(2,1)} %bitcast.25, bf16[576,128]{1,0:T(8,128)(2,1)} %bitcast.26, bf16[576,128]{1,0:T(8,128)(2,1)} %bitcast.27, bf16[128,1152]{1,0:T(8,128)(2,1)} %bitcast.24), custom_call_target="tpu_custom_call" | custom-call | flops 100000000 | bytes 1673764 | tf_op jit(solution)/shard_map/pallas_call | solution.py:249
  4.7 0.0 copy-start
  4.7 0.0 copy-start.1
  4.7 18.2 %all-to-all-start = ((bf16[64,2,3648]{2,1,0:T(2,128)(2,1)}), bf16[64,2,3648]{2,1,0:T(2,128)(2,1)S(1)}, u32[]{:S(2)}, u32[]{:S(2)}) async-start(bf16[64,2,3648]{2,1,0:T(2,128)(2,1)} %shard_map.119), calls=%async_computation | async-start | bytes 1900544 | tf_op jit(solution)/shard_map/all_to_all | solution.py:312
  23.5 0.0 copy-done
  23.5 0.0 copy-done.1
  23.6 0.1 sine_add_fusion
  23.6 31.7 %all-to-all-done.x_ref = bf16[64,2,3648]{2,1,0:T(2,128)(2,1)S(1)} async-done(((bf16[64,2,3648]{2,1,0:T(2,128)(2,1)}), bf16[64,2,3648]{2,1,0:T(2,128)(2,1)S(1)}, u32[]{:S(2)}, u32[]{:S(2)}) %all-to-all-start) | async-done | bytes 933920 | tf_op jit(solution)/shard_map/all_to_all | solution.py:312
  55.3 1.3 shard_map.120
  56.6 1.9 %collective-permute-start.1 = (bf16[128,1152]{1,0:T(8,128)(2,1)S(1)}, bf16[128,1152]{1,0:T(8,128)(2,1)S(1)}, u32[]{:S(2)}, u32[]{:S(2)}) collective-permute-start(bf16[128,1152]{1,0:T(8,128)(2,1)S(1)} %get-tuple-element.21.swap_ref), channel_id=1, source_target_pairs={{0,64},{64,0},{1,65},{65,1},{2,66},{66,2},{3,67},{67,3},{4,68},{68... | collective-permute-start | bytes 884744 | tf_op jit(solution)/shard_map/ppermute | solution.py:289
  58.6 0.1 slice.4
  58.7 0.7 collective-permute-start
  59.4 0.7 collective-permute-done.1.got_ref
  60.1 0.9 shard_map.121
  61.0 0.0 collective-permute-done.own_ref
  61.0 9.9 %collective-permute-start.4 = (bf16[64,2,768]{2,1,0:T(2,128)(2,1)S(1)}, bf16[64,2,768]{2,1,0:T(2,128)(2,1)S(1)}, u32[]{:S(2)}, u32[]{:S(2)}) collective-permute-start(bf16[64,2,768]{2,1,0:T(2,128)(2,1)S(1)} %collective-permute-done.own_ref), channel_id=1, source_target_pairs={{0,48},{16,0},{32,16},{48,32},{1,49},{17,1},{33,17},{49,33},{2,50}... | collective-permute-start | bytes 589832 | tf_op jit(solution)/shard_map/ppermute | solution.py:286
  70.9 3.6 %collective-permute-start.3 = (bf16[64,2,768]{2,1,0:T(2,128)(2,1)S(1)}, bf16[64,2,768]{2,1,0:T(2,128)(2,1)S(1)}, u32[]{:S(2)}, u32[]{:S(2)}) collective-permute-start(bf16[64,2,768]{2,1,0:T(2,128)(2,1)S(1)} %collective-permute-done.own_ref), channel_id=1, source_target_pairs={{0,32},{16,48},{32,0},{48,16},{1,33},{17,49},{33,1},{49,17},{2,34}... | collective-permute-start | bytes 589832 | tf_op jit(solution)/shard_map/ppermute | solution.py:286
  74.5 3.1 %collective-permute-start.2 = (bf16[64,2,768]{2,1,0:T(2,128)(2,1)S(1)}, bf16[64,2,768]{2,1,0:T(2,128)(2,1)S(1)}, u32[]{:S(2)}, u32[]{:S(2)}) collective-permute-start(bf16[64,2,768]{2,1,0:T(2,128)(2,1)S(1)} %collective-permute-done.own_ref), channel_id=1, source_target_pairs={{0,16},{16,32},{32,48},{48,0},{1,17},{17,33},{33,49},{49,1},{2,18}... | collective-permute-start | bytes 589832 | tf_op jit(solution)/shard_map/ppermute | solution.py:286
  77.5 2.5 %collective-permute-start.6 = (bf16[64,1296]{1,0:T(8,128)(2,1)S(1)}, bf16[64,1296]{1,0:T(8,128)(2,1)}, u32[]{:S(2)}, u32[]{:S(2)}) collective-permute-start(bf16[64,1296]{1,0:T(8,128)(2,1)S(1)} %get-tuple-element.29), channel_id=1, source_target_pairs={{0,128},{128,256},{256,384},{384,0},{1,129},{129,257},{257,385},{3... | collective-permute-start | bytes 497672 | tf_op jit(solution)/shard_map/ppermute | solution.py:276
  80.1 6.2 %collective-permute-start.7 = (bf16[64,1296]{1,0:T(8,128)(2,1)S(1)}, bf16[64,1296]{1,0:T(8,128)(2,1)}, u32[]{:S(2)}, u32[]{:S(2)}) collective-permute-start(bf16[64,1296]{1,0:T(8,128)(2,1)S(1)} %get-tuple-element.30), channel_id=1, source_target_pairs={{0,256},{128,384},{256,0},{384,128},{1,257},{129,385},{257,1},{385... | collective-permute-start | bytes 497672 | tf_op jit(solution)/shard_map/ppermute | solution.py:276
  86.3 0.0 collective-permute-done.4.r3_ref
  86.3 2.4 %collective-permute-start.8 = (bf16[64,1296]{1,0:T(8,128)(2,1)S(1)}, bf16[64,1296]{1,0:T(8,128)(2,1)}, u32[]{:S(2)}, u32[]{:S(2)}) collective-permute-start(bf16[64,1296]{1,0:T(8,128)(2,1)S(1)} %get-tuple-element.31), channel_id=1, source_target_pairs={{0,384},{128,0},{256,128},{384,256},{1,385},{129,1},{257,129},{385... | collective-permute-start | bytes 497672 | tf_op jit(solution)/shard_map/ppermute | solution.py:276
  88.7 0.0 collective-permute-done.3.r2_ref
  88.7 0.0 collective-permute-done.2.r1_ref
  88.8 0.6 shard_map.122.wm_ref
  89.4 1.9 %collective-permute-start.5 = (bf16[576,576]{1,0:T(8,128)(2,1)S(1)}, bf16[576,576]{1,0:T(8,128)(2,1)S(1)}, u32[]{:S(2)}, u32[]{:S(2)}) collective-permute-start(bf16[576,576]{1,0:T(8,128)(2,1)S(1)} %shard_map.122.wm_ref), channel_id=1, source_target_pairs={{0,64},{64,0},{1,65},{65,1},{2,66},{66,2},{3,67},{67,3},{4,68},{68... | collective-permute-start | bytes 1990664 | tf_op jit(solution)/shard_map/ppermute | solution.py:289
  91.3 0.0 collective-permute-done.6.p1_ref
  91.3 5.4 %collective-permute-done.7.p2_ref = bf16[64,1296]{1,0:T(8,128)(2,1)} collective-permute-done((bf16[64,1296]{1,0:T(8,128)(2,1)S(1)}, bf16[64,1296]{1,0:T(8,128)(2,1)}, u32[]{:S(2)}, u32[]{:S(2)}) %collective-permute-start.7) | collective-permute-done | bytes 165920 | tf_op jit(solution)/shard_map/ppermute | solution.py:276
  96.7 2.9 %collective-permute-done.8.p3_ref = bf16[64,1296]{1,0:T(8,128)(2,1)} collective-permute-done((bf16[64,1296]{1,0:T(8,128)(2,1)S(1)}, bf16[64,1296]{1,0:T(8,128)(2,1)}, u32[]{:S(2)}, u32[]{:S(2)}) %collective-permute-start.8) | collective-permute-done | bytes 165920 | tf_op jit(solution)/shard_map/ppermute | solution.py:276
  99.6 1.4 %shard_map.124.sum_ref = bf16[128,720]{1,0:T(8,128)(2,1)S(1)} custom-call(bf16[64,1296]{1,0:T(8,128)(2,1)S(1)} %get-tuple-element.24.p0_ref, bf16[64,1296]{1,0:T(8,128)(2,1)} %collective-permute-done.6.p1_ref, bf16[64,1296]{1,0:T(8,128)(2,1)} %collective-permute-done.7.p2_ref, bf16[64,1296]{1,0:T(8,128)(2,1)} %collective-permute-done.8.p3_ref), custom_call_target="tpu_custom_call" | custom-call | flops 10000000000 | bytes 847872 | tf_op jit(solution)/shard_map/pallas_call | solution.py:249
  101.0 0.0 collective-permute-done.5.wt_ref
  101.0 2.5 %shard_map.123 = (bf16[128,576]{1,0:T(8,128)(2,1)S(1)}, bf16[128,576]{1,0:T(8,128)(2,1)S(1)}, bf16[128,576]{1,0:T(8,128)(2,1)S(1)}) custom-call(f32[1,1152]{1,0:T(1,128)S(1)} %reshape.47.gate_ref, bf16[64,2,3648]{2,1,0:T(2,128)(2,1)S(1)} %all-to-all-done.x_ref, f32[8,128,128]{2,1,0:T(8,128)S(1)} %get-tuple-element.22.probs_ref, ...), custom_call_target="tpu_custom_call" | custom-call | flops 1000000000 | bytes 3232256 | tf_op jit(solution)/shard_map/pallas_call | solution.py:249
  103.5 0.2 shard_map.125
  103.7 35.6 %all_to_all.10.z_ref = bf16[64,2,3024]{2,1,0:T(2,128)(2,1)S(1)} all-to-all(bf16[64,2,3024]{2,1,0:T(2,128)(2,1)S(1)} %shard_map.125), channel_id=1, replica_groups=mesh['line'=4,'core'=2,'x'=4,'y'=2,'z'=8] {'x','y','z'}, dimensions={0} | all-to-all | bytes 1548288 | tf_op jit(solution)/shard_map/all_to_all | solution.py:343
  139.3 2.0 %shard_map.126 = (bf16[128,1152]{1,0:T(8,128)(2,1)}, bf16[576,128]{1,0:T(8,128)(2,1)}, bf16[576,128]{1,0:T(8,128)(2,1)}, bf16[576,128]{1,0:T(8,128)(2,1)}, f32[9,144]{1,0:T(8,128)}) custom-call(s32[1]{0:T(128)} %bitcast.core_ref, f32[1,1152]{1,0:T(1,128)S(1)} %reshape.47.gate_ref, bf16[64,2,3024]{2,1,0:T(2,128)(2,1)S(1)} %all_to_all.10.z_ref, ...), custom_call_target="tpu_custom_call" | custom-call | flops 100000000 | bytes 2848324 | tf_op jit(solution)/shard_map/pallas_call | solution.py:249
  (1 shorter events, 0.0 us)
Async XLA Ops:
  4.7 18.9 %copy-start = (f32[1152]{0:T(1024)S(1)}, f32[1152]{0:T(1024)}, u32[]{:S(2)}) copy-start(f32[1152]{0:T(1024)} %constant.42.clone) | copy-start | bytes 13828
  4.7 18.9 %copy-start.1 = (f32[1152]{0:T(1024)S(1)}, f32[1152]{0:T(1024)}, u32[]{:S(2)}) copy-start(f32[1152]{0:T(1024)} %constant.41.clone) | copy-start | bytes 13828
  4.7 50.6 %all-to-all-start = ((bf16[64,2,3648]{2,1,0:T(2,128)(2,1)}), bf16[64,2,3648]{2,1,0:T(2,128)(2,1)S(1)}, u32[]{:S(2)}, u32[]{:S(2)}) async-start(bf16[64,2,3648]{2,1,0:T(2,128)(2,1)} %shard_map.119), calls=%async_computation | async-start | bytes 1900544 | tf_op jit(solution)/shard_map/all_to_all | solution.py:312
  56.6 3.5 %collective-permute-start.1 = (bf16[128,1152]{1,0:T(8,128)(2,1)S(1)}, bf16[128,1152]{1,0:T(8,128)(2,1)S(1)}, u32[]{:S(2)}, u32[]{:S(2)}) collective-permute-start(bf16[128,1152]{1,0:T(8,128)(2,1)S(1)} %get-tuple-element.21.swap_ref), channel_id=1, source_target_pairs={{0,64},{64,0},{1,65},{65,1},{2,66},{66,2},{3,67},{67,3},{4,68},{68... | collective-permute-start | bytes 884744 | tf_op jit(solution)/shard_map/ppermute | solution.py:289
  58.7 2.3 %collective-permute-start = (bf16[64,2,768]{2,1,0:T(2,128)(2,1)S(1)}, bf16[64,2,768]{2,1,0:T(2,128)(2,1)S(1)}, u32[]{:S(2)}, u32[]{:S(2)}) collective-permute-start(bf16[64,2,768]{2,1,0:T(2,128)(2,1)S(1)} %slice.4), channel_id=1, source_target_pairs={{0,0},{144,16},{288,32},{432,48},{128,128},{272,144},{416,160},{48... | collective-permute-start | bytes 589832 | tf_op jit(solution)/shard_map/ppermute | solution.py:283
  61.0 25.3 %collective-permute-start.4 = (bf16[64,2,768]{2,1,0:T(2,128)(2,1)S(1)}, bf16[64,2,768]{2,1,0:T(2,128)(2,1)S(1)}, u32[]{:S(2)}, u32[]{:S(2)}) collective-permute-start(bf16[64,2,768]{2,1,0:T(2,128)(2,1)S(1)} %collective-permute-done.own_ref), channel_id=1, source_target_pairs={{0,48},{16,0},{32,16},{48,32},{1,49},{17,1},{33,17},{49,33},{2,50}... | collective-permute-start | bytes 589832 | tf_op jit(solution)/shard_map/ppermute | solution.py:286
  70.9 17.8 %collective-permute-start.3 = (bf16[64,2,768]{2,1,0:T(2,128)(2,1)S(1)}, bf16[64,2,768]{2,1,0:T(2,128)(2,1)S(1)}, u32[]{:S(2)}, u32[]{:S(2)}) collective-permute-start(bf16[64,2,768]{2,1,0:T(2,128)(2,1)S(1)} %collective-permute-done.own_ref), channel_id=1, source_target_pairs={{0,32},{16,48},{32,0},{48,16},{1,33},{17,49},{33,1},{49,17},{2,34}... | collective-permute-start | bytes 589832 | tf_op jit(solution)/shard_map/ppermute | solution.py:286
  74.5 14.3 %collective-permute-start.2 = (bf16[64,2,768]{2,1,0:T(2,128)(2,1)S(1)}, bf16[64,2,768]{2,1,0:T(2,128)(2,1)S(1)}, u32[]{:S(2)}, u32[]{:S(2)}) collective-permute-start(bf16[64,2,768]{2,1,0:T(2,128)(2,1)S(1)} %collective-permute-done.own_ref), channel_id=1, source_target_pairs={{0,16},{16,32},{32,48},{48,0},{1,17},{17,33},{33,49},{49,1},{2,18}... | collective-permute-start | bytes 589832 | tf_op jit(solution)/shard_map/ppermute | solution.py:286
  77.5 13.8 %collective-permute-start.6 = (bf16[64,1296]{1,0:T(8,128)(2,1)S(1)}, bf16[64,1296]{1,0:T(8,128)(2,1)}, u32[]{:S(2)}, u32[]{:S(2)}) collective-permute-start(bf16[64,1296]{1,0:T(8,128)(2,1)S(1)} %get-tuple-element.29), channel_id=1, source_target_pairs={{0,128},{128,256},{256,384},{384,0},{1,129},{129,257},{257,385},{3... | collective-permute-start | bytes 497672 | tf_op jit(solution)/shard_map/ppermute | solution.py:276
  80.1 16.6 %collective-permute-start.7 = (bf16[64,1296]{1,0:T(8,128)(2,1)S(1)}, bf16[64,1296]{1,0:T(8,128)(2,1)}, u32[]{:S(2)}, u32[]{:S(2)}) collective-permute-start(bf16[64,1296]{1,0:T(8,128)(2,1)S(1)} %get-tuple-element.30), channel_id=1, source_target_pairs={{0,256},{128,384},{256,0},{384,128},{1,257},{129,385},{257,1},{385... | collective-permute-start | bytes 497672 | tf_op jit(solution)/shard_map/ppermute | solution.py:276
  86.3 13.2 %collective-permute-start.8 = (bf16[64,1296]{1,0:T(8,128)(2,1)S(1)}, bf16[64,1296]{1,0:T(8,128)(2,1)}, u32[]{:S(2)}, u32[]{:S(2)}) collective-permute-start(bf16[64,1296]{1,0:T(8,128)(2,1)S(1)} %get-tuple-element.31), channel_id=1, source_target_pairs={{0,384},{128,0},{256,128},{384,256},{1,385},{129,1},{257,129},{385... | collective-permute-start | bytes 497672 | tf_op jit(solution)/shard_map/ppermute | solution.py:276
  89.4 11.6 %collective-permute-start.5 = (bf16[576,576]{1,0:T(8,128)(2,1)S(1)}, bf16[576,576]{1,0:T(8,128)(2,1)S(1)}, u32[]{:S(2)}, u32[]{:S(2)}) collective-permute-start(bf16[576,576]{1,0:T(8,128)(2,1)S(1)} %shard_map.122.wm_ref), channel_id=1, source_target_pairs={{0,64},{64,0},{1,65},{65,1},{2,66},{66,2},{3,67},{67,3},{4,68},{68... | collective-permute-start | bytes 1990664 | tf_op jit(solution)/shard_map/ppermute | solution.py:289

commit v8 on v6

--- a/solution.py
+++ b/solution.py
@@ -31,7 +31,7 @@
 AT_K = AT_Q + HD
 AT_V = AT_K + HD
 IN_LANES = AT_V + HD
-AT_G = 4 * HD
+AT_G = 3 * HD
 OUT_LANES = AT_G + SPLIT * COLS
 
 
@@ -61,7 +61,8 @@
     return x.reshape(SOURCES, PAIR, x.shape[-1])
 
 
-def repeat_kernel(line_ref, w0, w1, w2, w3, x_ref, slots):
+def repeat_kernel(line_ref, swap_ref, w0, w1, w2, w3, x_ref, slots):
+    x_ref[:, :, :HD] = spread(swap_ref[:, :HD])
     for s, ref in enumerate((w0, w1, w2, w3)):
         slots[s, :ROWS, :] = ref[...].astype(F32)
     line = line_ref[0]
@@ -72,7 +73,7 @@
     top = jnp.concatenate(rows[:mid] + [rows[mid][:, : HALF // 2]], axis=1)
     low = jnp.concatenate([rows[mid][:, HALF // 2 :]] + rows[mid + 1 :], axis=1)
     odd = (iota((TOKENS, W_LANES), 0) & 1) == 1
-    x_ref[...] = spread(jnp.where(odd, low, top).astype(BF16))
+    x_ref[:, :, HD:] = spread(jnp.where(odd, low, top).astype(BF16))
 
 
 def pack_kernel(core_ref, q_ref, k_ref, v_ref, u_ref, x_ref, feats, up, packed, sems):
@@ -120,7 +121,7 @@
 
 def weight_kernel(raw_ref, w_ref):
     pick = iota((SOURCES, TOKENS), 1) - PAIR * iota((SOURCES, TOKENS), 0)
-    raw = raw_ref[...].reshape(TOKENS, W_LANES)
+    raw = rows_of(raw_ref, HD, W_LANES)
     top = dot((pick == 0).astype(BF16), raw, NN, BF16)
     low = dot((pick == 1).astype(BF16), raw, NN, BF16)
     mid, part = ROWS // 2, HALF // 2
@@ -212,17 +213,14 @@
     o_ref[...] = mixed.astype(BF16)
 
 
-def back_kernel(swap_ref, dq_ref, dk_ref, dv_ref, sum_ref, x_ref):
-    x_ref[:, :, :HD] = spread(swap_ref[:, :HD])
+def back_kernel(dq_ref, dk_ref, dv_ref, sum_ref, x_ref):
     for n, ref in enumerate((dq_ref, dk_ref, dv_ref)):
-        x_ref[:, :, (n + 1) * HD : (n + 2) * HD] = spread(ref[...])
+        x_ref[:, :, n * HD : (n + 1) * HD] = spread(ref[...])
     x_ref[:, :, AT_G:OUT_LANES] = spread(sum_ref[...])
 
 
-def final_kernel(
-    core_ref, gate_ref, z_ref, wm_ref, wt_ref, out_ref, dq_ref, dk_ref, dv_ref, wg_ref
-):
-    att = rows_of(z_ref, 0, HD)
+def output_kernel(core_ref, gate_ref, raw_ref, wm_ref, wt_ref, out_ref):
+    att = rows_of(raw_ref, 0, HD)
     gate = gate_ref[...]
     mine = (gate[:, :HALF] * dot(att, wm_ref[...], NN)).astype(BF16)
     theirs = (gate[:, HALF:] * dot(att, wt_ref[...], NN)).astype(BF16)
@@ -233,9 +231,12 @@
         b = theirs[:, line * COLS : (line + 1) * COLS]
         parts += [jnp.where(first, a, b), jnp.where(first, b, a)]
     out_ref[...] = jnp.concatenate(parts, axis=1)
+
+
+def final_kernel(z_ref, dq_ref, dk_ref, dv_ref, wg_ref):
     order = order_matrix()
     for n, ref in enumerate((dq_ref, dk_ref, dv_ref)):
-        ref[...] = dot(order, rows_of(z_ref, (n + 1) * HD, HD), NT, BF16)
+        ref[...] = dot(order, rows_of(z_ref, n * HD, HD), NT, BF16)
     pick = ((iota((8, TOKENS), 1) & 1) == iota((8, TOKENS), 0)).astype(BF16)
     sums = dot(pick, rows_of(z_ref, AT_G, SPLIT * COLS), NN)
     for i in range(ROWS):
@@ -313,8 +314,8 @@
     *late, _ = lax.optimization_barrier((*weights, swap))
     w_sent = call(
         repeat_kernel,
-        [shape(SOURCES, PAIR, W_LANES)],
-        (line_s, *late),
+        [shape(SOURCES, PAIR, HD + W_LANES)],
+        (line_s, swap, *late),
         scalars=1,
         scratch=[pltpu.VMEM((LINES, 16, COLS), F32)],
     )
@@ -334,13 +335,13 @@
         backward_kernel, [shape(TOKENS, HD)] * 3, (gate, slab, probs, w_mine, w_theirs), flops=10**9
     )
     total = call(sum_kernel, [shape(TOKENS, SPLIT * COLS)], sums, flops=10**10)
-    back = call(back_kernel, [shape(SOURCES, PAIR, OUT_LANES)], (swap, *grads, total))
+    back = call(back_kernel, [shape(SOURCES, PAIR, OUT_LANES)], (*grads, total))
     frame = lax.all_to_all(back, OTHERS, split_axis=0, concat_axis=0, tiled=True)
-    output, dq, dk, dv, weight_grad = call(
-        final_kernel,
-        [shape(TOKENS, D)] + [shape(HD, TOKENS)] * 3 + [shape(ROWS, COLS, kind=F32)],
-        (core_s, gate, frame, w_mine, w_theirs),
-        scalars=1,
+    output = call(
+        output_kernel, [shape(TOKENS, D)], (core_s, gate, w_raw, w_mine, w_theirs), scalars=1
+    )
+    dq, dk, dv, weight_grad = call(
+        final_kernel, [shape(HD, TOKENS)] * 3 + [shape(ROWS, COLS, kind=F32)], (frame,)
     )
     dims = queries.shape
     return (output.reshape(upstream.shape), *(x.T.reshape(dims) for x in (dq, dk, dv)), weight_grad)

time: 139 us -> 140 us (level)
  blocking collectives: 40.8 us -> 0 us
  waiting for transfers between devices: 37.5 us -> 64.1 us
  starting transfers between devices: 45.1 us -> 57.4 us
  Pallas kernels: 13.2 us -> 16.1 us
    all_to_all x1 -> x0, blocking collectives: 40.8 us -> none  [shards(): lax.all_to_all(back, OTHERS, split_axis=0, concat_axis=0, tiled=True)]
    all_to_all x0 -> x1, waiting for transfers between devices: none -> 24.8 us  [shards(): lax.all_to_all(back, OTHERS, split_axis=0, concat_axis=0, tiled=True)]
    all_to_all x0 -> x1, starting transfers between devices: none -> 12.2 us  [shards(): lax.all_to_all(back, OTHERS, split_axis=0, concat_axis=0, tiled=True)]
    pallas_call x9 -> x10, Pallas kernels: 13.2 us -> 16.1 us  [call(): pl.pallas_call(kernel, out_shape=outs[0] if single else outs, in_specs=sm...]
    all_to_all x1, waiting for transfers between devices: 17 us -> 18.9 us  [shards(): lax.all_to_all(w_sent, OTHERS, split_axis=0, concat_axis=0, tiled=True)]
  transfers between devices with their start and end apart: 10 -> 11, of which waited for: 4 -> 5; matrix products, arithmetic and copies ran while one was open for 0% -> 0% of each run, Pallas kernels for 3% -> 5%
where the time goes in v8:
time: 140 us; the launch traced here: 139 us
  waiting for transfers between devices  64.1 us (46%)
  starting transfers between devices  57.4 us (41%)
  Pallas kernels  16.1 us (12%)
  between operations  1.55 us (1%)
    all_to_all x1, waiting for transfers between devices, shards(): lax.all_to_all(back, OTHERS, split_axis=0, concat_axis=0, tiled=True)  24.8 us
    all_to_all x1, waiting for transfers between devices, shards(): lax.all_to_all(w_sent, OTHERS, split_axis=0, concat_axis=0, tiled=True)  18.9 us
    ppermute x6, starting transfers between devices, shift_line(): return lax.ppermute(x, 'line', [(d, (d + s) % LINES) for d in range(LINES)])  18.3 us
    all_to_all x1, starting transfers between devices, shards(): slab = lax.all_to_all(sent, OTHERS, split_axis=0, concat_axis=0, tiled=True)  18.2 us
    all_to_all x1, waiting for transfers between devices, shards(): slab = lax.all_to_all(sent, OTHERS, split_axis=0, concat_axis=0, tiled=True)  18.1 us
    pallas_call x10, Pallas kernels, call(): pl.pallas_call(kernel, out_shape=outs[0] if single else outs, in_specs=sm...  16.1 us
    all_to_all x1, starting transfers between devices, shards(): lax.all_to_all(back, OTHERS, split_axis=0, concat_axis=0, tiled=True)  12.2 us
    all_to_all x1, starting transfers between devices, shards(): lax.all_to_all(w_sent, OTHERS, split_axis=0, concat_axis=0, tiled=True)  4.77 us
  transfers between devices with their start and end apart: 11, of which 5 were waited for; matrix products, arithmetic and copies ran while one was open for 0% of the time, Pallas kernels for 5%

profile of v8, /device:TPU:8, one launch (start us, length us, event | category | flops | bytes accessed | tf_op | source)
XLA Modules:
  0.0 139.3 jit_solution(13491610998501121063)
XLA Ops:
  0.6 3.4 %shard_map.119 = bf16[64,2,2880]{2,1,0:T(2,128)(2,1)} custom-call(s32[1]{0:T(128)} %bitcast.core_ref, bf16[576,128]{1,0:T(8,128)(2,1)} %bitcast.25, bf16[576,128]{1,0:T(8,128)(2,1)} %bitcast.26, bf16[576,128]{1,0:T(8,128)(2,1)} %bitcast.27, bf16[128,1152]{1,0:T(8,128)(2,1)} %bitcast.24), custom_call_target="tpu_custom_call" | custom-call | flops 100000000 | bytes 1474564 | tf_op jit(solution)/shard_map/pallas_call | solution.py:254
  4.0 0.0 copy-start
  4.0 0.0 copy-start.4
  4.0 18.2 %all-to-all-start = ((bf16[64,2,2880]{2,1,0:T(2,128)(2,1)}), bf16[64,2,2880]{2,1,0:T(2,128)(2,1)S(1)}, u32[]{:S(2)}, u32[]{:S(2)}) async-start(bf16[64,2,2880]{2,1,0:T(2,128)(2,1)} %shard_map.119), calls=%async_computation | async-start | bytes 1507328 | tf_op jit(solution)/shard_map/all_to_all | solution.py:307
  22.2 0.0 copy-done
  22.2 0.0 copy-start.3
  22.2 3.3 %collective-permute-start.2 = (bf16[9,144]{1,0:T(8,128)(2,1)S(1)}, bf16[9,144]{1,0:T(8,128)(2,1)S(1)}, u32[]{:S(2)}, u32[]{:S(2)}) collective-permute-start(bf16[9,144]{1,0:T(8,128)(2,1)S(1)} %copy-done), channel_id=1, source_target_pairs={{0,384},{128,0},{256,128},{384,256},{1,385},{129,1},{257,129},{385... | collective-permute-start | bytes 7784 | tf_op jit(solution)/shard_map/ppermute | solution.py:279
  25.5 2.7 %collective-permute-start.1 = (bf16[9,144]{1,0:T(8,128)(2,1)S(1)}, bf16[9,144]{1,0:T(8,128)(2,1)S(1)}, u32[]{:S(2)}, u32[]{:S(2)}) collective-permute-start(bf16[9,144]{1,0:T(8,128)(2,1)S(1)} %copy-done), channel_id=1, source_target_pairs={{0,256},{128,384},{256,0},{384,128},{1,257},{129,385},{257,1},{385... | collective-permute-start | bytes 7784 | tf_op jit(solution)/shard_map/ppermute | solution.py:279
  28.2 3.5 %collective-permute-start = (bf16[9,144]{1,0:T(8,128)(2,1)S(1)}, bf16[9,144]{1,0:T(8,128)(2,1)S(1)}, u32[]{:S(2)}, u32[]{:S(2)}) collective-permute-start(bf16[9,144]{1,0:T(8,128)(2,1)S(1)} %copy-done), channel_id=1, source_target_pairs={{0,128},{128,256},{256,384},{384,0},{1,129},{129,257},{257,385},{3... | collective-permute-start | bytes 7784 | tf_op jit(solution)/shard_map/ppermute | solution.py:279
  32.4 0.0 copy-done.4
  32.4 0.0 copy-done.3
  32.4 0.1 sine_add_fusion
  32.5 18.1 %all-to-all-done.x_ref = bf16[64,2,2880]{2,1,0:T(2,128)(2,1)S(1)} async-done(((bf16[64,2,2880]{2,1,0:T(2,128)(2,1)}), bf16[64,2,2880]{2,1,0:T(2,128)(2,1)S(1)}, u32[]{:S(2)}, u32[]{:S(2)}) %all-to-all-start) | async-done | bytes 737312 | tf_op jit(solution)/shard_map/all_to_all | solution.py:307
  50.5 1.3 shard_map.120
  51.9 0.0 copy-start.1
  51.9 0.0 collective-permute-done.2.w3
  51.9 0.0 collective-permute-done.1.w2
  51.9 0.0 collective-permute-done.w1
  51.9 1.4 shard_map.121
  53.3 0.0 copy-done.1
  53.3 4.8 %all-to-all-start.1 = ((bf16[64,2,3168]{2,1,0:T(2,128)(2,1)}), bf16[64,2,3168]{2,1,0:T(2,128)(2,1)S(1)}, u32[]{:S(2)}, u32[]{:S(2)}) async-start(bf16[64,2,3168]{2,1,0:T(2,128)(2,1)} %shard_map.121), calls=%async_computation.1 | async-start | bytes 1638400 | tf_op jit(solution)/shard_map/all_to_all | solution.py:322
  58.1 1.9 %collective-permute-start.3 = (bf16[128,1152]{1,0:T(8,128)(2,1)S(1)}, bf16[128,1152]{1,0:T(8,128)(2,1)S(1)}, u32[]{:S(2)}, u32[]{:S(2)}) collective-permute-start(bf16[128,1152]{1,0:T(8,128)(2,1)S(1)} %get-tuple-element.25.swap_ref), channel_id=1, source_target_pairs={{0,64},{64,0},{1,65},{65,1},{2,66},{66,2},{3,67},{67,3},{4,68},{68... | collective-permute-start | bytes 884744 | tf_op jit(solution)/shard_map/ppermute | solution.py:282
  60.0 1.5 %collective-permute-done.3.got_ref = bf16[128,1152]{1,0:T(8,128)(2,1)S(1)} collective-permute-done((bf16[128,1152]{1,0:T(8,128)(2,1)S(1)}, bf16[128,1152]{1,0:T(8,128)(2,1)S(1)}, u32[]{:S(2)}, u32[]{:S(2)}) %collective-permute-start.3) | collective-permute-done | bytes 294944 | tf_op jit(solution)/shard_map/ppermute | solution.py:282
  61.6 1.6 %shard_map.122 = (bf16[64,1296]{1,0:T(8,128)(2,1)S(1)}, bf16[64,1296]{1,0:T(8,128)(2,1)}, bf16[64,1296]{1,0:T(8,128)(2,1)}, bf16[64,1296]{1,0:T(8,128)(2,1)S(1)}) custom-call(s32[1]{0:T(128)} %bitcast.2.line_ref, bf16[128,1152]{1,0:T(8,128)(2,1)S(1)} %get-tuple-element.25.swap_ref, bf16[128,1152]{1,0:T(8,128)(2,1)S(1)} %collective-permute-done.3.got_ref, ...), custom_call_target="tpu_custom_call" | custom-call | flops 100000000 | bytes 1400836 | tf_op jit(solution)/shard_map/pallas_call | solution.py:254
  63.2 2.6 %collective-permute-start.5 = (bf16[64,1296]{1,0:T(8,128)(2,1)}, bf16[64,1296]{1,0:T(8,128)(2,1)}, u32[]{:S(2)}, u32[]{:S(2)}) collective-permute-start(bf16[64,1296]{1,0:T(8,128)(2,1)} %get-tuple-element.38), channel_id=1, source_target_pairs={{0,128},{128,256},{256,384},{384,0},{1,129},{129,257},{257,385},{3... | collective-permute-start | bytes 497672 | tf_op jit(solution)/shard_map/ppermute | solution.py:279
  65.8 4.4 %collective-permute-start.6 = (bf16[64,1296]{1,0:T(8,128)(2,1)}, bf16[64,1296]{1,0:T(8,128)(2,1)}, u32[]{:S(2)}, u32[]{:S(2)}) collective-permute-start(bf16[64,1296]{1,0:T(8,128)(2,1)} %get-tuple-element.39), channel_id=1, source_target_pairs={{0,256},{128,384},{256,0},{384,128},{1,257},{129,385},{257,1},{385... | collective-permute-start | bytes 497672 | tf_op jit(solution)/shard_map/ppermute | solution.py:279
  70.2 1.9 %collective-permute-start.7 = (bf16[64,1296]{1,0:T(8,128)(2,1)S(1)}, bf16[64,1296]{1,0:T(8,128)(2,1)}, u32[]{:S(2)}, u32[]{:S(2)}) collective-permute-start(bf16[64,1296]{1,0:T(8,128)(2,1)S(1)} %get-tuple-element.40), channel_id=1, source_target_pairs={{0,384},{128,0},{256,128},{384,256},{1,385},{129,1},{257,129},{385... | collective-permute-start | bytes 497672 | tf_op jit(solution)/shard_map/ppermute | solution.py:279
  72.1 18.9 %all-to-all-done.1.raw_ref = bf16[64,2,3168]{2,1,0:T(2,128)(2,1)S(1)} async-done(((bf16[64,2,3168]{2,1,0:T(2,128)(2,1)}), bf16[64,2,3168]{2,1,0:T(2,128)(2,1)S(1)}, u32[]{:S(2)}, u32[]{:S(2)}) %all-to-all-start.1) | async-done | bytes 811040 | tf_op jit(solution)/shard_map/all_to_all | solution.py:322
  91.0 0.6 shard_map.123.wm_ref
  91.7 0.0 copy-start.2
  91.7 2.1 %collective-permute-start.4 = (bf16[576,576]{1,0:T(8,128)(2,1)S(1)}, bf16[576,576]{1,0:T(8,128)(2,1)S(1)}, u32[]{:S(2)}, u32[]{:S(2)}) collective-permute-start(bf16[576,576]{1,0:T(8,128)(2,1)S(1)} %shard_map.123.wm_ref), channel_id=1, source_target_pairs={{0,64},{64,0},{1,65},{65,1},{2,66},{66,2},{3,67},{67,3},{4,68},{68... | collective-permute-start | bytes 1990664 | tf_op jit(solution)/shard_map/ppermute | solution.py:282
  93.7 0.0 collective-permute-done.5.p1_ref
  93.7 0.0 collective-permute-done.6.p2_ref
  93.7 0.0 collective-permute-done.7.p3_ref
  93.8 1.4 %shard_map.126.sum_ref = bf16[128,720]{1,0:T(8,128)(2,1)S(1)} custom-call(bf16[64,1296]{1,0:T(8,128)(2,1)S(1)} %get-tuple-element.32.p0_ref, bf16[64,1296]{1,0:T(8,128)(2,1)} %collective-permute-done.5.p1_ref, bf16[64,1296]{1,0:T(8,128)(2,1)} %collective-permute-done.6.p2_ref, bf16[64,1296]{1,0:T(8,128)(2,1)} %collective-permute-done.7.p3_ref), custom_call_target="tpu_custom_call" | custom-call | flops 10000000000 | bytes 847872 | tf_op jit(solution)/shard_map/pallas_call | solution.py:254
  95.2 0.7 collective-permute-done.4.wt_ref
  95.9 0.0 copy-done.2
  95.9 2.4 %shard_map.125 = (bf16[128,576]{1,0:T(8,128)(2,1)S(1)}, bf16[128,576]{1,0:T(8,128)(2,1)S(1)}, bf16[128,576]{1,0:T(8,128)(2,1)S(1)}) custom-call(f32[1,1152]{1,0:T(1,128)S(1)} %reshape.44.gate_ref, bf16[64,2,2880]{2,1,0:T(2,128)(2,1)S(1)} %all-to-all-done.x_ref, f32[8,128,128]{2,1,0:T(8,128)S(1)} %copy-done.2, bf16[576,576]{1,0:T(8,128)(2,1)S(1)} %shard_map.123.wm_ref, ...), custom_call_target="tpu_custom_call" | custom-call | flops 1000000000 | bytes 3035648 | tf_op jit(solution)/shard_map/pallas_call | solution.py:254
  98.3 1.1 shard_map.127
  99.4 12.2 %all-to-all-start.2 = ((bf16[64,2,2448]{2,1,0:T(2,128)(2,1)}), bf16[64,2,2448]{2,1,0:T(2,128)(2,1)S(1)}, u32[]{:S(2)}, u32[]{:S(2)}) async-start(bf16[64,2,2448]{2,1,0:T(2,128)(2,1)} %shard_map.127), calls=%async_computation.2 | async-start | bytes 1310720 | tf_op jit(solution)/shard_map/all_to_all | solution.py:339
  111.6 1.4 %shard_map.124 = bf16[128,1152]{1,0:T(8,128)(2,1)} custom-call(s32[1]{0:T(128)} %bitcast.core_ref, f32[1,1152]{1,0:T(1,128)S(1)} %reshape.44.gate_ref, bf16[64,2,3168]{2,1,0:T(2,128)(2,1)S(1)} %all-to-all-done.1.raw_ref, bf16[576,576]{1,0:T(8,128)(2,1)S(1)} %shard_map.123.wm_ref, bf16[576,576]{1,0:T(8,128)(2,1)S(1)} %collective-permute-done.4.wt_ref), custom_call_target="tpu_custom_call" | custom-call | flops 100000000 | bytes 2437636 | tf_op jit(solution)/shard_map/pallas_call | solution.py:254
  113.0 24.8 %all-to-all-done.2.z_ref = bf16[64,2,2448]{2,1,0:T(2,128)(2,1)S(1)} async-done(((bf16[64,2,2448]{2,1,0:T(2,128)(2,1)}), bf16[64,2,2448]{2,1,0:T(2,128)(2,1)S(1)}, u32[]{:S(2)}, u32[]{:S(2)}) %all-to-all-start.2) | async-done | bytes 626720 | tf_op jit(solution)/shard_map/all_to_all | solution.py:339
  137.9 1.5 %shard_map.128 = (bf16[576,128]{1,0:T(8,128)(2,1)}, bf16[576,128]{1,0:T(8,128)(2,1)}, bf16[576,128]{1,0:T(8,128)(2,1)}, f32[9,144]{1,0:T(8,128)}) custom-call(bf16[64,2,2448]{2,1,0:T(2,128)(2,1)S(1)} %all-to-all-done.2.z_ref), custom_call_target="tpu_custom_call" | custom-call | flops 100000000 | bytes 1074240 | tf_op jit(solution)/shard_map/pallas_call | solution.py:254
  (1 shorter events, 0.0 us)
Async XLA Ops:
  4.0 18.2 %copy-start = (bf16[9,144]{1,0:T(8,128)(2,1)S(1)}, bf16[9,144]{1,0:T(8,128)(2,1)}, u32[]{:S(2)}) copy-start(bf16[9,144]{1,0:T(8,128)(2,1)} %w0) | copy-start | bytes 7780
  4.0 28.3 %copy-start.4 = (f32[1152]{0:T(1024)S(1)}, f32[1152]{0:T(1024)}, u32[]{:S(2)}) copy-start(f32[1152]{0:T(1024)} %constant.25.clone) | copy-start | bytes 13828
  4.0 46.5 %all-to-all-start = ((bf16[64,2,2880]{2,1,0:T(2,128)(2,1)}), bf16[64,2,2880]{2,1,0:T(2,128)(2,1)S(1)}, u32[]{:S(2)}, u32[]{:S(2)}) async-start(bf16[64,2,2880]{2,1,0:T(2,128)(2,1)} %shard_map.119), calls=%async_computation | async-start | bytes 1507328 | tf_op jit(solution)/shard_map/all_to_all | solution.py:307
  22.2 10.1 %copy-start.3 = (f32[1152]{0:T(1024)S(1)}, f32[1152]{0:T(1024)}, u32[]{:S(2)}) copy-start(f32[1152]{0:T(1024)} %constant.26.clone) | copy-start | bytes 13828
  22.2 29.7 %collective-permute-start.2 = (bf16[9,144]{1,0:T(8,128)(2,1)S(1)}, bf16[9,144]{1,0:T(8,128)(2,1)S(1)}, u32[]{:S(2)}, u32[]{:S(2)}) collective-permute-start(bf16[9,144]{1,0:T(8,128)(2,1)S(1)} %copy-done), channel_id=1, source_target_pairs={{0,384},{128,0},{256,128},{384,256},{1,385},{129,1},{257,129},{385... | collective-permute-start | bytes 7784 | tf_op jit(solution)/shard_map/ppermute | solution.py:279
  25.5 26.4 %collective-permute-start.1 = (bf16[9,144]{1,0:T(8,128)(2,1)S(1)}, bf16[9,144]{1,0:T(8,128)(2,1)S(1)}, u32[]{:S(2)}, u32[]{:S(2)}) collective-permute-start(bf16[9,144]{1,0:T(8,128)(2,1)S(1)} %copy-done), channel_id=1, source_target_pairs={{0,256},{128,384},{256,0},{384,128},{1,257},{129,385},{257,1},{385... | collective-permute-start | bytes 7784 | tf_op jit(solution)/shard_map/ppermute | solution.py:279
  28.2 23.7 %collective-permute-start = (bf16[9,144]{1,0:T(8,128)(2,1)S(1)}, bf16[9,144]{1,0:T(8,128)(2,1)S(1)}, u32[]{:S(2)}, u32[]{:S(2)}) collective-permute-start(bf16[9,144]{1,0:T(8,128)(2,1)S(1)} %copy-done), channel_id=1, source_target_pairs={{0,128},{128,256},{256,384},{384,0},{1,129},{129,257},{257,385},{3... | collective-permute-start | bytes 7784 | tf_op jit(solution)/shard_map/ppermute | solution.py:279
  51.9 1.4 %copy-start.1 = (f32[8,128,128]{2,1,0:T(8,128)}, f32[8,128,128]{2,1,0:T(8,128)S(1)}, u32[]{:S(2)}) copy-start(f32[8,128,128]{2,1,0:T(8,128)S(1)} %get-tuple-element.34.probs_ref) | copy-start | bytes 1572868
  53.3 37.7 %all-to-all-start.1 = ((bf16[64,2,3168]{2,1,0:T(2,128)(2,1)}), bf16[64,2,3168]{2,1,0:T(2,128)(2,1)S(1)}, u32[]{:S(2)}, u32[]{:S(2)}) async-start(bf16[64,2,3168]{2,1,0:T(2,128)(2,1)} %shard_map.121), calls=%async_computation.1 | async-start | bytes 1638400 | tf_op jit(solution)/shard_map/all_to_all | solution.py:322
  58.1 3.5 %collective-permute-start.3 = (bf16[128,1152]{1,0:T(8,128)(2,1)S(1)}, bf16[128,1152]{1,0:T(8,128)(2,1)S(1)}, u32[]{:S(2)}, u32[]{:S(2)}) collective-permute-start(bf16[128,1152]{1,0:T(8,128)(2,1)S(1)} %get-tuple-element.25.swap_ref), channel_id=1, source_target_pairs={{0,64},{64,0},{1,65},{65,1},{2,66},{66,2},{3,67},{67,3},{4,68},{68... | collective-permute-start | bytes 884744 | tf_op jit(solution)/shard_map/ppermute | solution.py:282
  63.2 30.5 %collective-permute-start.5 = (bf16[64,1296]{1,0:T(8,128)(2,1)}, bf16[64,1296]{1,0:T(8,128)(2,1)}, u32[]{:S(2)}, u32[]{:S(2)}) collective-permute-start(bf16[64,1296]{1,0:T(8,128)(2,1)} %get-tuple-element.38), channel_id=1, source_target_pairs={{0,128},{128,256},{256,384},{384,0},{1,129},{129,257},{257,385},{3... | collective-permute-start | bytes 497672 | tf_op jit(solution)/shard_map/ppermute | solution.py:279
  65.8 28.0 %collective-permute-start.6 = (bf16[64,1296]{1,0:T(8,128)(2,1)}, bf16[64,1296]{1,0:T(8,128)(2,1)}, u32[]{:S(2)}, u32[]{:S(2)}) collective-permute-start(bf16[64,1296]{1,0:T(8,128)(2,1)} %get-tuple-element.39), channel_id=1, source_target_pairs={{0,256},{128,384},{256,0},{384,128},{1,257},{129,385},{257,1},{385... | collective-permute-start | bytes 497672 | tf_op jit(solution)/shard_map/ppermute | solution.py:279
  70.2 23.6 %collective-permute-start.7 = (bf16[64,1296]{1,0:T(8,128)(2,1)S(1)}, bf16[64,1296]{1,0:T(8,128)(2,1)}, u32[]{:S(2)}, u32[]{:S(2)}) collective-permute-start(bf16[64,1296]{1,0:T(8,128)(2,1)S(1)} %get-tuple-element.40), channel_id=1, source_target_pairs={{0,384},{128,0},{256,128},{384,256},{1,385},{129,1},{257,129},{385... | collective-permute-start | bytes 497672 | tf_op jit(solution)/shard_map/ppermute | solution.py:279
  91.7 4.3 %copy-start.2 = (f32[8,128,128]{2,1,0:T(8,128)S(1)}, f32[8,128,128]{2,1,0:T(8,128)}, u32[]{:S(2)}) copy-start(f32[8,128,128]{2,1,0:T(8,128)} %copy-done.1) | copy-start | bytes 1572868
  91.7 4.2 %collective-permute-start.4 = (bf16[576,576]{1,0:T(8,128)(2,1)S(1)}, bf16[576,576]{1,0:T(8,128)(2,1)S(1)}, u32[]{:S(2)}, u32[]{:S(2)}) collective-permute-start(bf16[576,576]{1,0:T(8,128)(2,1)S(1)} %shard_map.123.wm_ref), channel_id=1, source_target_pairs={{0,64},{64,0},{1,65},{65,1},{2,66},{66,2},{3,67},{67,3},{4,68},{68... | collective-permute-start | bytes 1990664 | tf_op jit(solution)/shard_map/ppermute | solution.py:282
  99.4 38.4 %all-to-all-start.2 = ((bf16[64,2,2448]{2,1,0:T(2,128)(2,1)}), bf16[64,2,2448]{2,1,0:T(2,128)(2,1)S(1)}, u32[]{:S(2)}, u32[]{:S(2)}) async-start(bf16[64,2,2448]{2,1,0:T(2,128)(2,1)} %shard_map.127), calls=%async_computation.2 | async-start | bytes 1310720 | tf_op jit(solution)/shard_map/all_to_all | solution.py:339

commit v9 on v4

--- a/solution.py
+++ b/solution.py
@@ -177,7 +177,9 @@
         ref[...] = packed[lax.rem(line + s, LINES)]
 
 
-def backward_kernel(gate_ref, x_ref, probs_ref, wm_ref, wt_ref, dq_ref, dk_ref, dv_ref):
+def backward_kernel(gate_ref, x_ref, probs_ref, wm_ref, wt_ref, swap_ref, sum_ref, z_ref):
+    z_ref[:, :, :HD] = spread(swap_ref[:, :HD])
+    z_ref[:, :, AT_G:OUT_LANES] = spread(sum_ref[...])
     q, k, v = (rows_of(x_ref, at, HD) for at in (AT_Q, AT_K, AT_V))
     factor = 1.0 / jnp.sqrt(F32(HEAD))
     scaled = scale_upstream(x_ref, gate_ref)
@@ -197,9 +199,11 @@
         k_rows.append(k * mask)
     wide = jnp.concatenate(score_grads, axis=1)
     tall = jnp.concatenate(score_grads, axis=0)
-    dq_ref[...] = (dot(wide, jnp.concatenate(k_rows, axis=0), NN) * factor).astype(BF16)
-    dk_ref[...] = (dot(tall, jnp.concatenate(q_rows, axis=0), TN) * factor).astype(BF16)
-    dv_ref[...] = dot(jnp.concatenate(low, axis=0), jnp.concatenate(g_rows, axis=0), TN, BF16)
+    dq = (dot(wide, jnp.concatenate(k_rows, axis=0), NN) * factor).astype(BF16)
+    dk = (dot(tall, jnp.concatenate(q_rows, axis=0), TN) * factor).astype(BF16)
+    dv = dot(jnp.concatenate(low, axis=0), jnp.concatenate(g_rows, axis=0), TN, BF16)
+    for n, x in enumerate((dq, dk, dv)):
+        z_ref[:, :, (n + 1) * HD : (n + 2) * HD] = spread(x)
 
 
 def sum_kernel(p0_ref, p1_ref, p2_ref, p3_ref, o_ref):
@@ -210,13 +214,6 @@
     put = iota((TOKENS, SOURCES), 0) - PAIR * iota((TOKENS, SOURCES), 1)
     mixed = dot((put == 0).astype(BF16), total[:, :lanes], NN) + dot((put == 1).astype(BF16), low, NN)
     o_ref[...] = mixed.astype(BF16)
-
-
-def back_kernel(swap_ref, dq_ref, dk_ref, dv_ref, sum_ref, x_ref):
-    x_ref[:, :, :HD] = spread(swap_ref[:, :HD])
-    for n, ref in enumerate((dq_ref, dk_ref, dv_ref)):
-        x_ref[:, :, (n + 1) * HD : (n + 2) * HD] = spread(ref[...])
-    x_ref[:, :, AT_G:OUT_LANES] = spread(sum_ref[...])
 
 
 def final_kernel(
@@ -331,11 +328,13 @@
     w_raw, _ = lax.optimization_barrier((w_raw, pieces[0]))
     w_mine = call(weight_kernel, [shape(HD, HALF)], (w_raw,))
     w_theirs = swap_core(w_mine)
-    grads = call(
-        backward_kernel, [shape(TOKENS, HD)] * 3, (gate, slab, probs, w_mine, w_theirs), flops=10**9
-    )
     total = call(sum_kernel, [shape(TOKENS, SPLIT * COLS)], sums, flops=10**10)
-    back = call(back_kernel, [shape(SOURCES, PAIR, OUT_LANES)], (swap, *grads, total))
+    back = call(
+        backward_kernel,
+        [shape(SOURCES, PAIR, OUT_LANES)],
+        (gate, slab, probs, w_mine, w_theirs, swap, total),
+        flops=10**9,
+    )
     frame = lax.all_to_all(back, OTHERS, split_axis=0, concat_axis=0, tiled=True)
     output, dq, dk, dv, weight_grad = call(
         final_kernel,

time: 135 us -> 135 us (level)
    pallas_call x9 -> x8, Pallas kernels: 12.2 us -> 12.2 us  [call(): pl.pallas_call(kernel, out_shape=outs[0] if single else outs, in_specs=sm...]
where the time goes in v9:
time: 135 us
  starting transfers between devices  46.6 us (35%)
  blocking collectives  39.2 us (29%)
  waiting for transfers between devices  35 us (26%)
  Pallas kernels  12.2 us (9%)
  between operations  1.48 us (1%)
    all_to_all x1, blocking collectives, shards(): lax.all_to_all(back, OTHERS, split_axis=0, concat_axis=0, tiled=True)  39.2 us
    ppermute x6, starting transfers between devices, shift_line(): return lax.ppermute(x, 'line', [(d, (d + s) % LINES) for d in range(LINES)])  19.1 us
    all_to_all x1, starting transfers between devices, shards(): slab = lax.all_to_all(sent, OTHERS, split_axis=0, concat_axis=0, tiled=True)  18.2 us
    ppermute x6, waiting for transfers between devices, shift_line(): return lax.ppermute(x, 'line', [(d, (d + s) % LINES) for d in range(LINES)])  12.6 us
    pallas_call x8, Pallas kernels, call(): pl.pallas_call(kernel, out_shape=outs[0] if single else outs, in_specs=sm...  12.2 us
    all_to_all x1, waiting for transfers between devices, shards(): slab = lax.all_to_all(sent, OTHERS, split_axis=0, concat_axis=0, tiled=True)  10.7 us
    all_to_all x1, waiting for transfers between devices, shards(): lax.all_to_all(w_sent, OTHERS, split_axis=0, concat_axis=0, tiled=True)  10.1 us
    all_to_all x1, starting transfers between devices, shards(): lax.all_to_all(w_sent, OTHERS, split_axis=0, concat_axis=0, tiled=True)  5.5 us
  transfers between devices with their start and end apart: 10, of which 6 were waited for; matrix products, arithmetic and copies ran while one was open for 0% of the time, Pallas kernels for 3%

profile of v9, /device:TPU:8, one launch (start us, length us, event | category | flops | bytes accessed | tf_op | source)
XLA Modules:
  0.0 134.5 jit_solution(10853522154084162091)
XLA Ops:
  0.6 3.4 %shard_map.119 = bf16[64,2,2880]{2,1,0:T(2,128)(2,1)} custom-call(s32[1]{0:T(128)} %bitcast.core_ref, bf16[576,128]{1,0:T(8,128)(2,1)} %bitcast.24, bf16[576,128]{1,0:T(8,128)(2,1)} %bitcast.25, bf16[576,128]{1,0:T(8,128)(2,1)} %bitcast.26, bf16[128,1152]{1,0:T(8,128)(2,1)} %bitcast.23), custom_call_target="tpu_custom_call" | custom-call | flops 100000000 | bytes 1474564 | tf_op jit(solution)/shard_map/pallas_call | solution.py:250
  4.0 0.0 copy-start
  4.0 18.2 %all-to-all-start = ((bf16[64,2,2880]{2,1,0:T(2,128)(2,1)}), bf16[64,2,2880]{2,1,0:T(2,128)(2,1)S(1)}, u32[]{:S(2)}, u32[]{:S(2)}) async-start(bf16[64,2,2880]{2,1,0:T(2,128)(2,1)} %shard_map.119), calls=%async_computation | async-start | bytes 1507328 | tf_op jit(solution)/shard_map/all_to_all | solution.py:303
  22.2 0.0 copy-done
  22.2 3.2 %collective-permute-start.2 = (bf16[9,144]{1,0:T(8,128)(2,1)S(1)}, bf16[9,144]{1,0:T(8,128)(2,1)S(1)}, u32[]{:S(2)}, u32[]{:S(2)}) collective-permute-start(bf16[9,144]{1,0:T(8,128)(2,1)S(1)} %copy-done), channel_id=1, source_target_pairs={{0,384},{128,0},{256,128},{384,256},{1,385},{129,1},{257,129},{385... | collective-permute-start | bytes 7784 | tf_op jit(solution)/shard_map/ppermute | solution.py:275
  25.5 2.7 %collective-permute-start.1 = (bf16[9,144]{1,0:T(8,128)(2,1)S(1)}, bf16[9,144]{1,0:T(8,128)(2,1)S(1)}, u32[]{:S(2)}, u32[]{:S(2)}) collective-permute-start(bf16[9,144]{1,0:T(8,128)(2,1)S(1)} %copy-done), channel_id=1, source_target_pairs={{0,256},{128,384},{256,0},{384,128},{1,257},{129,385},{257,1},{385... | collective-permute-start | bytes 7784 | tf_op jit(solution)/shard_map/ppermute | solution.py:275
  28.2 3.5 %collective-permute-start = (bf16[9,144]{1,0:T(8,128)(2,1)S(1)}, bf16[9,144]{1,0:T(8,128)(2,1)S(1)}, u32[]{:S(2)}, u32[]{:S(2)}) collective-permute-start(bf16[9,144]{1,0:T(8,128)(2,1)S(1)} %copy-done), channel_id=1, source_target_pairs={{0,128},{128,256},{256,384},{384,0},{1,129},{129,257},{257,385},{3... | collective-permute-start | bytes 7784 | tf_op jit(solution)/shard_map/ppermute | solution.py:275
  31.7 6.9 %collective-permute-done.2.w3 = bf16[9,144]{1,0:T(8,128)(2,1)S(1)} collective-permute-done((bf16[9,144]{1,0:T(8,128)(2,1)S(1)}, bf16[9,144]{1,0:T(8,128)(2,1)S(1)}, u32[]{:S(2)}, u32[]{:S(2)}) %collective-permute-start.2) | collective-permute-done | bytes 2624 | tf_op jit(solution)/shard_map/ppermute | solution.py:275
  38.5 0.0 collective-permute-done.1.w2
  38.5 0.0 collective-permute-done.w1
  38.5 1.2 shard_map.121
  39.8 10.7 %all-to-all-done.x_ref = bf16[64,2,2880]{2,1,0:T(2,128)(2,1)S(1)} async-done(((bf16[64,2,2880]{2,1,0:T(2,128)(2,1)}), bf16[64,2,2880]{2,1,0:T(2,128)(2,1)S(1)}, u32[]{:S(2)}, u32[]{:S(2)}) %all-to-all-start) | async-done | bytes 737312 | tf_op jit(solution)/shard_map/all_to_all | solution.py:303
  50.5 0.0 copy-start.1
  50.5 0.0 copy-start.2
  50.5 5.5 %all-to-all-start.1 = ((bf16[64,2,2592]{2,1,0:T(2,128)(2,1)}), bf16[64,2,2592]{2,1,0:T(2,128)(2,1)S(1)}, u32[]{:S(2)}, u32[]{:S(2)}) async-start(bf16[64,2,2592]{2,1,0:T(2,128)(2,1)} %shard_map.121), calls=%async_computation.1 | async-start | bytes 1376256 | tf_op jit(solution)/shard_map/all_to_all | solution.py:312
  56.7 0.0 copy-done.1
  56.7 0.0 copy-done.2
  56.7 0.1 sine_add_fusion
  56.8 1.3 shard_map.120
  58.1 1.9 %collective-permute-start.3 = (bf16[128,1152]{1,0:T(8,128)(2,1)S(1)}, bf16[128,1152]{1,0:T(8,128)(2,1)S(1)}, u32[]{:S(2)}, u32[]{:S(2)}) collective-permute-start(bf16[128,1152]{1,0:T(8,128)(2,1)S(1)} %get-tuple-element.23.swap_ref), channel_id=1, source_target_pairs={{0,64},{64,0},{1,65},{65,1},{2,66},{66,2},{3,67},{67,3},{4,68},{68... | collective-permute-start | bytes 884744 | tf_op jit(solution)/shard_map/ppermute | solution.py:278
  60.0 1.5 %collective-permute-done.3.got_ref = bf16[128,1152]{1,0:T(8,128)(2,1)S(1)} collective-permute-done((bf16[128,1152]{1,0:T(8,128)(2,1)S(1)}, bf16[128,1152]{1,0:T(8,128)(2,1)S(1)}, u32[]{:S(2)}, u32[]{:S(2)}) %collective-permute-start.3) | collective-permute-done | bytes 294944 | tf_op jit(solution)/shard_map/ppermute | solution.py:278
  61.6 0.9 shard_map.122
  62.5 2.7 %collective-permute-start.5 = (bf16[64,1296]{1,0:T(8,128)(2,1)S(1)}, bf16[64,1296]{1,0:T(8,128)(2,1)S(1)}, u32[]{:S(2)}, u32[]{:S(2)}) collective-permute-start(bf16[64,1296]{1,0:T(8,128)(2,1)S(1)} %get-tuple-element.27), channel_id=1, source_target_pairs={{0,128},{128,256},{256,384},{384,0},{1,129},{129,257},{257,385},{3... | collective-permute-start | bytes 497672 | tf_op jit(solution)/shard_map/ppermute | solution.py:275
  65.2 5.0 %collective-permute-start.6 = (bf16[64,1296]{1,0:T(8,128)(2,1)S(1)}, bf16[64,1296]{1,0:T(8,128)(2,1)S(1)}, u32[]{:S(2)}, u32[]{:S(2)}) collective-permute-start(bf16[64,1296]{1,0:T(8,128)(2,1)S(1)} %get-tuple-element.28), channel_id=1, source_target_pairs={{0,256},{128,384},{256,0},{384,128},{1,257},{129,385},{257,1},{385... | collective-permute-start | bytes 497672 | tf_op jit(solution)/shard_map/ppermute | solution.py:275
  70.2 1.9 %collective-permute-start.7 = (bf16[64,1296]{1,0:T(8,128)(2,1)S(1)}, bf16[64,1296]{1,0:T(8,128)(2,1)S(1)}, u32[]{:S(2)}, u32[]{:S(2)}) collective-permute-start(bf16[64,1296]{1,0:T(8,128)(2,1)S(1)} %get-tuple-element.29), channel_id=1, source_target_pairs={{0,384},{128,0},{256,128},{384,256},{1,385},{129,1},{257,129},{385... | collective-permute-start | bytes 497672 | tf_op jit(solution)/shard_map/ppermute | solution.py:275
  72.1 10.1 %all-to-all-done.1.raw_ref = bf16[64,2,2592]{2,1,0:T(2,128)(2,1)S(1)} async-done(((bf16[64,2,2592]{2,1,0:T(2,128)(2,1)}), bf16[64,2,2592]{2,1,0:T(2,128)(2,1)S(1)}, u32[]{:S(2)}, u32[]{:S(2)}) %all-to-all-start.1) | async-done | bytes 663584 | tf_op jit(solution)/shard_map/all_to_all | solution.py:312
  82.3 0.5 shard_map.123.wm_ref
  82.7 1.9 %collective-permute-start.4 = (bf16[576,576]{1,0:T(8,128)(2,1)S(1)}, bf16[576,576]{1,0:T(8,128)(2,1)S(1)}, u32[]{:S(2)}, u32[]{:S(2)}) collective-permute-start(bf16[576,576]{1,0:T(8,128)(2,1)S(1)} %shard_map.123.wm_ref), channel_id=1, source_target_pairs={{0,64},{64,0},{1,65},{65,1},{2,66},{66,2},{3,67},{67,3},{4,68},{68... | collective-permute-start | bytes 1990664 | tf_op jit(solution)/shard_map/ppermute | solution.py:278
  84.7 0.0 collective-permute-done.5.p1_ref
  84.7 2.5 %collective-permute-done.6.p2_ref = bf16[64,1296]{1,0:T(8,128)(2,1)S(1)} collective-permute-done((bf16[64,1296]{1,0:T(8,128)(2,1)S(1)}, bf16[64,1296]{1,0:T(8,128)(2,1)S(1)}, u32[]{:S(2)}, u32[]{:S(2)}) %collective-permute-start.6) | collective-permute-done | bytes 165920 | tf_op jit(solution)/shard_map/ppermute | solution.py:275
  87.1 3.2 %collective-permute-done.7.p3_ref = bf16[64,1296]{1,0:T(8,128)(2,1)S(1)} collective-permute-done((bf16[64,1296]{1,0:T(8,128)(2,1)S(1)}, bf16[64,1296]{1,0:T(8,128)(2,1)S(1)}, u32[]{:S(2)}, u32[]{:S(2)}) %collective-permute-start.7) | collective-permute-done | bytes 165920 | tf_op jit(solution)/shard_map/ppermute | solution.py:275
  90.4 0.3 shard_map.124.sum_ref
  90.7 0.0 collective-permute-done.4.wt_ref
  90.7 2.5 %shard_map.125 = bf16[64,2,3024]{2,1,0:T(2,128)(2,1)S(1)} custom-call(f32[1,1152]{1,0:T(1,128)S(1)} %reshape.44.gate_ref, bf16[64,2,2880]{2,1,0:T(2,128)(2,1)S(1)} %all-to-all-done.x_ref, f32[8,128,128]{2,1,0:T(8,128)S(1)} %get-tuple-element.20.probs_ref, bf16[576,576]{1,0:T(8,128)(2,1)S(1)} %shard_map.123.wm_ref, ...), custom_call_target="tpu_custom_call" | custom-call | flops 1000000000 | bytes 3846656 | tf_op jit(solution)/shard_map/pallas_call | solution.py:250
  93.3 39.2 %all_to_all.15.z_ref = bf16[64,2,3024]{2,1,0:T(2,128)(2,1)S(1)} all-to-all(bf16[64,2,3024]{2,1,0:T(2,128)(2,1)S(1)} %shard_map.125), channel_id=1, replica_groups=mesh['line'=4,'core'=2,'x'=4,'y'=2,'z'=8] {'x','y','z'}, dimensions={0} | all-to-all | bytes 1548288 | tf_op jit(solution)/shard_map/all_to_all | solution.py:338
  132.5 2.0 %shard_map.126 = (bf16[128,1152]{1,0:T(8,128)(2,1)}, bf16[576,128]{1,0:T(8,128)(2,1)}, bf16[576,128]{1,0:T(8,128)(2,1)}, bf16[576,128]{1,0:T(8,128)(2,1)}, f32[9,144]{1,0:T(8,128)}) custom-call(s32[1]{0:T(128)} %bitcast.core_ref, f32[1,1152]{1,0:T(1,128)S(1)} %reshape.44.gate_ref, bf16[64,2,3024]{2,1,0:T(2,128)(2,1)S(1)} %all_to_all.15.z_ref, ...), custom_call_target="tpu_custom_call" | custom-call | flops 100000000 | bytes 2848324 | tf_op jit(solution)/shard_map/pallas_call | solution.py:250
  (1 shorter events, 0.0 us)
Async XLA Ops:
  4.0 18.2 %copy-start = (bf16[9,144]{1,0:T(8,128)(2,1)S(1)}, bf16[9,144]{1,0:T(8,128)(2,1)}, u32[]{:S(2)}) copy-start(bf16[9,144]{1,0:T(8,128)(2,1)} %w0) | copy-start | bytes 7780
  4.0 46.5 %all-to-all-start = ((bf16[64,2,2880]{2,1,0:T(2,128)(2,1)}), bf16[64,2,2880]{2,1,0:T(2,128)(2,1)S(1)}, u32[]{:S(2)}, u32[]{:S(2)}) async-start(bf16[64,2,2880]{2,1,0:T(2,128)(2,1)} %shard_map.119), calls=%async_computation | async-start | bytes 1507328 | tf_op jit(solution)/shard_map/all_to_all | solution.py:303
  22.2 16.3 %collective-permute-start.2 = (bf16[9,144]{1,0:T(8,128)(2,1)S(1)}, bf16[9,144]{1,0:T(8,128)(2,1)S(1)}, u32[]{:S(2)}, u32[]{:S(2)}) collective-permute-start(bf16[9,144]{1,0:T(8,128)(2,1)S(1)} %copy-done), channel_id=1, source_target_pairs={{0,384},{128,0},{256,128},{384,256},{1,385},{129,1},{257,129},{385... | collective-permute-start | bytes 7784 | tf_op jit(solution)/shard_map/ppermute | solution.py:275
  25.5 13.1 %collective-permute-start.1 = (bf16[9,144]{1,0:T(8,128)(2,1)S(1)}, bf16[9,144]{1,0:T(8,128)(2,1)S(1)}, u32[]{:S(2)}, u32[]{:S(2)}) collective-permute-start(bf16[9,144]{1,0:T(8,128)(2,1)S(1)} %copy-done), channel_id=1, source_target_pairs={{0,256},{128,384},{256,0},{384,128},{1,257},{129,385},{257,1},{385... | collective-permute-start | bytes 7784 | tf_op jit(solution)/shard_map/ppermute | solution.py:275
  28.2 10.4 %collective-permute-start = (bf16[9,144]{1,0:T(8,128)(2,1)S(1)}, bf16[9,144]{1,0:T(8,128)(2,1)S(1)}, u32[]{:S(2)}, u32[]{:S(2)}) collective-permute-start(bf16[9,144]{1,0:T(8,128)(2,1)S(1)} %copy-done), channel_id=1, source_target_pairs={{0,128},{128,256},{256,384},{384,0},{1,129},{129,257},{257,385},{3... | collective-permute-start | bytes 7784 | tf_op jit(solution)/shard_map/ppermute | solution.py:275
  50.5 6.2 %copy-start.1 = (f32[1152]{0:T(1024)S(1)}, f32[1152]{0:T(1024)}, u32[]{:S(2)}) copy-start(f32[1152]{0:T(1024)} %constant.26.clone) | copy-start | bytes 13828
  50.5 6.2 %copy-start.2 = (f32[1152]{0:T(1024)S(1)}, f32[1152]{0:T(1024)}, u32[]{:S(2)}) copy-start(f32[1152]{0:T(1024)} %constant.25.clone) | copy-start | bytes 13828
  50.5 31.8 %all-to-all-start.1 = ((bf16[64,2,2592]{2,1,0:T(2,128)(2,1)}), bf16[64,2,2592]{2,1,0:T(2,128)(2,1)S(1)}, u32[]{:S(2)}, u32[]{:S(2)}) async-start(bf16[64,2,2592]{2,1,0:T(2,128)(2,1)} %shard_map.121), calls=%async_computation.1 | async-start | bytes 1376256 | tf_op jit(solution)/shard_map/all_to_all | solution.py:312
  58.1 3.5 %collective-permute-start.3 = (bf16[128,1152]{1,0:T(8,128)(2,1)S(1)}, bf16[128,1152]{1,0:T(8,128)(2,1)S(1)}, u32[]{:S(2)}, u32[]{:S(2)}) collective-permute-start(bf16[128,1152]{1,0:T(8,128)(2,1)S(1)} %get-tuple-element.23.swap_ref), channel_id=1, source_target_pairs={{0,64},{64,0},{1,65},{65,1},{2,66},{66,2},{3,67},{67,3},{4,68},{68... | collective-permute-start | bytes 884744 | tf_op jit(solution)/shard_map/ppermute | solution.py:278
  62.5 22.2 %collective-permute-start.5 = (bf16[64,1296]{1,0:T(8,128)(2,1)S(1)}, bf16[64,1296]{1,0:T(8,128)(2,1)S(1)}, u32[]{:S(2)}, u32[]{:S(2)}) collective-permute-start(bf16[64,1296]{1,0:T(8,128)(2,1)S(1)} %get-tuple-element.27), channel_id=1, source_target_pairs={{0,128},{128,256},{256,384},{384,0},{1,129},{129,257},{257,385},{3... | collective-permute-start | bytes 497672 | tf_op jit(solution)/shard_map/ppermute | solution.py:275
  65.2 21.9 %collective-permute-start.6 = (bf16[64,1296]{1,0:T(8,128)(2,1)S(1)}, bf16[64,1296]{1,0:T(8,128)(2,1)S(1)}, u32[]{:S(2)}, u32[]{:S(2)}) collective-permute-start(bf16[64,1296]{1,0:T(8,128)(2,1)S(1)} %get-tuple-element.28), channel_id=1, source_target_pairs={{0,256},{128,384},{256,0},{384,128},{1,257},{129,385},{257,1},{385... | collective-permute-start | bytes 497672 | tf_op jit(solution)/shard_map/ppermute | solution.py:275
  70.2 20.2 %collective-permute-start.7 = (bf16[64,1296]{1,0:T(8,128)(2,1)S(1)}, bf16[64,1296]{1,0:T(8,128)(2,1)S(1)}, u32[]{:S(2)}, u32[]{:S(2)}) collective-permute-start(bf16[64,1296]{1,0:T(8,128)(2,1)S(1)} %get-tuple-element.29), channel_id=1, source_target_pairs={{0,384},{128,0},{256,128},{384,256},{1,385},{129,1},{257,129},{385... | collective-permute-start | bytes 497672 | tf_op jit(solution)/shard_map/ppermute | solution.py:275
  82.7 8.0 %collective-permute-start.4 = (bf16[576,576]{1,0:T(8,128)(2,1)S(1)}, bf16[576,576]{1,0:T(8,128)(2,1)S(1)}, u32[]{:S(2)}, u32[]{:S(2)}) collective-permute-start(bf16[576,576]{1,0:T(8,128)(2,1)S(1)} %shard_map.123.wm_ref), channel_id=1, source_target_pairs={{0,64},{64,0},{1,65},{65,1},{2,66},{66,2},{3,67},{67,3},{4,68},{68... | collective-permute-start | bytes 1990664 | tf_op jit(solution)/shard_map/ppermute | solution.py:278
